TPU v7x, 32 devices: a whole 2x2x4 slice. The times are simulated.
32 devices in a mesh: freq: 4 (over y, x), mat: 8 (over z, core).
Axes of the slice: x: 2, y: 2, z: 4, core: 2. Of those that a mesh axis runs over, the one named last changes fastest.
Arguments:
- traces: bfloat16 [2048, 64, 4096], P('freq', None, 'mat'), may hold values from -6 to 6
- reflection: bfloat16 [8, 2, 4096, 4096], P('freq', None, 'mat'), may hold values from -0.0625 to 0.0625
- onset: int32 [64, 4096], P(None, 'mat'), may hold values from 512 to 2047
Outputs:
- windowed: bfloat16 [2048, 64, 4096], P('freq', None, 'mat')
Inputs may be any that keep to these rules, and one draw needn't show every extreme that they name: onset sample of the direct arrival for each focal point and receiver.
All inputs are finite; a program needn't handle non-finite values.
Results may differ from a plain program's by a relative error of at most 0.0069.
Values may be sent and summed in bfloat16 or wider, within the bound.
No kernel may reach another device: no remote copies, remote signals or barrier semaphores. Data moves between devices by JAX's collectives and lax.ppermute only.
A program may use at most 192 MiB of HBM per device.

v0:
```python
import math

import jax
import jax.numpy as jnp
from jax import lax
from jax.sharding import PartitionSpec as P


def forward_table(base_band, first_band, band_count, sample_time_count, sampling_interval):
    angular_freq_list = base_band + first_band + jnp.arange(band_count, dtype=jnp.int32)
    sample_moments = jnp.arange(sample_time_count, dtype=jnp.int32)
    phase_angles = (
        angular_freq_list[:, None] * sample_moments[None, :] % sampling_interval
    ).astype(jnp.float32) * (2.0 * math.pi / sampling_interval)
    factor = 1.0 / math.sqrt(sampling_interval)
    table = jnp.stack([jnp.cos(phase_angles) * factor, -jnp.sin(phase_angles) * factor], axis=1)
    return table.reshape(2 * band_count, sample_time_count).astype(jnp.bfloat16)


def inverse_table(
    base_band,
    first_band,
    band_count,
    earliest_sample_time,
    sample_time_count,
    sampling_interval,
    bands_total,
):
    angular_freq_list = base_band + first_band + jnp.arange(band_count, dtype=jnp.int32)
    sample_moments = earliest_sample_time + jnp.arange(sample_time_count, dtype=jnp.int32)
    phase_angles = (
        sample_moments[:, None] * angular_freq_list[None, :] % sampling_interval
    ).astype(jnp.float32) * (2.0 * math.pi / sampling_interval)
    factor = 1.0 / math.sqrt(bands_total)
    table = jnp.stack([jnp.cos(phase_angles) * factor, -jnp.sin(phase_angles) * factor], axis=2)
    return table.reshape(sample_time_count, 2 * band_count).astype(jnp.bfloat16)


def accumulate(reflection, panels):
    return jnp.einsum("kcpw,kdrw->kcpdr", panels, reflection, preferred_element_type=jnp.float32)


def on_device(traces, reflection, onset):
    temporal_rows, focal_count, recv_rows = traces.shape
    freq_devices = lax.axis_size("freq")
    sampling_interval = temporal_rows * freq_devices
    per_device = reflection.shape[0]
    bands_total = per_device * freq_devices
    base_band = sampling_interval // 16
    earliest_sample_time = lax.axis_index("freq") * temporal_rows
    gathered = lax.all_to_all(traces, "freq", split_axis=1, concat_axis=0, tiled=True)
    forward = forward_table(base_band, 0, bands_total, sampling_interval, sampling_interval)
    local_spectra = jnp.dot(
        forward, gathered.reshape(sampling_interval, -1), preferred_element_type=jnp.float32
    )
    local_spectra = local_spectra.astype(jnp.bfloat16).reshape(
        bands_total, 2, focal_count // freq_devices, recv_rows
    )
    spectra = lax.all_to_all(local_spectra, "freq", split_axis=0, concat_axis=2, tiled=True)
    products = accumulate(reflection, lax.all_gather(spectra, "mat", axis=3, tiled=True))
    real_part = products[:, 0, :, 0] - products[:, 1, :, 1]
    imag_part = products[:, 1, :, 0] + products[:, 0, :, 1]
    response = jnp.stack([real_part, imag_part], axis=1).astype(jnp.bfloat16)
    pieces = lax.all_gather(response, "freq", axis=0, tiled=True)
    piece_bands = pieces.shape[0]
    table = inverse_table(
        base_band,
        jnp.int32(0),
        piece_bands,
        earliest_sample_time,
        temporal_rows,
        sampling_interval,
        bands_total,
    )
    wavelet_trace = jnp.dot(
        table, pieces.reshape(2 * piece_bands, -1), preferred_element_type=jnp.float32
    )
    wavelet_trace = wavelet_trace.reshape(temporal_rows, focal_count, recv_rows)
    sample_moments = earliest_sample_time + jnp.arange(temporal_rows, dtype=jnp.int32)
    return jnp.where(sample_moments[:, None, None] < onset[None], wavelet_trace, 0.0).astype(
        jnp.bfloat16
    )


def solution(mesh):
    placed = (P("freq", None, "mat"), P("freq", None, "mat", None), P(None, "mat"))
    return jax.shard_map(
        on_device, mesh=mesh, in_specs=placed, out_specs=P("freq", None, "mat"), check_vma=False
    )
```

profile of v0, /device:TPU:0, one launch (start us, length us, event | category | flops | bytes accessed | tf_op | source)
XLA Modules:
  0.0 608.4 jit_solution(14475330966378735583)
XLA Ops:
  6.5 22.9 %copy.33 = bf16[512,64,512]{2,0,1:T(8,128)(2,1)} copy(bf16[512,64,512]{2,1,0:T(8,128)(2,1)} %param.3) | data formatting | bytes 67108864 | tf_op args[0]
  29.5 9.7 %all-to-all-start = ((bf16[512,64,512]{2,0,1:T(8,128)(2,1)}), bf16[512,64,512]{2,0,1:T(8,128)(2,1)}, u32[]{:S(2)}, u32[]{:S(2)}) async-start(bf16[512,64,512]{2,0,1:T(8,128)(2,1)} %copy.33), calls=%async_computation | async-start | bytes 67108864 | tf_op jit(solution)/shard_map/all_to_all | solution.py:51
  39.2 0.0 all-gather.3.cloned.1.call-start
  39.2 0.3 multiply_convert_fusion.1
  39.6 0.1 copy.32
  39.7 363.0 %all-to-all-done = bf16[512,64,512]{2,0,1:T(8,128)(2,1)} async-done(((bf16[512,64,512]{2,0,1:T(8,128)(2,1)}), bf16[512,64,512]{2,0,1:T(8,128)(2,1)}, u32[]{:S(2)}, u32[]{:S(2)}) %all-to-all-start) | async-done | bytes 33554464 | tf_op jit(solution)/shard_map/all_to_all | solution.py:51
  402.7 31.2 %copy.34 = bf16[512,4,16,512]{3,2,0,1:T(8,128)(2,1)} copy(bf16[512,4,16,512]{3,0,2,1:T(8,128)(2,1)} %bitcast) | data formatting | bytes 67108864 | tf_op jit(solution)/shard_map/all_to_all | solution.py:51
  433.8 31.0 %copy.46 = bf16[256,8,16,512]{3,1,2,0:T(8,128)(2,1)} copy(bf16[256,8,16,512]{3,2,1,0:T(8,128)(2,1)} %bitcast.58) | data formatting | bytes 67108864
  464.8 12.9 %convolution_convert_fusion = bf16[16,8192]{1,0:T(8,128)(2,1)S(1)} fusion(bf16[16,2048]{1,0:T(8,128)(2,1)S(1)} %convert_element_type.60, bf16[2048,8192]{1,0:T(8,128)(2,1)} %bitcast.57), kind=kOutput, calls=%fused_computation.3 | convolution fusion | flops 537001984 | bytes 33882112 | tf_op jit(solution)/shard_map/dot_general | solution.py:53
  477.7 0.1 copy.47
  477.8 8.3 %all_to_all.33 = bf16[8,2,16,512]{3,2,1,0:T(8,128)(2,1)S(1)} all-to-all(bf16[8,2,16,512]{3,2,1,0:T(8,128)(2,1)S(1)} %bitcast.62), channel_id=1, replica_groups=mesh['freq'=4,'mat'=8] {'freq'}, dimensions={0} | all-to-all | bytes 524288 | tf_op jit(solution)/shard_map/all_to_all | solution.py:59
  486.1 0.7 copy.35
  486.8 0.0 all-gather.3.cloned.1.call-update
  486.8 0.2 all-gather.5.cloned.1.call-start
  487.1 28.9 %all-gather.3.cloned.1.call-done = bf16[2,2,64,4096]{3,2,1,0:T(8,128)(2,1)} async-done(((bf16[2,2,64,512]{3,2,1,0:T(8,128)(2,1)}), bf16[2,2,64,4096]{3,2,1,0:T(8,128)(2,1)}) %all-gather.3.cloned.1.call-update) | async-done | bytes 2097168 | tf_op jit(solution)/shard_map/all_gather | solution.py:60
  516.0 12.1 %fusion = f32[2,2,64,2,512]{4,2,3,1,0:T(8,128)S(1)} fusion(bf16[2,2,512,4096]{3,2,1,0:T(8,128)(2,1)} %param.4, bf16[2,2,64,4096]{3,2,1,0:T(8,128)(2,1)} %all-gather.3.cloned.1.call-done), kind=kOutput, calls=%fused_computation.1 | convolution fusion | flops 2147483648 | bytes 19922944 | tf_op jit(solution)/shard_map/kcpw,kdrw->kcpdr/dot_general | solution.py:40
  528.2 0.7 pad_maximum_fusion
  528.9 0.0 all-gather.5.cloned.1.call-update
  529.0 0.2 multiply_convert_fusion.3
  529.2 26.0 %all-gather.5.cloned.1.call-done = bf16[8,2,64,512]{3,2,0,1:T(8,128)(2,1)} async-done(((bf16[2,2,64,512]{3,2,0,1:T(8,128)(2,1)}), bf16[8,2,64,512]{3,2,0,1:T(8,128)(2,1)}) %all-gather.5.cloned.1.call-update) | async-done | bytes 1048592 | tf_op jit(solution)/shard_map/all_gather | solution.py:64
  555.2 1.3 copy.38
  556.5 0.0 copy-done
  556.5 13.9 %select_convert_fusion = bf16[512,64,512]{2,0,1:T(8,128)(2,1)} fusion(s32[64,512]{1,0:T(8,128)S(1)} %copy-done, s32[512]{0:T(512)S(1)} %iota_add_fusion, bf16[512,16,1]{0,1,2:T(8,128)(2,1)S(1)} %reshape.327, bf16[2,8,64,512]{3,2,1,0:T(8,128)(2,1)S(1)} %bitcast.60), kind=kOutput, calls=%fused_computation | convolution fusion | flops 587202560 | bytes 34752512 | tf_op jit(solution)/shard_map/dot_general | solution.py:75
  570.4 31.1 %copy.40 = bf16[512,64,512]{2,1,0:T(8,128)(2,1)} copy(bf16[512,64,512]{2,0,1:T(8,128)(2,1)} %select_convert_fusion) | data formatting | bytes 67108864 | tf_op jit(solution)/shard_map/convert_element_type | solution.py:80
  (10 shorter events, 0.2 us)
Async XLA Ops:
  29.5 373.2 %all-to-all-start = ((bf16[512,64,512]{2,0,1:T(8,128)(2,1)}), bf16[512,64,512]{2,0,1:T(8,128)(2,1)}, u32[]{:S(2)}, u32[]{:S(2)}) async-start(bf16[512,64,512]{2,0,1:T(8,128)(2,1)} %copy.33), calls=%async_computation | async-start | bytes 67108864 | tf_op jit(solution)/shard_map/all_to_all | solution.py:51
  39.2 476.8 %all-gather.3.cloned.1.call-start = ((), (), s32[]{:S(2)}) async-start(), calls=%async_computation.2 | async-start | bytes 2359296 | tf_op jit(solution)/shard_map/all_gather | solution.py:60
  464.8 91.7 %copy-start = (s32[64,512]{1,0:T(8,128)S(1)}, s32[64,512]{1,0:T(8,128)}, u32[]{:S(2)}) copy-start(s32[64,512]{1,0:T(8,128)} %param.5) | copy-start | bytes 393220
  486.8 68.4 %all-gather.5.cloned.1.call-start = ((), (), s32[]{:S(2)}) async-start(), calls=%async_computation.3 | async-start | bytes 1310720 | tf_op jit(solution)/shard_map/all_gather | solution.py:64
Sparse Core Ops, SparseCore 0:
  487.0 29.0 all-gather.2
  529.1 26.1 all-gather.4
where the time goes:
time: 609 us; the launch traced here: 608 us
  waiting for transfers between devices  418 us (69%)
  local copies, waits for them, and re-layouts  118 us (19%)
  matrix products  38.9 us (6%)
  between operations  13.5 us (2%)
  starting transfers between devices  9.98 us (2%)
  blocking collectives  8.3 us (1%)
    all_to_all x1, waiting for transfers between devices, on_device(): lax.all_to_all(traces, 'freq', split_axis=1, concat_axis=0, tiled=True)  363 us
    unnamed x5, local copies, waits for them, and re-layouts  54 us
    all_to_all x1, local copies, waits for them, and re-layouts, on_device(): lax.all_to_all(traces, 'freq', split_axis=1, concat_axis=0, tiled=True)  31.2 us
    convert_element_type x1, local copies, waits for them, and re-layouts, on_device(): jnp.where(sample_moments[:, None, None] < onset[None], wavelet_trace, 0.0)  31.1 us
    all_gather x1, waiting for transfers between devices, on_device(): lax.all_gather(spectra, 'mat', axis=3, tiled=True)  28.9 us
    all_gather x1, waiting for transfers between devices, on_device(): pieces = lax.all_gather(response, 'freq', axis=0, tiled=True)  26 us
    dot_general x1, matrix products, on_device(): jnp.dot(table, pieces.reshape(2 * piece_bands, -1), preferred_element_typ...  13.9 us
    dot_general x1, matrix products, on_device(): jnp.dot(forward, gathered.reshape(sampling_interval, -1), preferred_eleme...  12.9 us
  transfers between devices with their start and end apart: 3, of which 3 were waited for; matrix products, arithmetic and copies ran while one was open for 0% of the time, Pallas kernels for 0%

commit v1 on v0

v1 whole, which is shorter than its diff:
```python
import functools
import math

import jax
import jax.numpy as jnp
from jax import lax
from jax.experimental import pallas as pl
from jax.experimental.pallas import tpu as pltpu
from jax.sharding import PartitionSpec as P

ROWS = 16
CHUNKS = 2
F_TIMES = 128
I_TIMES = 64
R_ROWS = 128
VMEM = 56 * 1024 * 1024


def phases(bands, times, samples):
    return (bands * times % samples).astype(jnp.float32) * (2.0 * math.pi / samples)


def tables(per_device, freq_devices, local_times):
    me = lax.axis_index("freq")
    samples = local_times * freq_devices
    owners = me ^ jnp.arange(freq_devices, dtype=jnp.int32)
    bands = samples // 16 + (owners[:, None] * per_device + jnp.arange(per_device, dtype=jnp.int32)).reshape(-1)
    times = me * local_times + jnp.arange(local_times, dtype=jnp.int32)
    rows = phases(bands[:, None], times[None, :], samples)
    factor = 1.0 / math.sqrt(samples)
    forward = jnp.stack([jnp.cos(rows) * factor, -jnp.sin(rows) * factor], axis=1)
    columns = phases(bands[None, :], times[:, None], samples)
    factor = 1.0 / math.sqrt(per_device * freq_devices)
    inverse = jnp.stack([jnp.cos(columns) * factor, -jnp.sin(columns) * factor], axis=2)
    return (
        forward.reshape(-1, local_times).astype(jnp.bfloat16),
        inverse.reshape(local_times, -1).astype(jnp.bfloat16),
    )


def forward_kernel(table_ref, traces_ref, *refs):
    outs, (spread, total) = refs[:-2], refs[-2:]
    block, step = pl.program_id(0), pl.program_id(1)
    times, rows, width = traces_ref.shape
    lanes = times * rows
    count = table_ref.shape[0]

    @pl.when(block == 0)
    def _():
        lane = lax.broadcasted_iota(jnp.int32, (times, lanes), 1)
        row = lax.broadcasted_iota(jnp.int32, (times, lanes), 0)
        repeat = jnp.where(lane // rows == row, 1.0, 0.0).astype(jnp.bfloat16)
        wide = jnp.dot(table_ref[...], repeat, preferred_element_type=jnp.float32)
        lane = lax.broadcasted_iota(jnp.int32, (rows, lanes), 1)
        row = lax.broadcasted_iota(jnp.int32, (rows, lanes), 0)
        own = lane % rows == row
        for i in range(count):
            spread[step, pl.ds(i * rows, rows), :] = jnp.where(own, wide[i : i + 1], 0.0).astype(jnp.bfloat16)

    part = jnp.dot(
        spread[step], traces_ref[...].reshape(lanes, width), preferred_element_type=jnp.float32
    )

    @pl.when(step == 0)
    def _():
        total[...] = part

    @pl.when(step > 0)
    def _():
        total[...] += part

    @pl.when(step == pl.num_programs(1) - 1)
    def _():
        share = count * rows // len(outs)
        for i, out in enumerate(outs):
            out[...] = total[pl.ds(i * share, share), :].reshape(out.shape).astype(out.dtype)


def forward(table, traces, first, focal, per_device, freq_devices):
    local_times, _, width = traces.shape
    count = table.shape[0]
    times = min(F_TIMES, local_times)
    steps = local_times // times
    shape = (per_device, 2, focal, width)
    return pl.pallas_call(
        forward_kernel,
        grid=(focal // ROWS, steps),
        in_specs=[
            pl.BlockSpec((count, times), lambda p, t: (0, t)),
            pl.BlockSpec((times, ROWS, width), lambda p, t: (t, first // ROWS + p, 0)),
        ],
        out_specs=[
            pl.BlockSpec((per_device, 2, ROWS, width), lambda p, t: (0, 0, p, 0)) for _ in range(freq_devices)
        ],
        out_shape=[
            jax.ShapeDtypeStruct(shape, jnp.float32 if i == 0 else jnp.bfloat16) for i in range(freq_devices)
        ],
        scratch_shapes=[
            pltpu.VMEM((steps, count * ROWS, times * ROWS), jnp.bfloat16),
            pltpu.VMEM((count * ROWS, width), jnp.float32),
        ],
        compiler_params=pltpu.CompilerParams(vmem_limit_bytes=VMEM),
        cost_estimate=pl.CostEstimate(
            flops=2 * count * ROWS * local_times * focal * width,
            bytes_accessed=2 * local_times * focal * width,
            transcendentals=0,
        ),
        name="forward",
    )(table, traces)


def response_kernel(place_ref, reflection_ref, *refs):
    pieces, (out, spectra) = refs[:-2], refs[-2:]
    band, step = pl.program_id(0), pl.program_id(1)
    _, _, rows, sources = reflection_ref.shape
    _, _, focal, width = pieces[0].shape

    @pl.when((band == 0) & (step == 0))
    def _():
        for i, piece in enumerate(pieces):
            start = pl.multiple_of(place_ref[i] * width, width)
            spectra[:, :, pl.ds(start, width)] = piece[...].reshape(-1, 2 * focal, width)

    product = lax.dot_general(
        spectra[band],
        reflection_ref[...].reshape(2 * rows, sources),
        (((1,), (1,)), ((), ())),
        preferred_element_type=jnp.float32,
    )
    out[0, 0] = (product[:focal, :rows] - product[focal:, rows:]).astype(out.dtype)
    out[0, 1] = (product[focal:, :rows] + product[:focal, rows:]).astype(out.dtype)


def respond(reflection, places, pieces):
    per_device, _, width, sources = reflection.shape
    focal = pieces[0].shape[2]
    rows = min(R_ROWS, width)
    return pl.pallas_call(
        response_kernel,
        grid=(per_device, width // rows),
        in_specs=[
            pl.BlockSpec(memory_space=pltpu.SMEM),
            pl.BlockSpec((1, 2, rows, sources), lambda k, r: (k, 0, r, 0)),
        ]
        + [pl.BlockSpec(p.shape, lambda k, r: (0, 0, 0, 0), pipeline_mode=pl.Buffered(1)) for p in pieces],
        out_specs=pl.BlockSpec((1, 2, focal, rows), lambda k, r: (k, 0, 0, r)),
        out_shape=jax.ShapeDtypeStruct((per_device, 2, focal, width), jnp.bfloat16),
        scratch_shapes=[pltpu.VMEM((per_device, 2 * focal, sources), jnp.bfloat16)],
        compiler_params=pltpu.CompilerParams(vmem_limit_bytes=VMEM),
        cost_estimate=pl.CostEstimate(
            flops=8 * per_device * focal * width * sources,
            bytes_accessed=4 * per_device * width * sources,
            transcendentals=0,
        ),
        name="respond",
    )(places, reflection, *pieces)


def inverse_kernel(has_before, table_ref, onset_ref, *refs):
    pieces, (out, spread, weights) = refs[: -3 - has_before], refs[-3:]
    block, step = pl.program_id(0), pl.program_id(1)
    times, rows, width = out.shape
    count = table_ref.shape[1]
    lanes = count * rows

    @pl.when(block == 0)
    def _():
        lane = lax.broadcasted_iota(jnp.int32, (count, lanes), 1)
        row = lax.broadcasted_iota(jnp.int32, (count, lanes), 0)
        repeat = jnp.where(lane // rows == row, 1.0, 0.0).astype(jnp.bfloat16)
        wide = jnp.dot(table_ref[...], repeat, preferred_element_type=jnp.float32)
        lane = lax.broadcasted_iota(jnp.int32, (rows, lanes), 1)
        row = lax.broadcasted_iota(jnp.int32, (rows, lanes), 0)
        own = lane % rows == row
        for i in range(times):
            spread[step, pl.ds(i * rows, rows), :] = jnp.where(own, wide[i : i + 1], 0.0).astype(jnp.bfloat16)

    @pl.when(step == 0)
    def _():
        share = lanes // len(pieces)
        for i, piece in enumerate(pieces):
            weights[pl.ds(i * share, share), :] = piece[...].reshape(share, width)

    signal = jnp.dot(spread[step], weights[...], preferred_element_type=jnp.float32)
    signal = signal.reshape(times, rows, width)
    first = (lax.axis_index("freq") * pl.num_programs(1) + step) * times
    moment = first + lax.broadcasted_iota(jnp.int32, (times, 1, 1), 0)
    out[...] = jnp.where(moment < onset_ref[...][None], signal, 0.0).astype(out.dtype)


def invert(table, onset, pieces, before, first, shape):
    local_times, _, width = shape
    focal = pieces[0].shape[2]
    count = table.shape[1]
    times = min(I_TIMES, local_times)
    steps = local_times // times
    has_before = before is not None
    operands = [table, onset, *pieces] + ([before] if has_before else [])
    return pl.pallas_call(
        functools.partial(inverse_kernel, has_before),
        grid=(focal // ROWS, steps),
        in_specs=[
            pl.BlockSpec((times, count), lambda p, t: (t, 0)),
            pl.BlockSpec((ROWS, width), lambda p, t: (first // ROWS + p, 0)),
        ]
        + [pl.BlockSpec((p.shape[0], 2, ROWS, width), lambda p, t: (0, 0, p, 0)) for p in pieces]
        + ([pl.BlockSpec(memory_space=pl.ANY)] if has_before else []),
        out_specs=pl.BlockSpec((times, ROWS, width), lambda p, t: (t, first // ROWS + p, 0)),
        out_shape=jax.ShapeDtypeStruct(shape, jnp.bfloat16),
        scratch_shapes=[
            pltpu.VMEM((steps, times * ROWS, count * ROWS), jnp.bfloat16),
            pltpu.VMEM((count * ROWS, width), jnp.bfloat16),
        ],
        input_output_aliases={len(operands) - 1: 0} if has_before else {},
        compiler_params=pltpu.CompilerParams(vmem_limit_bytes=VMEM),
        cost_estimate=pl.CostEstimate(
            flops=2 * count * ROWS * local_times * focal * width,
            bytes_accessed=2 * local_times * focal * width,
            transcendentals=0,
        ),
        name="invert",
    )(*operands)


def swap(array, axis, mask):
    return lax.ppermute(array, axis, [(i, i ^ mask) for i in range(lax.axis_size(axis))])


def on_device(traces, reflection, onset):
    local_times, focal_count, _ = traces.shape
    freq_devices, mat_devices = lax.axis_size("freq"), lax.axis_size("mat")
    per_device = reflection.shape[0]
    forward_table, inverse_table = tables(per_device, freq_devices, local_times)
    focal = focal_count // CHUNKS

    masks = list(range(0, mat_devices, 2))
    places = lax.axis_index("mat") ^ jnp.array([m ^ c for m in masks for c in (0, 1)], jnp.int32)

    parts = [
        forward(forward_table, traces, i * focal, focal, per_device, freq_devices) for i in range(CHUNKS)
    ]
    responses = []
    for part in parts:
        spectra = part[0]
        for mask in range(1, freq_devices):
            spectra = spectra + swap(part[mask], "freq", mask).astype(jnp.float32)
        spectra = spectra.astype(jnp.bfloat16)
        pieces = []
        for mask in masks:
            piece = swap(spectra, "mat", mask) if mask else spectra
            pieces += [piece, swap(piece, "mat", 1)]
        response = respond(reflection, places, pieces)
        responses.append([response] + [swap(response, "freq", mask) for mask in range(1, freq_devices)])
    windowed = None
    for i, pieces in enumerate(responses):
        windowed = invert(inverse_table, onset, pieces, windowed, i * focal, traces.shape)
    return windowed


def solution(mesh):
    placed = (P("freq", None, "mat"), P("freq", None, "mat", None), P(None, "mat"))
    return jax.shard_map(
        on_device, mesh=mesh, in_specs=placed, out_specs=P("freq", None, "mat"), check_vma=False
    )
```

time: 609 us -> 128 us (0.21)
  waiting for transfers between devices: 418 us -> 12 us
  local copies, waits for them, and re-layouts: 118 us -> 6.6 us
  Pallas kernels: 0 us -> 76.8 us
  matrix products: 38.9 us -> 0 us
  starting transfers between devices: 9.98 us -> 28.6 us
  between operations: 13.5 us -> 0.24 us
  blocking collectives: 8.3 us -> 0 us
    all_to_all x1 -> x0, waiting for transfers between devices: 363 us -> none  [on_device(): lax.all_to_all(traces, 'freq', split_axis=1, concat_axis=0, tiled=True)]
    pallas_call x0 -> x6, Pallas kernels: none -> 76.8 us  [the longest x2 28.3 us: invert(): pl.pallas_call(functools.partial(inverse_kernel, has_before), grid=(focal...]
    all_gather x2 -> x0, waiting for transfers between devices: 55 us -> none  [the longest x1 28.9 us: on_device(): lax.all_gather(spectra, 'mat', axis=3, tiled=True)]
    unnamed x5 -> x46, local copies, waits for them, and re-layouts: 54 us -> 5.09 us
    dot_general x3 -> x0, matrix products: 38.9 us -> none  [the longest x1 13.9 us: on_device(): jnp.dot(table, pieces.reshape(2 * piece_bands, -1), preferred_element_typ...]
    all_to_all x2 -> x0, local copies, waits for them, and re-layouts: 31.9 us -> none  [the longest x1 31.2 us: on_device(): lax.all_to_all(traces, 'freq', split_axis=1, concat_axis=0, tiled=True)]
    convert_element_type x3, local copies, waits for them, and re-layouts: 31.1 us -> 1.39 us  [the longest x2 0.78 us: tables(): inverse.reshape(local_times, -1).astype(jnp.bfloat16)]
    ppermute x0 -> x26, starting transfers between devices: none -> 28.6 us  [swap(): lax.ppermute(array, axis, [(i, i ^ mask) for i in range(lax.axis_size(axi...]
  transfers between devices with their start and end apart: 3 -> 26, of which waited for: 3 -> 4; matrix products, arithmetic and copies ran while one was open for 0% -> 2% of each run, Pallas kernels for 0% -> 40%
where the time goes in v1:
time: 128 us; the launch traced here: 126 us
  Pallas kernels  76.8 us (60%)
  starting transfers between devices  28.6 us (22%)
  waiting for transfers between devices  12 us (9%)
  local copies, waits for them, and re-layouts  6.6 us (5%)
  other arithmetic  2.01 us (2%)
    ppermute x26, starting transfers between devices, swap(): lax.ppermute(array, axis, [(i, i ^ mask) for i in range(lax.axis_size(axi...  28.6 us
    pallas_call x2, Pallas kernels, invert(): pl.pallas_call(functools.partial(inverse_kernel, has_before), grid=(focal...  28.3 us
    pallas_call x2, Pallas kernels, forward(): pl.pallas_call(forward_kernel, grid=(focal // ROWS, steps), in_specs=[pl....  25 us
    pallas_call x2, Pallas kernels, respond(): pl.pallas_call(response_kernel, grid=(per_device, width // rows), in_spec...  23.5 us
    ppermute x26, waiting for transfers between devices, swap(): lax.ppermute(array, axis, [(i, i ^ mask) for i in range(lax.axis_size(axi...  12 us
    unnamed x46, local copies, waits for them, and re-layouts  5.09 us
  transfers between devices with their start and end apart: 26, of which 4 were waited for; matrix products, arithmetic and copies ran while one was open for 2% of the time, Pallas kernels for 40%

profile of v1, /device:TPU:0, one launch (start us, length us, event | category | flops | bytes accessed | tf_op | source)
XLA Modules:
  0.0 126.2 jit_solution(2366959828578947700)
XLA Ops:
  1.0 12.5 %forward.3 = (f32[2,2,32,512]{3,2,1,0:T(8,128)}, bf16[2,2,32,512]{3,2,1,0:T(8,128)(2,1)}, bf16[2,2,32,512]{3,2,1,0:T(8,128)(2,1)}, bf16[2,2,32,512]{3,2,1,0:T(8,128)(2,1)}) custom-call(bf16[16,512]{1,0:T(8,128)(2,1)} %convert_element_type.61.table_ref, bf16[512,64,512]{2,1,0:T(8,128)(2,1)} %traces_ref.3), custom_call_target="tpu_custom_call" | custom-call | flops 4294967296 | bytes 16777216 | tf_op jit(solution)/shard_map/forward/pallas_call | solution.py:85
  13.5 3.0 %collective-permute-start.13 = (bf16[2,2,32,512]{3,2,1,0:T(8,128)(2,1)}, bf16[2,2,32,512]{3,2,1,0:T(8,128)(2,1)S(1)}, u32[]{:S(2)}, u32[]{:S(2)}) collective-permute-start(bf16[2,2,32,512]{3,2,1,0:T(8,128)(2,1)} %get-tuple-element.18), channel_id=1, source_target_pairs={{0,8},{8,0},{16,24},{24,16},{1,9},{9,1},{17,25},{25,17},{2,10},{10... | collective-permute-start | bytes 393224 | tf_op jit(solution)/shard_map/ppermute | solution.py:226
  16.5 1.5 %collective-permute-start.14 = (bf16[2,2,32,512]{3,2,1,0:T(8,128)(2,1)}, bf16[2,2,32,512]{3,2,1,0:T(8,128)(2,1)S(1)}, u32[]{:S(2)}, u32[]{:S(2)}) collective-permute-start(bf16[2,2,32,512]{3,2,1,0:T(8,128)(2,1)} %get-tuple-element.19), channel_id=1, source_target_pairs={{0,16},{8,24},{16,0},{24,8},{1,17},{9,25},{17,1},{25,9},{2,18},{10... | collective-permute-start | bytes 393224 | tf_op jit(solution)/shard_map/ppermute | solution.py:226
  18.0 12.5 %forward.2 = (f32[2,2,32,512]{3,2,1,0:T(8,128)}, bf16[2,2,32,512]{3,2,1,0:T(8,128)(2,1)}, bf16[2,2,32,512]{3,2,1,0:T(8,128)(2,1)}, bf16[2,2,32,512]{3,2,1,0:T(8,128)(2,1)}) custom-call(bf16[16,512]{1,0:T(8,128)(2,1)} %convert_element_type.61.table_ref, bf16[512,64,512]{2,1,0:T(8,128)(2,1)} %traces_ref.3), custom_call_target="tpu_custom_call" | custom-call | flops 4294967296 | bytes 16777216 | tf_op jit(solution)/shard_map/forward/pallas_call | solution.py:85
  30.5 2.0 %collective-permute-start = (bf16[2,2,32,512]{3,2,1,0:T(8,128)(2,1)}, bf16[2,2,32,512]{3,2,1,0:T(8,128)(2,1)S(1)}, u32[]{:S(2)}, u32[]{:S(2)}) collective-permute-start(bf16[2,2,32,512]{3,2,1,0:T(8,128)(2,1)} %get-tuple-element.14), channel_id=1, source_target_pairs={{0,8},{8,0},{16,24},{24,16},{1,9},{9,1},{17,25},{25,17},{2,10},{10... | collective-permute-start | bytes 393224 | tf_op jit(solution)/shard_map/ppermute | solution.py:226
  32.5 1.5 %collective-permute-start.1 = (bf16[2,2,32,512]{3,2,1,0:T(8,128)(2,1)}, bf16[2,2,32,512]{3,2,1,0:T(8,128)(2,1)S(1)}, u32[]{:S(2)}, u32[]{:S(2)}) collective-permute-start(bf16[2,2,32,512]{3,2,1,0:T(8,128)(2,1)} %get-tuple-element.15), channel_id=1, source_target_pairs={{0,16},{8,24},{16,0},{24,8},{1,17},{9,25},{17,1},{25,9},{2,18},{10... | collective-permute-start | bytes 393224 | tf_op jit(solution)/shard_map/ppermute | solution.py:226
  34.1 4.1 %collective-permute-start.21 = (bf16[2,2,32,512]{3,2,1,0:T(8,128)(2,1)S(1)}, bf16[2,2,32,512]{3,2,1,0:T(8,128)(2,1)S(1)}, u32[]{:S(2)}, u32[]{:S(2)}) collective-permute-start(bf16[2,2,32,512]{3,2,1,0:T(8,128)(2,1)S(1)} %add_convert_fusion.refs_0_), channel_id=1, source_target_pairs={{0,6},{1,7},{2,4},{3,5},{4,2},{5,3},{6,0},{7,1},{8,14},{9,15},{10,... | collective-permute-start | bytes 393224 | tf_op jit(solution)/shard_map/ppermute | solution.py:226
  38.9 1.5 %collective-permute-done.1 = bf16[2,2,32,512]{3,2,1,0:T(8,128)(2,1)S(1)} collective-permute-done((bf16[2,2,32,512]{3,2,1,0:T(8,128)(2,1)}, bf16[2,2,32,512]{3,2,1,0:T(8,128)(2,1)S(1)}, u32[]{:S(2)}, u32[]{:S(2)}) %collective-permute-start.1) | collective-permute-done | bytes 131104 | tf_op jit(solution)/shard_map/ppermute | solution.py:226
  40.4 1.0 add_convert_fusion.1.refs_0_
  41.4 3.7 %collective-permute-start.8 = (bf16[2,2,32,512]{3,2,1,0:T(8,128)(2,1)S(1)}, bf16[2,2,32,512]{3,2,1,0:T(8,128)(2,1)S(1)}, u32[]{:S(2)}, u32[]{:S(2)}) collective-permute-start(bf16[2,2,32,512]{3,2,1,0:T(8,128)(2,1)S(1)} %add_convert_fusion.1.refs_0_), channel_id=1, source_target_pairs={{0,6},{1,7},{2,4},{3,5},{4,2},{5,3},{6,0},{7,1},{8,14},{9,15},{10,... | collective-permute-start | bytes 393224 | tf_op jit(solution)/shard_map/ppermute | solution.py:226
  45.1 3.3 %collective-permute-start.6 = (bf16[2,2,32,512]{3,2,1,0:T(8,128)(2,1)S(1)}, bf16[2,2,32,512]{3,2,1,0:T(8,128)(2,1)S(1)}, u32[]{:S(2)}, u32[]{:S(2)}) collective-permute-start(bf16[2,2,32,512]{3,2,1,0:T(8,128)(2,1)S(1)} %add_convert_fusion.1.refs_0_), channel_id=1, source_target_pairs={{0,4},{1,5},{2,6},{3,7},{4,0},{5,1},{6,2},{7,3},{8,12},{9,13},{10,... | collective-permute-start | bytes 393224 | tf_op jit(solution)/shard_map/ppermute | solution.py:226
  48.4 5.9 %collective-permute-done.19.refs_4_ = bf16[2,2,32,512]{3,2,1,0:T(8,128)(2,1)S(1)} collective-permute-done((bf16[2,2,32,512]{3,2,1,0:T(8,128)(2,1)S(1)}, bf16[2,2,32,512]{3,2,1,0:T(8,128)(2,1)S(1)}, u32[]{:S(2)}, u32[]{:S(2)}) %collective-permute-start.19) | collective-permute-done | bytes 131104 | tf_op jit(solution)/shard_map/ppermute | solution.py:226
  54.3 0.7 collective-permute-start.4
  55.7 3.3 %collective-permute-done.6.refs_4_ = bf16[2,2,32,512]{3,2,1,0:T(8,128)(2,1)S(1)} collective-permute-done((bf16[2,2,32,512]{3,2,1,0:T(8,128)(2,1)S(1)}, bf16[2,2,32,512]{3,2,1,0:T(8,128)(2,1)S(1)}, u32[]{:S(2)}, u32[]{:S(2)}) %collective-permute-start.6) | collective-permute-done | bytes 131104 | tf_op jit(solution)/shard_map/ppermute | solution.py:226
  59.0 1.3 %collective-permute-done.4.refs_2_ = bf16[2,2,32,512]{3,2,1,0:T(8,128)(2,1)S(1)} collective-permute-done((bf16[2,2,32,512]{3,2,1,0:T(8,128)(2,1)S(1)}, bf16[2,2,32,512]{3,2,1,0:T(8,128)(2,1)S(1)}, u32[]{:S(2)}, u32[]{:S(2)}) %collective-permute-start.4) | collective-permute-done | bytes 131104 | tf_op jit(solution)/shard_map/ppermute | solution.py:226
  62.6 11.7 %respond.3.refs_0_ = bf16[2,2,32,512]{3,2,1,0:T(8,128)(2,1)} custom-call(s32[8]{0:T(128)} %iota_xor_fusion.place_ref, bf16[2,2,512,4096]{3,2,1,0:T(8,128)(2,1)} %reflection_ref.3, bf16[2,2,32,512]{3,2,1,0:T(8,128)(2,1)} %copy-done.1, bf16[2,2,32,512]{3,2,1,0:T(8,128)(2,1)} %copy-done.15, bf16[2,2,32,512]{3,2,1,0:T(8,128)(2,1)} %copy-done.14, ...), custom_call_target="tpu_custom_call" | custom-call | flops 1073741824 | bytes 16777216 | tf_op jit(solution)/shard_map/respond/pallas_call | solution.py:138
  74.4 2.1 %collective-permute-start.25 = (bf16[2,2,32,512]{3,2,1,0:T(8,128)(2,1)}, bf16[2,2,32,512]{3,2,1,0:T(8,128)(2,1)S(1)}, u32[]{:S(2)}, u32[]{:S(2)}) collective-permute-start(bf16[2,2,32,512]{3,2,1,0:T(8,128)(2,1)} %respond.3.refs_0_), channel_id=1, source_target_pairs={{0,24},{8,16},{16,8},{24,0},{1,25},{9,17},{17,9},{25,1},{2,26},{10... | collective-permute-start | bytes 393224 | tf_op jit(solution)/shard_map/ppermute | solution.py:226
  77.0 0.9 collective-permute-start.23
  77.9 0.8 copy.11.table_ref
  80.0 11.7 %respond.2.refs_0_ = bf16[2,2,32,512]{3,2,1,0:T(8,128)(2,1)} custom-call(s32[8]{0:T(128)} %iota_xor_fusion.place_ref, bf16[2,2,512,4096]{3,2,1,0:T(8,128)(2,1)} %reflection_ref.3, bf16[2,2,32,512]{3,2,1,0:T(8,128)(2,1)} %copy-done, bf16[2,2,32,512]{3,2,1,0:T(8,128)(2,1)} %copy-done.16, bf16[2,2,32,512]{3,2,1,0:T(8,128)(2,1)} %copy-done.13, ...), custom_call_target="tpu_custom_call" | custom-call | flops 1073741824 | bytes 16777216 | tf_op jit(solution)/shard_map/respond/pallas_call | solution.py:138
  91.7 2.1 %collective-permute-start.12 = (bf16[2,2,32,512]{3,2,1,0:T(8,128)(2,1)}, bf16[2,2,32,512]{3,2,1,0:T(8,128)(2,1)S(1)}, u32[]{:S(2)}, u32[]{:S(2)}) collective-permute-start(bf16[2,2,32,512]{3,2,1,0:T(8,128)(2,1)} %respond.2.refs_0_), channel_id=1, source_target_pairs={{0,24},{8,16},{16,8},{24,0},{1,25},{9,17},{17,9},{25,1},{2,26},{10... | collective-permute-start | bytes 393224 | tf_op jit(solution)/shard_map/ppermute | solution.py:226
  94.4 0.9 collective-permute-start.10
  96.5 14.1 %invert.2.refs_4_ = bf16[512,64,512]{2,1,0:T(8,128)(2,1)} custom-call(bf16[512,16]{1,0:T(8,128)(2,1)} %copy.11.table_ref, s32[64,512]{1,0:T(8,128)} %onset_ref.3, bf16[2,2,32,512]{3,2,1,0:T(8,128)(2,1)} %respond.3.refs_0_, bf16[2,2,32,512]{3,2,1,0:T(8,128)(2,1)} %copy-done.5, bf16[2,2,32,512]{3,2,1,0:T(8,128)(2,1)} %copy-done.4, ...), custom_call_target="tpu_custom_call" | custom-call | flops 4294967296 | bytes 16777216 | tf_op jit(solution)/shard_map/invert/pallas_call | solution.py:199
  112.0 14.2 %invert.3 = bf16[512,64,512]{2,1,0:T(8,128)(2,1)} custom-call(bf16[512,16]{1,0:T(8,128)(2,1)} %copy.11.table_ref, s32[64,512]{1,0:T(8,128)} %onset_ref.3, bf16[2,2,32,512]{3,2,1,0:T(8,128)(2,1)} %respond.2.refs_0_, bf16[2,2,32,512]{3,2,1,0:T(8,128)(2,1)} %copy-done.8, bf16[2,2,32,512]{3,2,1,0:T(8,128)(2,1)} %copy-done.7, ...), custom_call_target="tpu_custom_call", output_to_operand_aliasing={{}: (6, {})} | custom-call | flops 4294967296 | bytes 16777216 | tf_op jit(solution)/shard_map/invert/pallas_call | solution.py:199
  (96 shorter events, 9.7 us)
Async XLA Ops:
  13.5 20.5 %collective-permute-start.13 = (bf16[2,2,32,512]{3,2,1,0:T(8,128)(2,1)}, bf16[2,2,32,512]{3,2,1,0:T(8,128)(2,1)S(1)}, u32[]{:S(2)}, u32[]{:S(2)}) collective-permute-start(bf16[2,2,32,512]{3,2,1,0:T(8,128)(2,1)} %get-tuple-element.18), channel_id=1, source_target_pairs={{0,8},{8,0},{16,24},{24,16},{1,9},{9,1},{17,25},{25,17},{2,10},{10... | collective-permute-start | bytes 393224 | tf_op jit(solution)/shard_map/ppermute | solution.py:226
  16.5 17.6 %collective-permute-start.14 = (bf16[2,2,32,512]{3,2,1,0:T(8,128)(2,1)}, bf16[2,2,32,512]{3,2,1,0:T(8,128)(2,1)S(1)}, u32[]{:S(2)}, u32[]{:S(2)}) collective-permute-start(bf16[2,2,32,512]{3,2,1,0:T(8,128)(2,1)} %get-tuple-element.19), channel_id=1, source_target_pairs={{0,16},{8,24},{16,0},{24,8},{1,17},{9,25},{17,1},{25,9},{2,18},{10... | collective-permute-start | bytes 393224 | tf_op jit(solution)/shard_map/ppermute | solution.py:226
  18.0 16.0 %collective-permute-start.15 = (bf16[2,2,32,512]{3,2,1,0:T(8,128)(2,1)}, bf16[2,2,32,512]{3,2,1,0:T(8,128)(2,1)S(1)}, u32[]{:S(2)}, u32[]{:S(2)}) collective-permute-start(bf16[2,2,32,512]{3,2,1,0:T(8,128)(2,1)} %get-tuple-element.20), channel_id=1, source_target_pairs={{0,24},{8,16},{16,8},{24,0},{1,25},{9,17},{17,9},{25,1},{2,26},{10... | collective-permute-start | bytes 393224 | tf_op jit(solution)/shard_map/ppermute | solution.py:226
  30.5 7.7 %collective-permute-start = (bf16[2,2,32,512]{3,2,1,0:T(8,128)(2,1)}, bf16[2,2,32,512]{3,2,1,0:T(8,128)(2,1)S(1)}, u32[]{:S(2)}, u32[]{:S(2)}) collective-permute-start(bf16[2,2,32,512]{3,2,1,0:T(8,128)(2,1)} %get-tuple-element.14), channel_id=1, source_target_pairs={{0,8},{8,0},{16,24},{24,16},{1,9},{9,1},{17,25},{25,17},{2,10},{10... | collective-permute-start | bytes 393224 | tf_op jit(solution)/shard_map/ppermute | solution.py:226
  32.5 7.9 %collective-permute-start.1 = (bf16[2,2,32,512]{3,2,1,0:T(8,128)(2,1)}, bf16[2,2,32,512]{3,2,1,0:T(8,128)(2,1)S(1)}, u32[]{:S(2)}, u32[]{:S(2)}) collective-permute-start(bf16[2,2,32,512]{3,2,1,0:T(8,128)(2,1)} %get-tuple-element.15), channel_id=1, source_target_pairs={{0,16},{8,24},{16,0},{24,8},{1,17},{9,25},{17,1},{25,9},{2,18},{10... | collective-permute-start | bytes 393224 | tf_op jit(solution)/shard_map/ppermute | solution.py:226
  34.0 6.4 %collective-permute-start.2 = (bf16[2,2,32,512]{3,2,1,0:T(8,128)(2,1)}, bf16[2,2,32,512]{3,2,1,0:T(8,128)(2,1)S(1)}, u32[]{:S(2)}, u32[]{:S(2)}) collective-permute-start(bf16[2,2,32,512]{3,2,1,0:T(8,128)(2,1)} %get-tuple-element.16), channel_id=1, source_target_pairs={{0,24},{8,16},{16,8},{24,0},{1,25},{9,17},{17,9},{25,1},{2,26},{10... | collective-permute-start | bytes 393224 | tf_op jit(solution)/shard_map/ppermute | solution.py:226
  34.1 11.0 %collective-permute-start.21 = (bf16[2,2,32,512]{3,2,1,0:T(8,128)(2,1)S(1)}, bf16[2,2,32,512]{3,2,1,0:T(8,128)(2,1)S(1)}, u32[]{:S(2)}, u32[]{:S(2)}) collective-permute-start(bf16[2,2,32,512]{3,2,1,0:T(8,128)(2,1)S(1)} %add_convert_fusion.refs_0_), channel_id=1, source_target_pairs={{0,6},{1,7},{2,4},{3,5},{4,2},{5,3},{6,0},{7,1},{8,14},{9,15},{10,... | collective-permute-start | bytes 393224 | tf_op jit(solution)/shard_map/ppermute | solution.py:226
  38.3 16.0 %collective-permute-start.19 = (bf16[2,2,32,512]{3,2,1,0:T(8,128)(2,1)S(1)}, bf16[2,2,32,512]{3,2,1,0:T(8,128)(2,1)S(1)}, u32[]{:S(2)}, u32[]{:S(2)}) collective-permute-start(bf16[2,2,32,512]{3,2,1,0:T(8,128)(2,1)S(1)} %add_convert_fusion.refs_0_), channel_id=1, source_target_pairs={{0,4},{1,5},{2,6},{3,7},{4,0},{5,1},{6,2},{7,3},{8,12},{9,13},{10,... | collective-permute-start | bytes 393224 | tf_op jit(solution)/shard_map/ppermute | solution.py:226
  38.3 16.7 %collective-permute-start.17 = (bf16[2,2,32,512]{3,2,1,0:T(8,128)(2,1)S(1)}, bf16[2,2,32,512]{3,2,1,0:T(8,128)(2,1)S(1)}, u32[]{:S(2)}, u32[]{:S(2)}) collective-permute-start(bf16[2,2,32,512]{3,2,1,0:T(8,128)(2,1)S(1)} %add_convert_fusion.refs_0_), channel_id=1, source_target_pairs={{0,2},{1,3},{2,0},{3,1},{4,6},{5,7},{6,4},{7,5},{8,10},{9,11},{10,... | collective-permute-start | bytes 393224 | tf_op jit(solution)/shard_map/ppermute | solution.py:226
  40.4 14.6 %collective-permute-start.16 = (bf16[2,2,32,512]{3,2,1,0:T(8,128)(2,1)S(1)}, bf16[2,2,32,512]{3,2,1,0:T(8,128)(2,1)S(1)}, u32[]{:S(2)}, u32[]{:S(2)}) collective-permute-start(bf16[2,2,32,512]{3,2,1,0:T(8,128)(2,1)S(1)} %add_convert_fusion.refs_0_), channel_id=1, source_target_pairs={{0,1},{1,0},{2,3},{3,2},{4,5},{5,4},{6,7},{7,6},{8,9},{9,8},{10,11... | collective-permute-start | bytes 393224 | tf_op jit(solution)/shard_map/ppermute | solution.py:226
  41.4 14.1 %collective-permute-start.8 = (bf16[2,2,32,512]{3,2,1,0:T(8,128)(2,1)S(1)}, bf16[2,2,32,512]{3,2,1,0:T(8,128)(2,1)S(1)}, u32[]{:S(2)}, u32[]{:S(2)}) collective-permute-start(bf16[2,2,32,512]{3,2,1,0:T(8,128)(2,1)S(1)} %add_convert_fusion.1.refs_0_), channel_id=1, source_target_pairs={{0,6},{1,7},{2,4},{3,5},{4,2},{5,3},{6,0},{7,1},{8,14},{9,15},{10,... | collective-permute-start | bytes 393224 | tf_op jit(solution)/shard_map/ppermute | solution.py:226
  45.1 13.9 %collective-permute-start.6 = (bf16[2,2,32,512]{3,2,1,0:T(8,128)(2,1)S(1)}, bf16[2,2,32,512]{3,2,1,0:T(8,128)(2,1)S(1)}, u32[]{:S(2)}, u32[]{:S(2)}) collective-permute-start(bf16[2,2,32,512]{3,2,1,0:T(8,128)(2,1)S(1)} %add_convert_fusion.1.refs_0_), channel_id=1, source_target_pairs={{0,4},{1,5},{2,6},{3,7},{4,0},{5,1},{6,2},{7,3},{8,12},{9,13},{10,... | collective-permute-start | bytes 393224 | tf_op jit(solution)/shard_map/ppermute | solution.py:226
  54.3 6.0 %collective-permute-start.4 = (bf16[2,2,32,512]{3,2,1,0:T(8,128)(2,1)S(1)}, bf16[2,2,32,512]{3,2,1,0:T(8,128)(2,1)S(1)}, u32[]{:S(2)}, u32[]{:S(2)}) collective-permute-start(bf16[2,2,32,512]{3,2,1,0:T(8,128)(2,1)S(1)} %add_convert_fusion.1.refs_0_), channel_id=1, source_target_pairs={{0,2},{1,3},{2,0},{3,1},{4,6},{5,7},{6,4},{7,5},{8,10},{9,11},{10,... | collective-permute-start | bytes 393224 | tf_op jit(solution)/shard_map/ppermute | solution.py:226
  55.0 6.3 %collective-permute-start.20 = (bf16[2,2,32,512]{3,2,1,0:T(8,128)(2,1)S(1)}, bf16[2,2,32,512]{3,2,1,0:T(8,128)(2,1)S(1)}, u32[]{:S(2)}, u32[]{:S(2)}) collective-permute-start(bf16[2,2,32,512]{3,2,1,0:T(8,128)(2,1)S(1)} %collective-permute-done.19.refs_4_), channel_id=1, source_target_pairs={{0,1},{1,0},{2,3},{3,2},{4,5},{5,4},{6,7},{7,6},{8,9},{9,8},{10,11... | collective-permute-start | bytes 393224 | tf_op jit(solution)/shard_map/ppermute | solution.py:226
  59.0 17.5 %collective-permute-start.3 = (bf16[2,2,32,512]{3,2,1,0:T(8,128)(2,1)S(1)}, bf16[2,2,32,512]{3,2,1,0:T(8,128)(2,1)S(1)}, u32[]{:S(2)}, u32[]{:S(2)}) collective-permute-start(bf16[2,2,32,512]{3,2,1,0:T(8,128)(2,1)S(1)} %add_convert_fusion.1.refs_0_), channel_id=1, source_target_pairs={{0,1},{1,0},{2,3},{3,2},{4,5},{5,4},{6,7},{7,6},{8,9},{9,8},{10,11... | collective-permute-start | bytes 393224 | tf_op jit(solution)/shard_map/ppermute | solution.py:226
  60.3 16.7 %collective-permute-start.9 = (bf16[2,2,32,512]{3,2,1,0:T(8,128)(2,1)S(1)}, bf16[2,2,32,512]{3,2,1,0:T(8,128)(2,1)S(1)}, u32[]{:S(2)}, u32[]{:S(2)}) collective-permute-start(bf16[2,2,32,512]{3,2,1,0:T(8,128)(2,1)S(1)} %collective-permute-done.8.refs_6_), channel_id=1, source_target_pairs={{0,1},{1,0},{2,3},{3,2},{4,5},{5,4},{6,7},{7,6},{8,9},{9,8},{10,11... | collective-permute-start | bytes 393224 | tf_op jit(solution)/shard_map/ppermute | solution.py:226
  60.8 17.8 %collective-permute-start.7 = (bf16[2,2,32,512]{3,2,1,0:T(8,128)(2,1)S(1)}, bf16[2,2,32,512]{3,2,1,0:T(8,128)(2,1)S(1)}, u32[]{:S(2)}, u32[]{:S(2)}) collective-permute-start(bf16[2,2,32,512]{3,2,1,0:T(8,128)(2,1)S(1)} %collective-permute-done.6.refs_4_), channel_id=1, source_target_pairs={{0,1},{1,0},{2,3},{3,2},{4,5},{5,4},{6,7},{7,6},{8,9},{9,8},{10,11... | collective-permute-start | bytes 393224 | tf_op jit(solution)/shard_map/ppermute | solution.py:226
  61.3 17.4 %collective-permute-start.5 = (bf16[2,2,32,512]{3,2,1,0:T(8,128)(2,1)S(1)}, bf16[2,2,32,512]{3,2,1,0:T(8,128)(2,1)S(1)}, u32[]{:S(2)}, u32[]{:S(2)}) collective-permute-start(bf16[2,2,32,512]{3,2,1,0:T(8,128)(2,1)S(1)} %collective-permute-done.4.refs_2_), channel_id=1, source_target_pairs={{0,1},{1,0},{2,3},{3,2},{4,5},{5,4},{6,7},{7,6},{8,9},{9,8},{10,11... | collective-permute-start | bytes 393224 | tf_op jit(solution)/shard_map/ppermute | solution.py:226
  74.4 20.0 %collective-permute-start.25 = (bf16[2,2,32,512]{3,2,1,0:T(8,128)(2,1)}, bf16[2,2,32,512]{3,2,1,0:T(8,128)(2,1)S(1)}, u32[]{:S(2)}, u32[]{:S(2)}) collective-permute-start(bf16[2,2,32,512]{3,2,1,0:T(8,128)(2,1)} %respond.3.refs_0_), channel_id=1, source_target_pairs={{0,24},{8,16},{16,8},{24,0},{1,25},{9,17},{17,9},{25,1},{2,26},{10... | collective-permute-start | bytes 393224 | tf_op jit(solution)/shard_map/ppermute | solution.py:226
  76.5 18.7 %collective-permute-start.24 = (bf16[2,2,32,512]{3,2,1,0:T(8,128)(2,1)}, bf16[2,2,32,512]{3,2,1,0:T(8,128)(2,1)S(1)}, u32[]{:S(2)}, u32[]{:S(2)}) collective-permute-start(bf16[2,2,32,512]{3,2,1,0:T(8,128)(2,1)} %respond.3.refs_0_), channel_id=1, source_target_pairs={{0,16},{8,24},{16,0},{24,8},{1,17},{9,25},{17,1},{25,9},{2,18},{10... | collective-permute-start | bytes 393224 | tf_op jit(solution)/shard_map/ppermute | solution.py:226
  77.0 18.2 %collective-permute-start.23 = (bf16[2,2,32,512]{3,2,1,0:T(8,128)(2,1)}, bf16[2,2,32,512]{3,2,1,0:T(8,128)(2,1)S(1)}, u32[]{:S(2)}, u32[]{:S(2)}) collective-permute-start(bf16[2,2,32,512]{3,2,1,0:T(8,128)(2,1)} %respond.3.refs_0_), channel_id=1, source_target_pairs={{0,8},{8,0},{16,24},{24,16},{1,9},{9,1},{17,25},{25,17},{2,10},{10... | collective-permute-start | bytes 393224 | tf_op jit(solution)/shard_map/ppermute | solution.py:226
  91.7 18.9 %collective-permute-start.12 = (bf16[2,2,32,512]{3,2,1,0:T(8,128)(2,1)}, bf16[2,2,32,512]{3,2,1,0:T(8,128)(2,1)S(1)}, u32[]{:S(2)}, u32[]{:S(2)}) collective-permute-start(bf16[2,2,32,512]{3,2,1,0:T(8,128)(2,1)} %respond.2.refs_0_), channel_id=1, source_target_pairs={{0,24},{8,16},{16,8},{24,0},{1,25},{9,17},{17,9},{25,1},{2,26},{10... | collective-permute-start | bytes 393224 | tf_op jit(solution)/shard_map/ppermute | solution.py:226
  93.8 16.8 %collective-permute-start.11 = (bf16[2,2,32,512]{3,2,1,0:T(8,128)(2,1)}, bf16[2,2,32,512]{3,2,1,0:T(8,128)(2,1)S(1)}, u32[]{:S(2)}, u32[]{:S(2)}) collective-permute-start(bf16[2,2,32,512]{3,2,1,0:T(8,128)(2,1)} %respond.2.refs_0_), channel_id=1, source_target_pairs={{0,16},{8,24},{16,0},{24,8},{1,17},{9,25},{17,1},{25,9},{2,18},{10... | collective-permute-start | bytes 393224 | tf_op jit(solution)/shard_map/ppermute | solution.py:226
  94.4 16.3 %collective-permute-start.10 = (bf16[2,2,32,512]{3,2,1,0:T(8,128)(2,1)}, bf16[2,2,32,512]{3,2,1,0:T(8,128)(2,1)S(1)}, u32[]{:S(2)}, u32[]{:S(2)}) collective-permute-start(bf16[2,2,32,512]{3,2,1,0:T(8,128)(2,1)} %respond.2.refs_0_), channel_id=1, source_target_pairs={{0,8},{8,0},{16,24},{24,16},{1,9},{9,1},{17,25},{25,17},{2,10},{10... | collective-permute-start | bytes 393224 | tf_op jit(solution)/shard_map/ppermute | solution.py:226
  (25 other events, 206.0 us)

commit v2 on v1

v2 whole, which is shorter than its diff:
```python
import functools
import math

import jax
import jax.numpy as jnp
from jax import lax
from jax.experimental import pallas as pl
from jax.experimental.pallas import tpu as pltpu
from jax.sharding import PartitionSpec as P

ROWS = 16
CHUNKS = 2
F_TIMES = 128
F_SLOTS = 3
I_TIMES = 128
I_SLOTS = 3
R_ROWS = 128
R_FLIGHT = 3
MIB = 1024 * 1024
F_VMEM = 40 * MIB
R_VMEM = 47 * MIB
I_VMEM = 24 * MIB
S_VMEM = 40 * MIB


def phases(bands, times, samples):
    return (bands * times % samples).astype(jnp.float32) * (2.0 * math.pi / samples)


def tables(per_device, freq_devices, local_times):
    me = lax.axis_index("freq")
    samples = local_times * freq_devices
    owners = me ^ jnp.arange(freq_devices, dtype=jnp.int32)
    bands = samples // 16 + (owners[:, None] * per_device + jnp.arange(per_device, dtype=jnp.int32)).reshape(-1)
    times = me * local_times + jnp.arange(local_times, dtype=jnp.int32)
    rows = phases(bands[:, None], times[None, :], samples)
    factor = 1.0 / math.sqrt(samples)
    forward = jnp.stack([jnp.cos(rows) * factor, -jnp.sin(rows) * factor], axis=1)
    columns = phases(bands[None, :], times[:, None], samples)
    factor = 1.0 / math.sqrt(per_device * freq_devices)
    inverse = jnp.stack([jnp.cos(columns) * factor, -jnp.sin(columns) * factor], axis=2)
    return (
        forward.reshape(-1, local_times).astype(jnp.bfloat16),
        inverse.reshape(local_times, -1).astype(jnp.bfloat16),
    )


def expand(table, rows):
    count = table.shape[1]
    lane = lax.broadcasted_iota(jnp.int32, (count, count * rows), 1)
    row = lax.broadcasted_iota(jnp.int32, (count, count * rows), 0)
    repeat = jnp.where(lane // rows == row, 1.0, 0.0).astype(jnp.bfloat16)
    return jnp.dot(table, repeat, preferred_element_type=jnp.float32)


def spread_rows(store, wide):
    lane = lax.broadcasted_iota(jnp.int32, (ROWS, wide.shape[1]), 1)
    row = lax.broadcasted_iota(jnp.int32, (ROWS, wide.shape[1]), 0)
    own = lane % ROWS == row
    for i in range(wide.shape[0]):
        store(i, jnp.where(own, wide[i : i + 1], 0.0).astype(jnp.bfloat16))


def forward_kernel(first, focal, table_ref, traces_ref, *refs):
    *outs, spread, total, slots, sems = refs
    depth, times, rows, width = slots.shape
    steps = spread.shape[0]
    count = steps * (focal // rows)

    def fetch(i):
        slot = lax.rem(i, depth)
        source = traces_ref.at[
            pl.ds(lax.rem(i, steps) * times, times), pl.ds(first + i // steps * rows, rows), :
        ]
        return pltpu.make_async_copy(source, slots.at[slot], sems.at[slot])

    for i in range(min(depth - 1, count)):
        fetch(jnp.int32(i)).start()

    for step in range(steps):

        def store(i, block, step=step):
            spread[step, pl.ds(i * rows, rows), :] = block

        spread_rows(store, expand(table_ref[:, pl.ds(step * times, times)], rows))

    @pl.loop(0, count)
    def _(i):
        step = lax.rem(i, steps)

        @pl.when(i + depth - 1 < count)
        def _():
            fetch(i + depth - 1).start()

        fetch(i).wait()
        block = slots[lax.rem(i, depth)].reshape(times * rows, width)
        part = jnp.dot(spread[step], block, preferred_element_type=jnp.float32)

        @pl.when(step == 0)
        def _():
            total[...] = part

        @pl.when(step > 0)
        def _():
            total[...] += part

        @pl.when(step == steps - 1)
        def _():
            share = total.shape[0] // len(outs)
            place = pl.ds(pl.multiple_of(i // steps * rows, rows), rows)
            for j, out in enumerate(outs):
                value = total[pl.ds(j * share, share), :].reshape(*out.shape[:2], rows, width)
                out[:, :, place, :] = value.astype(out.dtype)


def forward(table, traces, first, focal, per_device, freq_devices):
    local_times, _, width = traces.shape
    times = min(F_TIMES, local_times)
    steps = local_times // times
    count = 2 * per_device * freq_devices
    shape = (per_device, 2, focal, width)
    whole = pl.BlockSpec(memory_space=pltpu.VMEM)
    return pl.pallas_call(
        functools.partial(forward_kernel, first, focal),
        in_specs=[whole, pl.BlockSpec(memory_space=pl.ANY)],
        out_specs=[whole] * freq_devices,
        out_shape=[jax.ShapeDtypeStruct(shape, jnp.float32 if i == 0 else jnp.bfloat16) for i in range(freq_devices)],
        scratch_shapes=[
            pltpu.VMEM((steps, count * ROWS, times * ROWS), jnp.bfloat16),
            pltpu.VMEM((count * ROWS, width), jnp.float32),
            pltpu.VMEM((F_SLOTS, times, ROWS, width), jnp.bfloat16),
            pltpu.SemaphoreType.DMA((F_SLOTS,)),
        ],
        compiler_params=pltpu.CompilerParams(vmem_limit_bytes=F_VMEM),
        cost_estimate=pl.CostEstimate(
            flops=2 * count * ROWS * local_times * focal * width,
            bytes_accessed=2 * local_times * focal * width,
            transcendentals=0,
        ),
        name="forward",
    )(table, traces)


def response_kernel(place_ref, reflection_ref, own_ref, other_ref, out, spectra, slots, sems):
    bands, cuts, _, rows, sources = slots.shape
    _, _, _, focal, width = own_ref.shape

    def fetch(band, cut):
        source = reflection_ref.at[band, :, pl.ds(cut * rows, rows), :]
        return pltpu.make_async_copy(source, slots.at[band, cut], sems.at[band, cut])

    order = [(band, cut) for band in range(bands) for cut in range(cuts)]
    for block in order[:R_FLIGHT]:
        fetch(*block).start()
    for i in range(2 * own_ref.shape[0]):
        start = pl.multiple_of(place_ref[i] * width, width)
        for band in range(bands):
            piece = (own_ref, other_ref)[i % 2][i // 2, band].reshape(2 * focal, width)
            spectra[band, pl.ds(start, width), :] = piece.T
    for i, (band, cut) in enumerate(order):
        fetch(band, cut).wait()
        for block in order[i + R_FLIGHT : i + R_FLIGHT + 1]:
            fetch(*block).start()
        product = jnp.dot(
            slots[band, cut].reshape(2 * rows, sources), spectra[band], preferred_element_type=jnp.float32
        ).T
        place = pl.ds(cut * rows, rows)
        out[band, 0, :, place] = (product[:focal, :rows] - product[focal:, rows:]).astype(out.dtype)
        out[band, 1, :, place] = (product[focal:, :rows] + product[:focal, rows:]).astype(out.dtype)


def respond(reflection, places, own, other):
    per_device, _, width, sources = reflection.shape
    focal = own.shape[3]
    cuts = max(1, width // R_ROWS)
    whole = pl.BlockSpec(memory_space=pltpu.VMEM)
    return pl.pallas_call(
        response_kernel,
        in_specs=[pl.BlockSpec(memory_space=pltpu.SMEM), pl.BlockSpec(memory_space=pl.ANY), whole, whole],
        out_specs=whole,
        out_shape=jax.ShapeDtypeStruct((per_device, 2, focal, width), jnp.bfloat16),
        scratch_shapes=[
            pltpu.VMEM((per_device, sources, 2 * focal), jnp.bfloat16),
            pltpu.VMEM((per_device, cuts, 2, width // cuts, sources), jnp.bfloat16),
            pltpu.SemaphoreType.DMA((per_device, cuts)),
        ],
        compiler_params=pltpu.CompilerParams(vmem_limit_bytes=R_VMEM),
        cost_estimate=pl.CostEstimate(
            flops=8 * per_device * focal * width * sources,
            bytes_accessed=4 * per_device * width * sources,
            transcendentals=0,
        ),
        name="respond",
    )(places, reflection, own, other)


def inverse_kernel(first, has_before, table_ref, onset_ref, *refs):
    pieces, (out, spread, weights, slots, sems) = refs[: -5 - has_before], refs[-5:]
    depth, times, rows, width = slots.shape
    focal = pieces[0].shape[2]
    local_times = out.shape[0]
    steps = local_times // times
    count = steps * (focal // rows)
    share = weights.shape[0] // len(pieces)
    begin = lax.axis_index("freq") * local_times

    def store(i, block):
        spread[pl.ds(i * rows, rows), :] = block

    spread_rows(store, expand(table_ref[...], rows))

    def send(i):
        slot = lax.rem(i, depth)
        target = out.at[pl.ds(lax.rem(i, steps) * times, times), pl.ds(first + i // steps * rows, rows), :]
        return pltpu.make_async_copy(slots.at[slot], target, sems.at[slot])

    @pl.loop(0, count)
    def _(i):
        step = lax.rem(i, steps)
        slot = lax.rem(i, depth)
        place = pl.ds(pl.multiple_of(i // steps * rows, rows), rows)

        @pl.when(i >= depth)
        def _():
            send(i - depth).wait()

        @pl.when(step == 0)
        def _():
            for j, piece in enumerate(pieces):
                weights[pl.ds(j * share, share), :] = piece[:, :, place, :].reshape(share, width)

        lines = pl.ds(pl.multiple_of(step * times * rows, times * rows), times * rows)
        signal = jnp.dot(spread[lines, :], weights[...], preferred_element_type=jnp.float32)
        signal = signal.reshape(times, rows, width)
        moment = begin + step * times + lax.broadcasted_iota(jnp.int32, (times, 1, 1), 0)
        onset = onset_ref[pl.ds(pl.multiple_of(first + i // steps * rows, rows), rows), :]
        slots[slot] = jnp.where(moment < onset[None], signal, 0.0).astype(out.dtype)
        send(i).start()

    for i in range(max(0, count - depth), count):
        send(jnp.int32(i)).wait()


def invert(table, onset, pieces, before, first, shape):
    local_times, _, width = shape
    focal = pieces[0].shape[2]
    times = min(I_TIMES, local_times)
    has_before = before is not None
    operands = [table, onset, *pieces] + ([before] if has_before else [])
    whole = pl.BlockSpec(memory_space=pltpu.VMEM)
    anywhere = pl.BlockSpec(memory_space=pl.ANY)
    return pl.pallas_call(
        functools.partial(inverse_kernel, first, has_before),
        in_specs=[whole] * (2 + len(pieces)) + [anywhere] * has_before,
        out_specs=anywhere,
        out_shape=jax.ShapeDtypeStruct(shape, jnp.bfloat16),
        scratch_shapes=[
            pltpu.VMEM((local_times * ROWS, table.shape[1] * ROWS), jnp.bfloat16),
            pltpu.VMEM((table.shape[1] * ROWS, width), jnp.bfloat16),
            pltpu.VMEM((I_SLOTS, times, ROWS, width), jnp.bfloat16),
            pltpu.SemaphoreType.DMA((I_SLOTS,)),
        ],
        input_output_aliases={len(operands) - 1: 0} if has_before else {},
        compiler_params=pltpu.CompilerParams(vmem_limit_bytes=I_VMEM),
        cost_estimate=pl.CostEstimate(
            flops=2 * table.shape[1] * ROWS * local_times * focal * width,
            bytes_accessed=2 * local_times * focal * width,
            transcendentals=0,
        ),
        name="invert",
    )(*operands)


def stack_kernel(*refs):
    *pieces, _, out = refs
    for i, piece in enumerate(pieces):
        out[i] = piece[...]


def stack(pieces, earlier):
    whole = pl.BlockSpec(memory_space=pltpu.VMEM)
    return pl.pallas_call(
        stack_kernel,
        in_specs=[whole] * len(pieces) + [pl.BlockSpec(memory_space=pl.ANY)],
        out_specs=whole,
        out_shape=jax.ShapeDtypeStruct((len(pieces), *pieces[0].shape), pieces[0].dtype),
        compiler_params=pltpu.CompilerParams(vmem_limit_bytes=S_VMEM),
        name="stack",
    )(*pieces, earlier)


def swap(array, axis, mask):
    return lax.ppermute(array, axis, [(i, i ^ mask) for i in range(lax.axis_size(axis))])


def on_device(traces, reflection, onset):
    local_times, focal_count, _ = traces.shape
    freq_devices, mat_devices = lax.axis_size("freq"), lax.axis_size("mat")
    per_device = reflection.shape[0]
    forward_table, inverse_table = tables(per_device, freq_devices, local_times)
    focal = focal_count // CHUNKS

    masks = list(range(0, mat_devices, 2))
    places = lax.axis_index("mat") ^ jnp.array([m ^ c for m in masks for c in (0, 1)], jnp.int32)

    parts = [
        forward(forward_table, traces, i * focal, focal, per_device, freq_devices) for i in range(CHUNKS)
    ]
    spectra = []
    for part in parts:
        total = part[0]
        for mask in range(1, freq_devices):
            total = total + swap(part[mask], "freq", mask).astype(jnp.float32)
        spectra.append(total.astype(jnp.bfloat16))
    gathered = [[swap(own, "mat", mask) if mask else own for mask in masks] for own in spectra]
    responses = []
    for i, pieces in enumerate(gathered):
        own = stack(pieces, responses[-1][0] if responses else spectra[-1])
        response = respond(reflection, places, own, swap(own, "mat", 1))
        responses.append([response] + [swap(response, "freq", mask) for mask in range(1, freq_devices)])
    windowed = None
    for i, pieces in enumerate(responses):
        windowed = invert(inverse_table, onset, pieces, windowed, i * focal, traces.shape)
    return windowed


def solution(mesh):
    placed = (P("freq", None, "mat"), P("freq", None, "mat", None), P(None, "mat"))
    return jax.shard_map(
        on_device, mesh=mesh, in_specs=placed, out_specs=P("freq", None, "mat"), check_vma=False
    )
```

time: 128 us -> 85.3 us (0.67); the launches traced: 126 us -> 85.2 us
  Pallas kernels: 76.8 us -> 50.2 us
  local copies, waits for them, and re-layouts: 6.6 us -> 0.27 us
  starting transfers between devices: 28.6 us -> 24.6 us
  waiting for transfers between devices: 12 us -> 9.19 us
  other arithmetic: 2.01 us -> 0.53 us
    pallas_call x6 -> x8, Pallas kernels: 76.8 us -> 50.2 us  [the longest x2 17.5 us: respond(): pl.pallas_call(response_kernel, in_specs=[pl.BlockSpec(memory_space=pltpu...]
    unnamed x46 -> x2, local copies, waits for them, and re-layouts: 5.09 us -> 0.01 us
    ppermute x26 -> x20, starting transfers between devices: 28.6 us -> 24.6 us  [swap(): lax.ppermute(array, axis, [(i, i ^ mask) for i in range(lax.axis_size(axi...]
    ppermute x26 -> x20, waiting for transfers between devices: 12 us -> 9.19 us  [swap(): lax.ppermute(array, axis, [(i, i ^ mask) for i in range(lax.axis_size(axi...]
  transfers between devices with their start and end apart: 26 -> 20, of which waited for: 4 -> 4; matrix products, arithmetic and copies ran while one was open for 2% -> 1% of each run, Pallas kernels for 40% -> 40%
where the time goes in v2:
time: 85.3 us; the launch traced here: 85.2 us
  Pallas kernels  50.2 us (59%)
  starting transfers between devices  24.6 us (29%)
  waiting for transfers between devices  9.19 us (11%)
    ppermute x20, starting transfers between devices, swap(): lax.ppermute(array, axis, [(i, i ^ mask) for i in range(lax.axis_size(axi...  24.6 us
    pallas_call x2, Pallas kernels, respond(): pl.pallas_call(response_kernel, in_specs=[pl.BlockSpec(memory_space=pltpu...  17.5 us
    pallas_call x2, Pallas kernels, forward(): pl.pallas_call(functools.partial(forward_kernel, first, focal), in_specs=...  16.9 us
    pallas_call x2, Pallas kernels, invert(): pl.pallas_call(functools.partial(inverse_kernel, first, has_before), in_s...  15.7 us
    ppermute x20, waiting for transfers between devices, swap(): lax.ppermute(array, axis, [(i, i ^ mask) for i in range(lax.axis_size(axi...  9.19 us
  transfers between devices with their start and end apart: 20, of which 4 were waited for; matrix products, arithmetic and copies ran while one was open for 1% of the time, Pallas kernels for 40%

profile of v2, /device:TPU:0, one launch (start us, length us, event | category | flops | bytes accessed | tf_op | source)
XLA Modules:
  0.0 85.2 jit_solution(8088784185798253940)
XLA Ops:
  0.4 8.4 %forward.3 = (f32[2,2,32,512]{3,2,1,0:T(8,128)S(1)}, bf16[2,2,32,512]{3,2,1,0:T(8,128)(2,1)S(1)}, bf16[2,2,32,512]{3,2,1,0:T(8,128)(2,1)S(1)}, bf16[2,2,32,512]{3,2,1,0:T(8,128)(2,1)S(1)}) custom-call(bf16[16,512]{1,0:T(8,128)(2,1)S(1)} %convert_element_type.61.table_ref, bf16[512,64,512]{2,1,0:T(8,128)(2,1)} %traces_ref.3), custom_call_target="tpu_custom_call" | custom-call | flops 4294967296 | bytes 16777216 | tf_op jit(solution)/shard_map/forward/pallas_call | solution.py:123
  8.8 3.0 %collective-permute-start.6 = (bf16[2,2,32,512]{3,2,1,0:T(8,128)(2,1)S(1)}, bf16[2,2,32,512]{3,2,1,0:T(8,128)(2,1)S(1)}, u32[]{:S(2)}, u32[]{:S(2)}) collective-permute-start(bf16[2,2,32,512]{3,2,1,0:T(8,128)(2,1)S(1)} %get-tuple-element.18), channel_id=1, source_target_pairs={{0,8},{8,0},{16,24},{24,16},{1,9},{9,1},{17,25},{25,17},{2,10},{10... | collective-permute-start | bytes 393224 | tf_op jit(solution)/shard_map/ppermute | solution.py:293
  11.8 1.5 %collective-permute-start.7 = (bf16[2,2,32,512]{3,2,1,0:T(8,128)(2,1)S(1)}, bf16[2,2,32,512]{3,2,1,0:T(8,128)(2,1)S(1)}, u32[]{:S(2)}, u32[]{:S(2)}) collective-permute-start(bf16[2,2,32,512]{3,2,1,0:T(8,128)(2,1)S(1)} %get-tuple-element.19), channel_id=1, source_target_pairs={{0,16},{8,24},{16,0},{24,8},{1,17},{9,25},{17,1},{25,9},{2,18},{10... | collective-permute-start | bytes 393224 | tf_op jit(solution)/shard_map/ppermute | solution.py:293
  13.3 8.5 %forward.2 = (f32[2,2,32,512]{3,2,1,0:T(8,128)S(1)}, bf16[2,2,32,512]{3,2,1,0:T(8,128)(2,1)S(1)}, bf16[2,2,32,512]{3,2,1,0:T(8,128)(2,1)S(1)}, bf16[2,2,32,512]{3,2,1,0:T(8,128)(2,1)S(1)}) custom-call(bf16[16,512]{1,0:T(8,128)(2,1)S(1)} %convert_element_type.61.table_ref, bf16[512,64,512]{2,1,0:T(8,128)(2,1)} %traces_ref.3), custom_call_target="tpu_custom_call" | custom-call | flops 4294967296 | bytes 16777216 | tf_op jit(solution)/shard_map/forward/pallas_call | solution.py:123
  21.9 2.0 %collective-permute-start = (bf16[2,2,32,512]{3,2,1,0:T(8,128)(2,1)S(1)}, bf16[2,2,32,512]{3,2,1,0:T(8,128)(2,1)S(1)}, u32[]{:S(2)}, u32[]{:S(2)}) collective-permute-start(bf16[2,2,32,512]{3,2,1,0:T(8,128)(2,1)S(1)} %get-tuple-element.14), channel_id=1, source_target_pairs={{0,8},{8,0},{16,24},{24,16},{1,9},{9,1},{17,25},{25,17},{2,10},{10... | collective-permute-start | bytes 393224 | tf_op jit(solution)/shard_map/ppermute | solution.py:293
  23.9 1.5 %collective-permute-start.1 = (bf16[2,2,32,512]{3,2,1,0:T(8,128)(2,1)S(1)}, bf16[2,2,32,512]{3,2,1,0:T(8,128)(2,1)S(1)}, u32[]{:S(2)}, u32[]{:S(2)}) collective-permute-start(bf16[2,2,32,512]{3,2,1,0:T(8,128)(2,1)S(1)} %get-tuple-element.15), channel_id=1, source_target_pairs={{0,16},{8,24},{16,0},{24,8},{1,17},{9,25},{17,1},{25,9},{2,18},{10... | collective-permute-start | bytes 393224 | tf_op jit(solution)/shard_map/ppermute | solution.py:293
  25.5 4.1 %collective-permute-start.11 = (bf16[2,2,32,512]{3,2,1,0:T(8,128)(2,1)S(1)}, bf16[2,2,32,512]{3,2,1,0:T(8,128)(2,1)S(1)}, u32[]{:S(2)}, u32[]{:S(2)}) collective-permute-start(bf16[2,2,32,512]{3,2,1,0:T(8,128)(2,1)S(1)} %add_convert_fusion.refs_0_), channel_id=1, source_target_pairs={{0,6},{1,7},{2,4},{3,5},{4,2},{5,3},{6,0},{7,1},{8,14},{9,15},{10,... | collective-permute-start | bytes 393224 | tf_op jit(solution)/shard_map/ppermute | solution.py:293
  29.6 0.6 collective-permute-start.9
  30.3 1.3 %collective-permute-done.1 = bf16[2,2,32,512]{3,2,1,0:T(8,128)(2,1)S(1)} collective-permute-done((bf16[2,2,32,512]{3,2,1,0:T(8,128)(2,1)S(1)}, bf16[2,2,32,512]{3,2,1,0:T(8,128)(2,1)S(1)}, u32[]{:S(2)}, u32[]{:S(2)}) %collective-permute-start.1) | collective-permute-done | bytes 131104 | tf_op jit(solution)/shard_map/ppermute | solution.py:293
  31.6 2.0 %collective-permute-done.11.refs_3_ = bf16[2,2,32,512]{3,2,1,0:T(8,128)(2,1)S(1)} collective-permute-done((bf16[2,2,32,512]{3,2,1,0:T(8,128)(2,1)S(1)}, bf16[2,2,32,512]{3,2,1,0:T(8,128)(2,1)S(1)}, u32[]{:S(2)}, u32[]{:S(2)}) %collective-permute-start.11) | collective-permute-done | bytes 131104 | tf_op jit(solution)/shard_map/ppermute | solution.py:293
  33.6 5.4 %collective-permute-done.10.refs_2_ = bf16[2,2,32,512]{3,2,1,0:T(8,128)(2,1)S(1)} collective-permute-done((bf16[2,2,32,512]{3,2,1,0:T(8,128)(2,1)S(1)}, bf16[2,2,32,512]{3,2,1,0:T(8,128)(2,1)S(1)}, u32[]{:S(2)}, u32[]{:S(2)}) %collective-permute-start.10) | collective-permute-done | bytes 131104 | tf_op jit(solution)/shard_map/ppermute | solution.py:293
  39.1 2.5 %collective-permute-start.5 = (bf16[2,2,32,512]{3,2,1,0:T(8,128)(2,1)S(1)}, bf16[2,2,32,512]{3,2,1,0:T(8,128)(2,1)S(1)}, u32[]{:S(2)}, u32[]{:S(2)}) collective-permute-start(bf16[2,2,32,512]{3,2,1,0:T(8,128)(2,1)S(1)} %add_convert_fusion.1.refs_4_.refs_0_), channel_id=1, source_target_pairs={{0,6},{1,7},{2,4},{3,5},{4,2},{5,3},{6,0},{7,1},{8,14},{9,15},{10,... | collective-permute-start | bytes 393224 | tf_op jit(solution)/shard_map/ppermute | solution.py:293
  41.7 1.9 %collective-permute-start.3 = (bf16[2,2,32,512]{3,2,1,0:T(8,128)(2,1)S(1)}, bf16[2,2,32,512]{3,2,1,0:T(8,128)(2,1)S(1)}, u32[]{:S(2)}, u32[]{:S(2)}) collective-permute-start(bf16[2,2,32,512]{3,2,1,0:T(8,128)(2,1)S(1)} %add_convert_fusion.1.refs_4_.refs_0_), channel_id=1, source_target_pairs={{0,2},{1,3},{2,0},{3,1},{4,6},{5,7},{6,4},{7,5},{8,10},{9,11},{10,... | collective-permute-start | bytes 393224 | tf_op jit(solution)/shard_map/ppermute | solution.py:293
  43.6 8.6 %respond.2.refs_4_.refs_0_ = bf16[2,2,32,512]{3,2,1,0:T(8,128)(2,1)S(1)} custom-call(s32[8]{0:T(128)S(1)} %iota_xor_fusion.place_ref, bf16[2,2,512,4096]{3,2,1,0:T(8,128)(2,1)} %reflection_ref.3, bf16[4,2,2,32,512]{4,3,2,1,0:T(8,128)(2,1)S(1)} %stack.16.own_ref, bf16[4,2,2,32,512]{4,3,2,1,0:T(8,128)(2,1)S(1)} %collective-permute-done.12.other_ref), custom_call_target="tpu_custom_call" | custom-call | flops 1073741824 | bytes 16777216 | tf_op jit(solution)/shard_map/respond/pallas_call | solution.py:177
  52.2 0.5 collective-permute-done.4.refs_2_
  53.0 2.5 %collective-permute-start.19 = (bf16[2,2,32,512]{3,2,1,0:T(8,128)(2,1)S(1)}, bf16[2,2,32,512]{3,2,1,0:T(8,128)(2,1)S(1)}, u32[]{:S(2)}, u32[]{:S(2)}) collective-permute-start(bf16[2,2,32,512]{3,2,1,0:T(8,128)(2,1)S(1)} %respond.2.refs_4_.refs_0_), channel_id=1, source_target_pairs={{0,24},{8,16},{16,8},{24,0},{1,25},{9,17},{17,9},{25,1},{2,26},{10... | collective-permute-start | bytes 393224 | tf_op jit(solution)/shard_map/ppermute | solution.py:293
  55.5 0.5 collective-permute-start.18
  56.0 0.5 collective-permute-start.17
  56.7 8.9 %respond.3.refs_0_ = bf16[2,2,32,512]{3,2,1,0:T(8,128)(2,1)S(1)} custom-call(s32[8]{0:T(128)S(1)} %iota_xor_fusion.place_ref, bf16[2,2,512,4096]{3,2,1,0:T(8,128)(2,1)} %reflection_ref.3, bf16[4,2,2,32,512]{4,3,2,1,0:T(8,128)(2,1)S(1)} %stack.17.own_ref, bf16[4,2,2,32,512]{4,3,2,1,0:T(8,128)(2,1)S(1)} %collective-permute-done.13.other_ref), custom_call_target="tpu_custom_call" | custom-call | flops 1073741824 | bytes 16777216 | tf_op jit(solution)/shard_map/respond/pallas_call | solution.py:177
  65.6 2.5 %collective-permute-start.16 = (bf16[2,2,32,512]{3,2,1,0:T(8,128)(2,1)S(1)}, bf16[2,2,32,512]{3,2,1,0:T(8,128)(2,1)S(1)}, u32[]{:S(2)}, u32[]{:S(2)}) collective-permute-start(bf16[2,2,32,512]{3,2,1,0:T(8,128)(2,1)S(1)} %respond.3.refs_0_), channel_id=1, source_target_pairs={{0,24},{8,16},{16,8},{24,0},{1,25},{9,17},{17,9},{25,1},{2,26},{10... | collective-permute-start | bytes 393224 | tf_op jit(solution)/shard_map/ppermute | solution.py:293
  68.1 0.5 collective-permute-start.15
  68.7 0.5 collective-permute-start.14
  69.2 7.9 %invert.2.refs_4_ = bf16[512,64,512]{2,1,0:T(8,128)(2,1)} custom-call(bf16[512,16]{1,0:T(8,128)(2,1)S(1)} %copy.11.table_ref, s32[64,512]{1,0:T(8,128)S(1)} %copy-done, bf16[2,2,32,512]{3,2,1,0:T(8,128)(2,1)S(1)} %respond.2.refs_4_.refs_0_, bf16[2,2,32,512]{3,2,1,0:T(8,128)(2,1)S(1)} %collective-permute-done.17.refs_1_, ...), custom_call_target="tpu_custom_call" | custom-call | flops 4294967296 | bytes 16777216 | tf_op jit(solution)/shard_map/invert/pallas_call | solution.py:252
  77.1 7.9 %invert.3 = bf16[512,64,512]{2,1,0:T(8,128)(2,1)} custom-call(bf16[512,16]{1,0:T(8,128)(2,1)S(1)} %copy.11.table_ref, s32[64,512]{1,0:T(8,128)S(1)} %copy-done, bf16[2,2,32,512]{3,2,1,0:T(8,128)(2,1)S(1)} %respond.3.refs_0_, bf16[2,2,32,512]{3,2,1,0:T(8,128)(2,1)S(1)} %collective-permute-done.14.refs_1_, ...), custom_call_target="tpu_custom_call", output_to_operand_aliasing={{}: (6, {})} | custom-call | flops 4294967296 | bytes 16777216 | tf_op jit(solution)/shard_map/invert/pallas_call | solution.py:252
  (42 shorter events, 1.1 us)
Async XLA Ops:
  8.8 16.6 %collective-permute-start.6 = (bf16[2,2,32,512]{3,2,1,0:T(8,128)(2,1)S(1)}, bf16[2,2,32,512]{3,2,1,0:T(8,128)(2,1)S(1)}, u32[]{:S(2)}, u32[]{:S(2)}) collective-permute-start(bf16[2,2,32,512]{3,2,1,0:T(8,128)(2,1)S(1)} %get-tuple-element.18), channel_id=1, source_target_pairs={{0,8},{8,0},{16,24},{24,16},{1,9},{9,1},{17,25},{25,17},{2,10},{10... | collective-permute-start | bytes 393224 | tf_op jit(solution)/shard_map/ppermute | solution.py:293
  11.8 13.7 %collective-permute-start.7 = (bf16[2,2,32,512]{3,2,1,0:T(8,128)(2,1)S(1)}, bf16[2,2,32,512]{3,2,1,0:T(8,128)(2,1)S(1)}, u32[]{:S(2)}, u32[]{:S(2)}) collective-permute-start(bf16[2,2,32,512]{3,2,1,0:T(8,128)(2,1)S(1)} %get-tuple-element.19), channel_id=1, source_target_pairs={{0,16},{8,24},{16,0},{24,8},{1,17},{9,25},{17,1},{25,9},{2,18},{10... | collective-permute-start | bytes 393224 | tf_op jit(solution)/shard_map/ppermute | solution.py:293
  13.3 55.9 %copy-start = (s32[64,512]{1,0:T(8,128)S(1)}, s32[64,512]{1,0:T(8,128)}, u32[]{:S(2)}) copy-start(s32[64,512]{1,0:T(8,128)} %onset_ref.3) | copy-start | bytes 393220
  13.3 12.1 %collective-permute-start.8 = (bf16[2,2,32,512]{3,2,1,0:T(8,128)(2,1)S(1)}, bf16[2,2,32,512]{3,2,1,0:T(8,128)(2,1)S(1)}, u32[]{:S(2)}, u32[]{:S(2)}) collective-permute-start(bf16[2,2,32,512]{3,2,1,0:T(8,128)(2,1)S(1)} %get-tuple-element.20), channel_id=1, source_target_pairs={{0,24},{8,16},{16,8},{24,0},{1,25},{9,17},{17,9},{25,1},{2,26},{10... | collective-permute-start | bytes 393224 | tf_op jit(solution)/shard_map/ppermute | solution.py:293
  21.9 7.8 %collective-permute-start = (bf16[2,2,32,512]{3,2,1,0:T(8,128)(2,1)S(1)}, bf16[2,2,32,512]{3,2,1,0:T(8,128)(2,1)S(1)}, u32[]{:S(2)}, u32[]{:S(2)}) collective-permute-start(bf16[2,2,32,512]{3,2,1,0:T(8,128)(2,1)S(1)} %get-tuple-element.14), channel_id=1, source_target_pairs={{0,8},{8,0},{16,24},{24,16},{1,9},{9,1},{17,25},{25,17},{2,10},{10... | collective-permute-start | bytes 393224 | tf_op jit(solution)/shard_map/ppermute | solution.py:293
  23.9 7.7 %collective-permute-start.1 = (bf16[2,2,32,512]{3,2,1,0:T(8,128)(2,1)S(1)}, bf16[2,2,32,512]{3,2,1,0:T(8,128)(2,1)S(1)}, u32[]{:S(2)}, u32[]{:S(2)}) collective-permute-start(bf16[2,2,32,512]{3,2,1,0:T(8,128)(2,1)S(1)} %get-tuple-element.15), channel_id=1, source_target_pairs={{0,16},{8,24},{16,0},{24,8},{1,17},{9,25},{17,1},{25,9},{2,18},{10... | collective-permute-start | bytes 393224 | tf_op jit(solution)/shard_map/ppermute | solution.py:293
  25.4 6.2 %collective-permute-start.2 = (bf16[2,2,32,512]{3,2,1,0:T(8,128)(2,1)S(1)}, bf16[2,2,32,512]{3,2,1,0:T(8,128)(2,1)S(1)}, u32[]{:S(2)}, u32[]{:S(2)}) collective-permute-start(bf16[2,2,32,512]{3,2,1,0:T(8,128)(2,1)S(1)} %get-tuple-element.16), channel_id=1, source_target_pairs={{0,24},{8,16},{16,8},{24,0},{1,25},{9,17},{17,9},{25,1},{2,26},{10... | collective-permute-start | bytes 393224 | tf_op jit(solution)/shard_map/ppermute | solution.py:293
  25.5 8.1 %collective-permute-start.11 = (bf16[2,2,32,512]{3,2,1,0:T(8,128)(2,1)S(1)}, bf16[2,2,32,512]{3,2,1,0:T(8,128)(2,1)S(1)}, u32[]{:S(2)}, u32[]{:S(2)}) collective-permute-start(bf16[2,2,32,512]{3,2,1,0:T(8,128)(2,1)S(1)} %add_convert_fusion.refs_0_), channel_id=1, source_target_pairs={{0,6},{1,7},{2,4},{3,5},{4,2},{5,3},{6,0},{7,1},{8,14},{9,15},{10,... | collective-permute-start | bytes 393224 | tf_op jit(solution)/shard_map/ppermute | solution.py:293
  29.6 9.4 %collective-permute-start.10 = (bf16[2,2,32,512]{3,2,1,0:T(8,128)(2,1)S(1)}, bf16[2,2,32,512]{3,2,1,0:T(8,128)(2,1)S(1)}, u32[]{:S(2)}, u32[]{:S(2)}) collective-permute-start(bf16[2,2,32,512]{3,2,1,0:T(8,128)(2,1)S(1)} %add_convert_fusion.refs_0_), channel_id=1, source_target_pairs={{0,4},{1,5},{2,6},{3,7},{4,0},{5,1},{6,2},{7,3},{8,12},{9,13},{10,... | collective-permute-start | bytes 393224 | tf_op jit(solution)/shard_map/ppermute | solution.py:293
  29.6 9.4 %collective-permute-start.9 = (bf16[2,2,32,512]{3,2,1,0:T(8,128)(2,1)S(1)}, bf16[2,2,32,512]{3,2,1,0:T(8,128)(2,1)S(1)}, u32[]{:S(2)}, u32[]{:S(2)}) collective-permute-start(bf16[2,2,32,512]{3,2,1,0:T(8,128)(2,1)S(1)} %add_convert_fusion.refs_0_), channel_id=1, source_target_pairs={{0,2},{1,3},{2,0},{3,1},{4,6},{5,7},{6,4},{7,5},{8,10},{9,11},{10,... | collective-permute-start | bytes 393224 | tf_op jit(solution)/shard_map/ppermute | solution.py:293
  39.0 4.5 %collective-permute-start.12 = (bf16[4,2,2,32,512]{4,3,2,1,0:T(8,128)(2,1)S(1)}, bf16[4,2,2,32,512]{4,3,2,1,0:T(8,128)(2,1)S(1)}, u32[]{:S(2)}, u32[]{:S(2)}) collective-permute-start(bf16[4,2,2,32,512]{4,3,2,1,0:T(8,128)(2,1)S(1)} %stack.16.own_ref), channel_id=1, source_target_pairs={{0,1},{1,0},{2,3},{3,2},{4,5},{5,4},{6,7},{7,6},{8,9},{9,8},{10,11... | collective-permute-start | bytes 1572872 | tf_op jit(solution)/shard_map/ppermute | solution.py:293
  39.1 13.1 %collective-permute-start.5 = (bf16[2,2,32,512]{3,2,1,0:T(8,128)(2,1)S(1)}, bf16[2,2,32,512]{3,2,1,0:T(8,128)(2,1)S(1)}, u32[]{:S(2)}, u32[]{:S(2)}) collective-permute-start(bf16[2,2,32,512]{3,2,1,0:T(8,128)(2,1)S(1)} %add_convert_fusion.1.refs_4_.refs_0_), channel_id=1, source_target_pairs={{0,6},{1,7},{2,4},{3,5},{4,2},{5,3},{6,0},{7,1},{8,14},{9,15},{10,... | collective-permute-start | bytes 393224 | tf_op jit(solution)/shard_map/ppermute | solution.py:293
  41.7 11.1 %collective-permute-start.4 = (bf16[2,2,32,512]{3,2,1,0:T(8,128)(2,1)S(1)}, bf16[2,2,32,512]{3,2,1,0:T(8,128)(2,1)S(1)}, u32[]{:S(2)}, u32[]{:S(2)}) collective-permute-start(bf16[2,2,32,512]{3,2,1,0:T(8,128)(2,1)S(1)} %add_convert_fusion.1.refs_4_.refs_0_), channel_id=1, source_target_pairs={{0,4},{1,5},{2,6},{3,7},{4,0},{5,1},{6,2},{7,3},{8,12},{9,13},{10,... | collective-permute-start | bytes 393224 | tf_op jit(solution)/shard_map/ppermute | solution.py:293
  41.7 11.1 %collective-permute-start.3 = (bf16[2,2,32,512]{3,2,1,0:T(8,128)(2,1)S(1)}, bf16[2,2,32,512]{3,2,1,0:T(8,128)(2,1)S(1)}, u32[]{:S(2)}, u32[]{:S(2)}) collective-permute-start(bf16[2,2,32,512]{3,2,1,0:T(8,128)(2,1)S(1)} %add_convert_fusion.1.refs_4_.refs_0_), channel_id=1, source_target_pairs={{0,2},{1,3},{2,0},{3,1},{4,6},{5,7},{6,4},{7,5},{8,10},{9,11},{10,... | collective-permute-start | bytes 393224 | tf_op jit(solution)/shard_map/ppermute | solution.py:293
  52.8 4.0 %collective-permute-start.13 = (bf16[4,2,2,32,512]{4,3,2,1,0:T(8,128)(2,1)S(1)}, bf16[4,2,2,32,512]{4,3,2,1,0:T(8,128)(2,1)S(1)}, u32[]{:S(2)}, u32[]{:S(2)}) collective-permute-start(bf16[4,2,2,32,512]{4,3,2,1,0:T(8,128)(2,1)S(1)} %stack.17.own_ref), channel_id=1, source_target_pairs={{0,1},{1,0},{2,3},{3,2},{4,5},{5,4},{6,7},{7,6},{8,9},{9,8},{10,11... | collective-permute-start | bytes 1572872 | tf_op jit(solution)/shard_map/ppermute | solution.py:293
  53.0 15.7 %collective-permute-start.19 = (bf16[2,2,32,512]{3,2,1,0:T(8,128)(2,1)S(1)}, bf16[2,2,32,512]{3,2,1,0:T(8,128)(2,1)S(1)}, u32[]{:S(2)}, u32[]{:S(2)}) collective-permute-start(bf16[2,2,32,512]{3,2,1,0:T(8,128)(2,1)S(1)} %respond.2.refs_4_.refs_0_), channel_id=1, source_target_pairs={{0,24},{8,16},{16,8},{24,0},{1,25},{9,17},{17,9},{25,1},{2,26},{10... | collective-permute-start | bytes 393224 | tf_op jit(solution)/shard_map/ppermute | solution.py:293
  55.5 13.7 %collective-permute-start.18 = (bf16[2,2,32,512]{3,2,1,0:T(8,128)(2,1)S(1)}, bf16[2,2,32,512]{3,2,1,0:T(8,128)(2,1)S(1)}, u32[]{:S(2)}, u32[]{:S(2)}) collective-permute-start(bf16[2,2,32,512]{3,2,1,0:T(8,128)(2,1)S(1)} %respond.2.refs_4_.refs_0_), channel_id=1, source_target_pairs={{0,16},{8,24},{16,0},{24,8},{1,17},{9,25},{17,1},{25,9},{2,18},{10... | collective-permute-start | bytes 393224 | tf_op jit(solution)/shard_map/ppermute | solution.py:293
  56.0 13.2 %collective-permute-start.17 = (bf16[2,2,32,512]{3,2,1,0:T(8,128)(2,1)S(1)}, bf16[2,2,32,512]{3,2,1,0:T(8,128)(2,1)S(1)}, u32[]{:S(2)}, u32[]{:S(2)}) collective-permute-start(bf16[2,2,32,512]{3,2,1,0:T(8,128)(2,1)S(1)} %respond.2.refs_4_.refs_0_), channel_id=1, source_target_pairs={{0,8},{8,0},{16,24},{24,16},{1,9},{9,1},{17,25},{25,17},{2,10},{10... | collective-permute-start | bytes 393224 | tf_op jit(solution)/shard_map/ppermute | solution.py:293
  65.6 11.4 %collective-permute-start.16 = (bf16[2,2,32,512]{3,2,1,0:T(8,128)(2,1)S(1)}, bf16[2,2,32,512]{3,2,1,0:T(8,128)(2,1)S(1)}, u32[]{:S(2)}, u32[]{:S(2)}) collective-permute-start(bf16[2,2,32,512]{3,2,1,0:T(8,128)(2,1)S(1)} %respond.3.refs_0_), channel_id=1, source_target_pairs={{0,24},{8,16},{16,8},{24,0},{1,25},{9,17},{17,9},{25,1},{2,26},{10... | collective-permute-start | bytes 393224 | tf_op jit(solution)/shard_map/ppermute | solution.py:293
  68.1 8.9 %collective-permute-start.15 = (bf16[2,2,32,512]{3,2,1,0:T(8,128)(2,1)S(1)}, bf16[2,2,32,512]{3,2,1,0:T(8,128)(2,1)S(1)}, u32[]{:S(2)}, u32[]{:S(2)}) collective-permute-start(bf16[2,2,32,512]{3,2,1,0:T(8,128)(2,1)S(1)} %respond.3.refs_0_), channel_id=1, source_target_pairs={{0,16},{8,24},{16,0},{24,8},{1,17},{9,25},{17,1},{25,9},{2,18},{10... | collective-permute-start | bytes 393224 | tf_op jit(solution)/shard_map/ppermute | solution.py:293
  68.7 8.4 %collective-permute-start.14 = (bf16[2,2,32,512]{3,2,1,0:T(8,128)(2,1)S(1)}, bf16[2,2,32,512]{3,2,1,0:T(8,128)(2,1)S(1)}, u32[]{:S(2)}, u32[]{:S(2)}) collective-permute-start(bf16[2,2,32,512]{3,2,1,0:T(8,128)(2,1)S(1)} %respond.3.refs_0_), channel_id=1, source_target_pairs={{0,8},{8,0},{16,24},{24,16},{1,9},{9,1},{17,25},{25,17},{2,10},{10... | collective-permute-start | bytes 393224 | tf_op jit(solution)/shard_map/ppermute | solution.py:293

commit v3 on v2

v3 whole, which is shorter than its diff:
```python
import functools
import math

import jax
import jax.numpy as jnp
from jax import lax
from jax.experimental import pallas as pl
from jax.experimental.pallas import tpu as pltpu
from jax.sharding import PartitionSpec as P

ROWS = 16
CHUNKS = 2
F_TIMES = 256
F_SLOTS = 3
I_TIMES = 128
I_SLOTS = 3
MIB = 1024 * 1024
F_VMEM = 40 * MIB
R_VMEM = 12 * MIB
I_VMEM = 20 * MIB
S_VMEM = 16 * MIB
L_VMEM = 32 * MIB


def phases(bands, times, samples):
    return (bands * times % samples).astype(jnp.float32) * (2.0 * math.pi / samples)


def tables(per_device, freq_devices, local_times):
    me = lax.axis_index("freq")
    samples = local_times * freq_devices
    owners = me ^ jnp.arange(freq_devices, dtype=jnp.int32)
    bands = samples // 16 + (owners[:, None] * per_device + jnp.arange(per_device, dtype=jnp.int32)).reshape(-1)
    times = me * local_times + jnp.arange(local_times, dtype=jnp.int32)
    angles = phases(bands[:, None], times[None, :], samples)
    parts = jnp.stack([jnp.cos(angles), -jnp.sin(angles)], axis=1).reshape(-1, local_times)
    factors = (1.0 / math.sqrt(samples), 1.0 / math.sqrt(per_device * freq_devices))
    return jnp.stack([parts * factor for factor in factors]).astype(jnp.bfloat16)


def repeats(count):
    lane = lax.broadcasted_iota(jnp.int32, (count, count * ROWS), 1)
    row = lax.broadcasted_iota(jnp.int32, (count, count * ROWS), 0)
    return jnp.where(lane // ROWS == row, 1.0, 0.0).astype(jnp.bfloat16)


def spread_rows(store, wide):
    lane = lax.broadcasted_iota(jnp.int32, (ROWS, wide.shape[1]), 1)
    row = lax.broadcasted_iota(jnp.int32, (ROWS, wide.shape[1]), 0)
    own = lane % ROWS == row
    for i in range(wide.shape[0]):
        store(i, jnp.where(own, wide[i : i + 1], 0.0).astype(jnp.bfloat16))


def forward_kernel(first, focal, table_ref, traces_ref, *refs):
    *outs, spread, total, slots, sems = refs
    depth, times, rows, width = slots.shape
    steps = spread.shape[0]
    count = steps * (focal // rows)

    def fetch(i):
        slot = lax.rem(i, depth)
        source = traces_ref.at[
            pl.ds(lax.rem(i, steps) * times, times), pl.ds(first + i // steps * rows, rows), :
        ]
        return pltpu.make_async_copy(source, slots.at[slot], sems.at[slot])

    for i in range(min(depth - 1, count)):
        fetch(jnp.int32(i)).start()

    for step in range(steps):

        def store(i, block, step=step):
            spread[step, pl.ds(i * rows, rows), :] = block

        some = table_ref[0, :, pl.ds(step * times, times)]
        spread_rows(store, jnp.dot(some, repeats(times), preferred_element_type=jnp.float32))

    @pl.loop(0, count)
    def _(i):
        step = lax.rem(i, steps)

        @pl.when(i + depth - 1 < count)
        def _():
            fetch(i + depth - 1).start()

        fetch(i).wait()
        block = slots[lax.rem(i, depth)].reshape(times * rows, width)
        part = jnp.dot(spread[step], block, preferred_element_type=jnp.float32)

        @pl.when(step == 0)
        def _():
            total[...] = part

        @pl.when(step > 0)
        def _():
            total[...] += part

        @pl.when(step == steps - 1)
        def _():
            share = total.shape[0] // len(outs)
            place = pl.ds(pl.multiple_of(i // steps * rows, rows), rows)
            for j, out in enumerate(outs):
                value = total[pl.ds(j * share, share), :].reshape(*out.shape[:2], rows, width)
                out[:, :, place, :] = value.astype(out.dtype)


def forward(table, traces, first, focal, per_device, freq_devices):
    local_times, _, width = traces.shape
    times = min(F_TIMES, local_times)
    steps = local_times // times
    count = 2 * per_device * freq_devices
    shape = (per_device, 2, focal, width)
    whole = pl.BlockSpec(memory_space=pltpu.VMEM)
    return pl.pallas_call(
        functools.partial(forward_kernel, first, focal),
        in_specs=[whole, pl.BlockSpec(memory_space=pl.ANY)],
        out_specs=[whole] * freq_devices,
        out_shape=[jax.ShapeDtypeStruct(shape, jnp.float32 if i == 0 else jnp.bfloat16) for i in range(freq_devices)],
        scratch_shapes=[
            pltpu.VMEM((steps, count * ROWS, times * ROWS), jnp.bfloat16),
            pltpu.VMEM((count * ROWS, width), jnp.float32),
            pltpu.VMEM((F_SLOTS, times, ROWS, width), jnp.bfloat16),
            pltpu.SemaphoreType.DMA((F_SLOTS,)),
        ],
        compiler_params=pltpu.CompilerParams(vmem_limit_bytes=F_VMEM),
        cost_estimate=pl.CostEstimate(
            flops=2 * count * ROWS * local_times * focal * width,
            bytes_accessed=2 * local_times * focal * width,
            transcendentals=0,
        ),
        name="forward",
    )(table, traces)


def load_kernel(reflection_ref, *refs):
    out, sems = refs[-2:]

    def fetch(i):
        return pltpu.make_async_copy(reflection_ref.at[i], out.at[i], sems.at[i])

    for i in range(out.shape[0]):
        fetch(i).start()
    for i in range(out.shape[0]):
        fetch(i).wait()


def load(reflection, earlier):
    return pl.pallas_call(
        load_kernel,
        in_specs=[pl.BlockSpec(memory_space=pl.ANY)] * (1 + len(earlier)),
        out_specs=pl.BlockSpec(memory_space=pltpu.VMEM),
        out_shape=jax.ShapeDtypeStruct(reflection.shape, reflection.dtype),
        scratch_shapes=[pltpu.SemaphoreType.DMA((reflection.shape[0],))],
        compiler_params=pltpu.CompilerParams(vmem_limit_bytes=L_VMEM),
        name="load",
    )(reflection, *earlier)


def response_kernel(masks, reflection_ref, *refs):
    out, spectra = refs[-2:]
    bands, _, rows, sources = reflection_ref.shape
    _, _, _, focal, width = refs[0].shape
    me = lax.axis_index("mat")
    for pieces, origins in zip(refs, masks):
        for i, mask in enumerate(origins):
            start = pl.multiple_of((me ^ mask) * width, width)
            spectra[:, :, pl.ds(start, width)] = pieces[i].reshape(bands, 2 * focal, width)
    for band in range(bands):
        product = lax.dot_general(
            reflection_ref[band].reshape(2 * rows, sources),
            spectra[band],
            (((1,), (1,)), ((), ())),
            preferred_element_type=jnp.float32,
        ).T
        out[band, 0] = (product[:focal, :rows] - product[focal:, rows:]).astype(out.dtype)
        out[band, 1] = (product[focal:, :rows] + product[:focal, rows:]).astype(out.dtype)


def respond(reflection, pieces, masks, earlier):
    per_device, _, rows, sources = reflection.shape
    focal, width = pieces[0].shape[3:]
    whole = pl.BlockSpec(memory_space=pltpu.VMEM)
    return pl.pallas_call(
        functools.partial(response_kernel, masks),
        in_specs=[whole] * (1 + len(pieces)) + [pl.BlockSpec(memory_space=pl.ANY)] * len(earlier),
        out_specs=whole,
        out_shape=jax.ShapeDtypeStruct((per_device, 2, focal, rows), jnp.bfloat16),
        scratch_shapes=[pltpu.VMEM((per_device, 2 * focal, sources), jnp.bfloat16)],
        compiler_params=pltpu.CompilerParams(vmem_limit_bytes=R_VMEM),
        cost_estimate=pl.CostEstimate(flops=0, bytes_accessed=1024, transcendentals=0),
        name="respond",
    )(reflection, *pieces, *earlier)


def spread_kernel(table_ref, out):
    def store(i, block):
        out[pl.ds(i * ROWS, ROWS), :] = block

    table = table_ref[1]
    wide = lax.dot_general(
        table, repeats(table.shape[0]), (((0,), (0,)), ((), ())), preferred_element_type=jnp.float32
    )
    spread_rows(store, wide)


def spread(table):
    _, count, times = table.shape
    whole = pl.BlockSpec(memory_space=pltpu.VMEM)
    return pl.pallas_call(
        spread_kernel,
        in_specs=[whole],
        out_specs=whole,
        out_shape=jax.ShapeDtypeStruct((times * ROWS, count * ROWS), jnp.bfloat16),
        compiler_params=pltpu.CompilerParams(vmem_limit_bytes=S_VMEM),
        cost_estimate=pl.CostEstimate(flops=0, bytes_accessed=2 * times * ROWS * count * ROWS, transcendentals=0),
        name="spread",
    )(table)


def inverse_kernel(first, has_before, spread, onset_ref, *refs):
    pieces, (out, weights, slots, sems) = refs[: -4 - has_before], refs[-4:]
    depth, times, rows, width = slots.shape
    focal = pieces[0].shape[2]
    local_times = out.shape[0]
    steps = local_times // times
    count = steps * (focal // rows)
    share = weights.shape[0] // len(pieces)
    begin = lax.axis_index("freq") * local_times

    def send(i):
        slot = lax.rem(i, depth)
        target = out.at[pl.ds(lax.rem(i, steps) * times, times), pl.ds(first + i // steps * rows, rows), :]
        return pltpu.make_async_copy(slots.at[slot], target, sems.at[slot])

    @pl.loop(0, count)
    def _(i):
        step = lax.rem(i, steps)
        slot = lax.rem(i, depth)
        place = pl.ds(pl.multiple_of(i // steps * rows, rows), rows)

        @pl.when(i >= depth)
        def _():
            send(i - depth).wait()

        @pl.when(step == 0)
        def _():
            for j, piece in enumerate(pieces):
                weights[pl.ds(j * share, share), :] = piece[:, :, place, :].reshape(share, width)

        lines = pl.ds(pl.multiple_of(step * times * rows, times * rows), times * rows)
        signal = jnp.dot(spread[lines, :], weights[...], preferred_element_type=jnp.float32)
        signal = signal.reshape(times, rows, width)
        moment = begin + step * times + lax.broadcasted_iota(jnp.int32, (times, 1, 1), 0)
        onset = onset_ref[pl.ds(pl.multiple_of(first + i // steps * rows, rows), rows), :]
        slots[slot] = jnp.where(moment < onset[None], signal, 0.0).astype(out.dtype)
        send(i).start()

    for i in range(max(0, count - depth), count):
        send(jnp.int32(i)).wait()


def invert(table, onset, pieces, before, first, shape):
    local_times, _, width = shape
    focal = pieces[0].shape[2]
    times = min(I_TIMES, local_times)
    has_before = before is not None
    operands = [table, onset, *pieces] + ([before] if has_before else [])
    whole = pl.BlockSpec(memory_space=pltpu.VMEM)
    anywhere = pl.BlockSpec(memory_space=pl.ANY)
    return pl.pallas_call(
        functools.partial(inverse_kernel, first, has_before),
        in_specs=[whole] * (2 + len(pieces)) + [anywhere] * has_before,
        out_specs=anywhere,
        out_shape=jax.ShapeDtypeStruct(shape, jnp.bfloat16),
        scratch_shapes=[
            pltpu.VMEM((table.shape[1], width), jnp.bfloat16),
            pltpu.VMEM((I_SLOTS, times, ROWS, width), jnp.bfloat16),
            pltpu.SemaphoreType.DMA((I_SLOTS,)),
        ],
        input_output_aliases={len(operands) - 1: 0} if has_before else {},
        compiler_params=pltpu.CompilerParams(vmem_limit_bytes=I_VMEM),
        cost_estimate=pl.CostEstimate(
            flops=2 * table.shape[1] * local_times * focal * width,
            bytes_accessed=2 * local_times * focal * width,
            transcendentals=0,
        ),
        name="invert",
    )(*operands)


def sum_kernel(count, *refs):
    out = refs[-1]
    total = refs[0][...]
    for part in refs[1:count]:
        total = total + part[...].astype(jnp.float32)
    out[0] = total.astype(out.dtype)


def add(parts, earlier):
    whole = pl.BlockSpec(memory_space=pltpu.VMEM)
    return pl.pallas_call(
        functools.partial(sum_kernel, len(parts)),
        in_specs=[whole] * len(parts) + [pl.BlockSpec(memory_space=pl.ANY)] * len(earlier),
        out_specs=whole,
        out_shape=jax.ShapeDtypeStruct((1, *parts[0].shape), jnp.bfloat16),
        compiler_params=pltpu.CompilerParams(vmem_limit_bytes=S_VMEM),
        name="add",
    )(*parts, *earlier)


def stack_kernel(count, *refs):
    out, place = refs[-1], 0
    for piece in refs[:count]:
        out[pl.ds(place, piece.shape[0])] = piece[...]
        place += piece.shape[0]


def stack(pieces, earlier):
    whole = pl.BlockSpec(memory_space=pltpu.VMEM)
    total = sum(piece.shape[0] for piece in pieces)
    return pl.pallas_call(
        functools.partial(stack_kernel, len(pieces)),
        in_specs=[whole] * len(pieces) + [pl.BlockSpec(memory_space=pl.ANY)] * len(earlier),
        out_specs=whole,
        out_shape=jax.ShapeDtypeStruct((total, *pieces[0].shape[1:]), pieces[0].dtype),
        compiler_params=pltpu.CompilerParams(vmem_limit_bytes=S_VMEM),
        name="stack",
    )(*pieces, *earlier)


def swap(array, axis, mask):
    return lax.ppermute(array, axis, [(i, i ^ mask) for i in range(lax.axis_size(axis))])


def on_device(traces, reflection, onset):
    local_times, focal_count, _ = traces.shape
    freq_devices, mat_devices = lax.axis_size("freq"), lax.axis_size("mat")
    per_device = reflection.shape[0]
    table = tables(per_device, freq_devices, local_times)
    focal = focal_count // CHUNKS

    steps = [1 << bit for bit in reversed(range(1, mat_devices.bit_length() - 1))]

    parts = [forward(table, traces, i * focal, focal, per_device, freq_devices) for i in range(CHUNKS)]
    spectra = []
    for i, part in enumerate(parts):
        arrived = [swap(part[mask], "freq", mask) for mask in range(1, freq_devices)]
        spectra.append(add([part[0], *arrived], [later[0] for later in parts[i + 1 :]]))
    held, masks, tied = [], [0], []
    for block in spectra:
        for step in steps[:-1]:
            block = stack([block, swap(block, "mat", step)], tied or [spectra[-1]])
        if not tied:
            tied = [spread(table), load(reflection, [block])]
        held.append((block, swap(block, "mat", steps[-1])))
    for step in steps[:-1]:
        masks = masks + [mask ^ step for mask in masks]
    masks = [masks, [mask ^ steps[-1] for mask in masks]]
    masks += [[mask ^ 1 for mask in some] for some in masks]

    inverse_spread, loaded = tied
    responses = []
    for i, (block, other) in enumerate(held):
        if responses:
            other = stack([other], [responses[-1][0]])
        pieces = [block, other, swap(block, "mat", 1), swap(other, "mat", 1)]
        response = respond(loaded, pieces, masks, [later for later, _ in held[i + 1 :]])
        responses.append([response] + [swap(response, "freq", mask) for mask in range(1, freq_devices)])
    windowed = None
    for i, pieces in enumerate(responses):
        windowed = invert(inverse_spread, onset, pieces, windowed, i * focal, traces.shape)
    return windowed


def solution(mesh):
    placed = (P("freq", None, "mat"), P("freq", None, "mat", None), P(None, "mat"))
    return jax.shard_map(
        on_device, mesh=mesh, in_specs=placed, out_specs=P("freq", None, "mat"), check_vma=False
    )
```

time: 85.3 us -> 78 us (0.914)
  Pallas kernels: 50.2 us -> 45.8 us
  starting transfers between devices: 24.6 us -> 23.4 us
  waiting for transfers between devices: 9.19 us -> 8.09 us
    pallas_call x4 -> x9, Pallas kernels: 17.6 us -> 16 us  [the longest x2 9.25 us: respond(): pl.pallas_call(functools.partial(response_kernel, masks), in_specs=[whole...]
    pallas_call x2, Pallas kernels: 15.7 us -> 14.3 us  [invert(): pl.pallas_call(functools.partial(inverse_kernel, first, has_before), in_s...]
    pallas_call x2, Pallas kernels: 16.9 us -> 15.5 us  [forward(): pl.pallas_call(functools.partial(forward_kernel, first, focal), in_specs=...]
    ppermute x20, starting transfers between devices: 24.6 us -> 23.4 us  [swap(): lax.ppermute(array, axis, [(i, i ^ mask) for i in range(lax.axis_size(axi...]
    ppermute x20, waiting for transfers between devices: 9.19 us -> 8.09 us  [swap(): lax.ppermute(array, axis, [(i, i ^ mask) for i in range(lax.axis_size(axi...]
  transfers between devices with their start and end apart: 20 -> 20, of which waited for: 4 -> 4; matrix products, arithmetic and copies ran while one was open for 1% -> 0% of each run, Pallas kernels for 40% -> 39%
where the time goes in v3:
time: 78 us; the launch traced here: 77.8 us
  Pallas kernels  45.8 us (59%)
  starting transfers between devices  23.4 us (30%)
  waiting for transfers between devices  8.09 us (10%)
    ppermute x20, starting transfers between devices, swap(): lax.ppermute(array, axis, [(i, i ^ mask) for i in range(lax.axis_size(axi...  23.4 us
    pallas_call x2, Pallas kernels, forward(): pl.pallas_call(functools.partial(forward_kernel, first, focal), in_specs=...  15.5 us
    pallas_call x2, Pallas kernels, invert(): pl.pallas_call(functools.partial(inverse_kernel, first, has_before), in_s...  14.3 us
    pallas_call x2, Pallas kernels, respond(): pl.pallas_call(functools.partial(response_kernel, masks), in_specs=[whole...  9.25 us
    ppermute x20, waiting for transfers between devices, swap(): lax.ppermute(array, axis, [(i, i ^ mask) for i in range(lax.axis_size(axi...  8.09 us
    pallas_call x1, Pallas kernels, load(): pl.pallas_call(load_kernel, in_specs=[pl.BlockSpec(memory_space=pl.ANY)]...  5.79 us
  transfers between devices with their start and end apart: 20, of which 4 were waited for; matrix products, arithmetic and copies ran while one was open for 0% of the time, Pallas kernels for 39%

profile of v3, /device:TPU:0, one launch (start us, length us, event | category | flops | bytes accessed | tf_op | source)
XLA Modules:
  0.0 77.8 jit_solution(12839218887609474040)
XLA Ops:
  0.5 7.9 %forward.2 = (f32[2,2,32,512]{3,2,1,0:T(8,128)S(1)}, bf16[2,2,32,512]{3,2,1,0:T(8,128)(2,1)S(1)}, bf16[2,2,32,512]{3,2,1,0:T(8,128)(2,1)S(1)}, bf16[2,2,32,512]{3,2,1,0:T(8,128)(2,1)S(1)}) custom-call(bf16[2,16,512]{2,1,0:T(8,128)(2,1)S(1)} %constant_dynamic-update-slice_fusion.table_ref, bf16[512,64,512]{2,1,0:T(8,128)(2,1)} %traces_ref.3), custom_call_target="tpu_custom_call" | custom-call | flops 4294967296 | bytes 16777216 | tf_op jit(solution)/shard_map/forward/pallas_call | solution.py:115
  8.4 3.0 %collective-permute-start = (bf16[2,2,32,512]{3,2,1,0:T(8,128)(2,1)S(1)}, bf16[2,2,32,512]{3,2,1,0:T(8,128)(2,1)S(1)}, u32[]{:S(2)}, u32[]{:S(2)}) collective-permute-start(bf16[2,2,32,512]{3,2,1,0:T(8,128)(2,1)S(1)} %get-tuple-element.14), channel_id=1, source_target_pairs={{0,8},{8,0},{16,24},{24,16},{1,9},{9,1},{17,25},{25,17},{2,10},{10... | collective-permute-start | bytes 393224 | tf_op jit(solution)/shard_map/ppermute | solution.py:333
  11.4 1.5 %collective-permute-start.1 = (bf16[2,2,32,512]{3,2,1,0:T(8,128)(2,1)S(1)}, bf16[2,2,32,512]{3,2,1,0:T(8,128)(2,1)S(1)}, u32[]{:S(2)}, u32[]{:S(2)}) collective-permute-start(bf16[2,2,32,512]{3,2,1,0:T(8,128)(2,1)S(1)} %get-tuple-element.15), channel_id=1, source_target_pairs={{0,16},{8,24},{16,0},{24,8},{1,17},{9,25},{17,1},{25,9},{2,18},{10... | collective-permute-start | bytes 393224 | tf_op jit(solution)/shard_map/ppermute | solution.py:333
  13.0 7.5 %forward.3 = (f32[2,2,32,512]{3,2,1,0:T(8,128)S(1)}, bf16[2,2,32,512]{3,2,1,0:T(8,128)(2,1)S(1)}, bf16[2,2,32,512]{3,2,1,0:T(8,128)(2,1)S(1)}, bf16[2,2,32,512]{3,2,1,0:T(8,128)(2,1)S(1)}) custom-call(bf16[2,16,512]{2,1,0:T(8,128)(2,1)S(1)} %constant_dynamic-update-slice_fusion.table_ref, bf16[512,64,512]{2,1,0:T(8,128)(2,1)} %traces_ref.3), custom_call_target="tpu_custom_call" | custom-call | flops 4294967296 | bytes 16777216 | tf_op jit(solution)/shard_map/forward/pallas_call | solution.py:115
  20.5 2.0 %collective-permute-start.4 = (bf16[2,2,32,512]{3,2,1,0:T(8,128)(2,1)S(1)}, bf16[2,2,32,512]{3,2,1,0:T(8,128)(2,1)S(1)}, u32[]{:S(2)}, u32[]{:S(2)}) collective-permute-start(bf16[2,2,32,512]{3,2,1,0:T(8,128)(2,1)S(1)} %get-tuple-element.18), channel_id=1, source_target_pairs={{0,8},{8,0},{16,24},{24,16},{1,9},{9,1},{17,25},{25,17},{2,10},{10... | collective-permute-start | bytes 393224 | tf_op jit(solution)/shard_map/ppermute | solution.py:333
  22.5 1.5 %collective-permute-start.5 = (bf16[2,2,32,512]{3,2,1,0:T(8,128)(2,1)S(1)}, bf16[2,2,32,512]{3,2,1,0:T(8,128)(2,1)S(1)}, u32[]{:S(2)}, u32[]{:S(2)}) collective-permute-start(bf16[2,2,32,512]{3,2,1,0:T(8,128)(2,1)S(1)} %get-tuple-element.19), channel_id=1, source_target_pairs={{0,16},{8,24},{16,0},{24,8},{1,17},{9,25},{17,1},{25,9},{2,18},{10... | collective-permute-start | bytes 393224 | tf_op jit(solution)/shard_map/ppermute | solution.py:333
  24.1 3.1 %collective-permute-start.3 = (bf16[1,2,2,32,512]{4,3,2,1,0:T(8,128)(2,1)S(1)}, bf16[1,2,2,32,512]{4,3,2,1,0:T(8,128)(2,1)S(1)}, u32[]{:S(2)}, u32[]{:S(2)}) collective-permute-start(bf16[1,2,2,32,512]{4,3,2,1,0:T(8,128)(2,1)S(1)} %add.81.refs_0_), channel_id=1, source_target_pairs={{0,4},{1,5},{2,6},{3,7},{4,0},{5,1},{6,2},{7,3},{8,12},{9,13},{10,... | collective-permute-start | bytes 393224 | tf_op jit(solution)/shard_map/ppermute | solution.py:333
  27.2 3.0 %collective-permute-done.5.refs_2_ = bf16[2,2,32,512]{3,2,1,0:T(8,128)(2,1)S(1)} collective-permute-done((bf16[2,2,32,512]{3,2,1,0:T(8,128)(2,1)S(1)}, bf16[2,2,32,512]{3,2,1,0:T(8,128)(2,1)S(1)}, u32[]{:S(2)}, u32[]{:S(2)}) %collective-permute-start.5) | collective-permute-done | bytes 131104 | tf_op jit(solution)/shard_map/ppermute | solution.py:333
  30.3 1.6 %collective-permute-done.3.refs_1_ = bf16[1,2,2,32,512]{4,3,2,1,0:T(8,128)(2,1)S(1)} collective-permute-done((bf16[1,2,2,32,512]{4,3,2,1,0:T(8,128)(2,1)S(1)}, bf16[1,2,2,32,512]{4,3,2,1,0:T(8,128)(2,1)S(1)}, u32[]{:S(2)}, u32[]{:S(2)}) %collective-permute-start.3) | collective-permute-done | bytes 131104 | tf_op jit(solution)/shard_map/ppermute | solution.py:333
  31.9 0.8 %collective-permute-start.9 = (bf16[2,2,2,32,512]{4,3,2,1,0:T(8,128)(2,1)S(1)}, bf16[2,2,2,32,512]{4,3,2,1,0:T(8,128)(2,1)S(1)}, u32[]{:S(2)}, u32[]{:S(2)}) collective-permute-start(bf16[2,2,2,32,512]{4,3,2,1,0:T(8,128)(2,1)S(1)} %stack.16.refs_0_), channel_id=1, source_target_pairs={{0,2},{1,3},{2,0},{3,1},{4,6},{5,7},{6,4},{7,5},{8,10},{9,11},{10,... | collective-permute-start | bytes 786440 | tf_op jit(solution)/shard_map/ppermute | solution.py:333
  32.7 3.4 %collective-permute-start.7 = (bf16[1,2,2,32,512]{4,3,2,1,0:T(8,128)(2,1)S(1)}, bf16[1,2,2,32,512]{4,3,2,1,0:T(8,128)(2,1)S(1)}, u32[]{:S(2)}, u32[]{:S(2)}) collective-permute-start(bf16[1,2,2,32,512]{4,3,2,1,0:T(8,128)(2,1)S(1)} %add.82.refs_2_.refs_0_), channel_id=1, source_target_pairs={{0,4},{1,5},{2,6},{3,7},{4,0},{5,1},{6,2},{7,3},{8,12},{9,13},{10,... | collective-permute-start | bytes 393224 | tf_op jit(solution)/shard_map/ppermute | solution.py:333
  36.1 0.8 spread.1.refs_2_
  36.9 5.8 %load.1.refs_3_.reflection_ref = bf16[2,2,512,4096]{3,2,1,0:T(8,128)(2,1)S(1)} custom-call(bf16[2,2,512,4096]{3,2,1,0:T(8,128)(2,1)} %reflection_ref.1, bf16[2,2,2,32,512]{4,3,2,1,0:T(8,128)(2,1)S(1)} %stack.16.refs_0_), custom_call_target="tpu_custom_call" | custom-call | tf_op jit(solution)/shard_map/load/pallas_call | solution.py:149
  42.7 0.6 collective-permute-start.11
  43.5 1.0 %collective-permute-done.11.refs_3_ = bf16[2,2,2,32,512]{4,3,2,1,0:T(8,128)(2,1)S(1)} collective-permute-done((bf16[2,2,2,32,512]{4,3,2,1,0:T(8,128)(2,1)S(1)}, bf16[2,2,2,32,512]{4,3,2,1,0:T(8,128)(2,1)S(1)}, u32[]{:S(2)}, u32[]{:S(2)}) %collective-permute-start.11) | collective-permute-done | bytes 262176 | tf_op jit(solution)/shard_map/ppermute | solution.py:333
  44.5 4.6 %respond.2.refs_1_.refs_0_ = bf16[2,2,32,512]{3,2,1,0:T(8,128)(2,1)S(1)} custom-call(bf16[2,2,512,4096]{3,2,1,0:T(8,128)(2,1)S(1)} %load.1.refs_3_.reflection_ref, bf16[2,2,2,32,512]{4,3,2,1,0:T(8,128)(2,1)S(1)} %stack.16.refs_0_, bf16[2,2,2,32,512]{4,3,2,1,0:T(8,128)(2,1)S(1)} %collective-permute-done.9.refs_1_, ...), custom_call_target="tpu_custom_call" | custom-call | bytes 1024 | tf_op jit(solution)/shard_map/respond/pallas_call | solution.py:184
  49.1 2.5 %collective-permute-done.8.refs_0_ = bf16[2,2,2,32,512]{4,3,2,1,0:T(8,128)(2,1)S(1)} collective-permute-done((bf16[2,2,2,32,512]{4,3,2,1,0:T(8,128)(2,1)S(1)}, bf16[2,2,2,32,512]{4,3,2,1,0:T(8,128)(2,1)S(1)}, u32[]{:S(2)}, u32[]{:S(2)}) %collective-permute-start.8) | collective-permute-done | bytes 262176 | tf_op jit(solution)/shard_map/ppermute | solution.py:333
  51.7 2.5 %collective-permute-start.19 = (bf16[2,2,32,512]{3,2,1,0:T(8,128)(2,1)S(1)}, bf16[2,2,32,512]{3,2,1,0:T(8,128)(2,1)S(1)}, u32[]{:S(2)}, u32[]{:S(2)}) collective-permute-start(bf16[2,2,32,512]{3,2,1,0:T(8,128)(2,1)S(1)} %respond.2.refs_1_.refs_0_), channel_id=1, source_target_pairs={{0,24},{8,16},{16,8},{24,0},{1,25},{9,17},{17,9},{25,1},{2,26},{10... | collective-permute-start | bytes 393224 | tf_op jit(solution)/shard_map/ppermute | solution.py:333
  54.7 0.5 collective-permute-start.17
  55.3 4.6 %respond.3.refs_0_ = bf16[2,2,32,512]{3,2,1,0:T(8,128)(2,1)S(1)} custom-call(bf16[2,2,512,4096]{3,2,1,0:T(8,128)(2,1)S(1)} %load.1.refs_3_.reflection_ref, bf16[2,2,2,32,512]{4,3,2,1,0:T(8,128)(2,1)S(1)} %stack.17.refs_4_.refs_0_, bf16[2,2,2,32,512]{4,3,2,1,0:T(8,128)(2,1)S(1)} %stack.18.refs_1_, ...), custom_call_target="tpu_custom_call" | custom-call | bytes 1024 | tf_op jit(solution)/shard_map/respond/pallas_call | solution.py:184
  59.9 2.5 %collective-permute-start.16 = (bf16[2,2,32,512]{3,2,1,0:T(8,128)(2,1)S(1)}, bf16[2,2,32,512]{3,2,1,0:T(8,128)(2,1)S(1)}, u32[]{:S(2)}, u32[]{:S(2)}) collective-permute-start(bf16[2,2,32,512]{3,2,1,0:T(8,128)(2,1)S(1)} %respond.3.refs_0_), channel_id=1, source_target_pairs={{0,24},{8,16},{16,8},{24,0},{1,25},{9,17},{17,9},{25,1},{2,26},{10... | collective-permute-start | bytes 393224 | tf_op jit(solution)/shard_map/ppermute | solution.py:333
  62.9 0.5 collective-permute-start.14
  63.5 7.2 %invert.2.refs_4_ = bf16[512,64,512]{2,1,0:T(8,128)(2,1)} custom-call(bf16[8192,256]{1,0:T(8,128)(2,1)S(1)} %spread.1.refs_2_, s32[64,512]{1,0:T(8,128)S(1)} %copy-done, bf16[2,2,32,512]{3,2,1,0:T(8,128)(2,1)S(1)} %respond.2.refs_1_.refs_0_, bf16[2,2,32,512]{3,2,1,0:T(8,128)(2,1)S(1)} %collective-permute-done.17.refs_1_, ...), custom_call_target="tpu_custom_call" | custom-call | flops 4294967296 | bytes 16777216 | tf_op jit(solution)/shard_map/invert/pallas_call | solution.py:271
  70.7 7.2 %invert.3 = bf16[512,64,512]{2,1,0:T(8,128)(2,1)} custom-call(bf16[8192,256]{1,0:T(8,128)(2,1)S(1)} %spread.1.refs_2_, s32[64,512]{1,0:T(8,128)S(1)} %copy-done, bf16[2,2,32,512]{3,2,1,0:T(8,128)(2,1)S(1)} %respond.3.refs_0_, bf16[2,2,32,512]{3,2,1,0:T(8,128)(2,1)S(1)} %collective-permute-done.14.refs_1_, ...), custom_call_target="tpu_custom_call", output_to_operand_aliasing={{}: (6, {})} | custom-call | flops 4294967296 | bytes 16777216 | tf_op jit(solution)/shard_map/invert/pallas_call | solution.py:271
  (43 shorter events, 1.9 us)
Async XLA Ops:
  8.4 15.6 %collective-permute-start = (bf16[2,2,32,512]{3,2,1,0:T(8,128)(2,1)S(1)}, bf16[2,2,32,512]{3,2,1,0:T(8,128)(2,1)S(1)}, u32[]{:S(2)}, u32[]{:S(2)}) collective-permute-start(bf16[2,2,32,512]{3,2,1,0:T(8,128)(2,1)S(1)} %get-tuple-element.14), channel_id=1, source_target_pairs={{0,8},{8,0},{16,24},{24,16},{1,9},{9,1},{17,25},{25,17},{2,10},{10... | collective-permute-start | bytes 393224 | tf_op jit(solution)/shard_map/ppermute | solution.py:333
  11.4 12.7 %collective-permute-start.1 = (bf16[2,2,32,512]{3,2,1,0:T(8,128)(2,1)S(1)}, bf16[2,2,32,512]{3,2,1,0:T(8,128)(2,1)S(1)}, u32[]{:S(2)}, u32[]{:S(2)}) collective-permute-start(bf16[2,2,32,512]{3,2,1,0:T(8,128)(2,1)S(1)} %get-tuple-element.15), channel_id=1, source_target_pairs={{0,16},{8,24},{16,0},{24,8},{1,17},{9,25},{17,1},{25,9},{2,18},{10... | collective-permute-start | bytes 393224 | tf_op jit(solution)/shard_map/ppermute | solution.py:333
  12.9 11.1 %collective-permute-start.2 = (bf16[2,2,32,512]{3,2,1,0:T(8,128)(2,1)S(1)}, bf16[2,2,32,512]{3,2,1,0:T(8,128)(2,1)S(1)}, u32[]{:S(2)}, u32[]{:S(2)}) collective-permute-start(bf16[2,2,32,512]{3,2,1,0:T(8,128)(2,1)S(1)} %get-tuple-element.16), channel_id=1, source_target_pairs={{0,24},{8,16},{16,8},{24,0},{1,25},{9,17},{17,9},{25,1},{2,26},{10... | collective-permute-start | bytes 393224 | tf_op jit(solution)/shard_map/ppermute | solution.py:333
  20.5 6.7 %collective-permute-start.4 = (bf16[2,2,32,512]{3,2,1,0:T(8,128)(2,1)S(1)}, bf16[2,2,32,512]{3,2,1,0:T(8,128)(2,1)S(1)}, u32[]{:S(2)}, u32[]{:S(2)}) collective-permute-start(bf16[2,2,32,512]{3,2,1,0:T(8,128)(2,1)S(1)} %get-tuple-element.18), channel_id=1, source_target_pairs={{0,8},{8,0},{16,24},{24,16},{1,9},{9,1},{17,25},{25,17},{2,10},{10... | collective-permute-start | bytes 393224 | tf_op jit(solution)/shard_map/ppermute | solution.py:333
  22.5 7.7 %collective-permute-start.5 = (bf16[2,2,32,512]{3,2,1,0:T(8,128)(2,1)S(1)}, bf16[2,2,32,512]{3,2,1,0:T(8,128)(2,1)S(1)}, u32[]{:S(2)}, u32[]{:S(2)}) collective-permute-start(bf16[2,2,32,512]{3,2,1,0:T(8,128)(2,1)S(1)} %get-tuple-element.19), channel_id=1, source_target_pairs={{0,16},{8,24},{16,0},{24,8},{1,17},{9,25},{17,1},{25,9},{2,18},{10... | collective-permute-start | bytes 393224 | tf_op jit(solution)/shard_map/ppermute | solution.py:333
  24.0 6.2 %collective-permute-start.6 = (bf16[2,2,32,512]{3,2,1,0:T(8,128)(2,1)S(1)}, bf16[2,2,32,512]{3,2,1,0:T(8,128)(2,1)S(1)}, u32[]{:S(2)}, u32[]{:S(2)}) collective-permute-start(bf16[2,2,32,512]{3,2,1,0:T(8,128)(2,1)S(1)} %get-tuple-element.20), channel_id=1, source_target_pairs={{0,24},{8,16},{16,8},{24,0},{1,25},{9,17},{17,9},{25,1},{2,26},{10... | collective-permute-start | bytes 393224 | tf_op jit(solution)/shard_map/ppermute | solution.py:333
  24.1 7.7 %collective-permute-start.3 = (bf16[1,2,2,32,512]{4,3,2,1,0:T(8,128)(2,1)S(1)}, bf16[1,2,2,32,512]{4,3,2,1,0:T(8,128)(2,1)S(1)}, u32[]{:S(2)}, u32[]{:S(2)}) collective-permute-start(bf16[1,2,2,32,512]{4,3,2,1,0:T(8,128)(2,1)S(1)} %add.81.refs_0_), channel_id=1, source_target_pairs={{0,4},{1,5},{2,6},{3,7},{4,0},{5,1},{6,2},{7,3},{8,12},{9,13},{10,... | collective-permute-start | bytes 393224 | tf_op jit(solution)/shard_map/ppermute | solution.py:333
  31.9 10.8 %collective-permute-start.9 = (bf16[2,2,2,32,512]{4,3,2,1,0:T(8,128)(2,1)S(1)}, bf16[2,2,2,32,512]{4,3,2,1,0:T(8,128)(2,1)S(1)}, u32[]{:S(2)}, u32[]{:S(2)}) collective-permute-start(bf16[2,2,2,32,512]{4,3,2,1,0:T(8,128)(2,1)S(1)} %stack.16.refs_0_), channel_id=1, source_target_pairs={{0,2},{1,3},{2,0},{3,1},{4,6},{5,7},{6,4},{7,5},{8,10},{9,11},{10,... | collective-permute-start | bytes 786440 | tf_op jit(solution)/shard_map/ppermute | solution.py:333
  32.7 10.6 %collective-permute-start.7 = (bf16[1,2,2,32,512]{4,3,2,1,0:T(8,128)(2,1)S(1)}, bf16[1,2,2,32,512]{4,3,2,1,0:T(8,128)(2,1)S(1)}, u32[]{:S(2)}, u32[]{:S(2)}) collective-permute-start(bf16[1,2,2,32,512]{4,3,2,1,0:T(8,128)(2,1)S(1)} %add.82.refs_2_.refs_0_), channel_id=1, source_target_pairs={{0,4},{1,5},{2,6},{3,7},{4,0},{5,1},{6,2},{7,3},{8,12},{9,13},{10,... | collective-permute-start | bytes 393224 | tf_op jit(solution)/shard_map/ppermute | solution.py:333
  36.8 6.7 %collective-permute-start.10 = (bf16[2,2,2,32,512]{4,3,2,1,0:T(8,128)(2,1)S(1)}, bf16[2,2,2,32,512]{4,3,2,1,0:T(8,128)(2,1)S(1)}, u32[]{:S(2)}, u32[]{:S(2)}) collective-permute-start(bf16[2,2,2,32,512]{4,3,2,1,0:T(8,128)(2,1)S(1)} %stack.16.refs_0_), channel_id=1, source_target_pairs={{0,1},{1,0},{2,3},{3,2},{4,5},{5,4},{6,7},{7,6},{8,9},{9,8},{10,11... | collective-permute-start | bytes 786440 | tf_op jit(solution)/shard_map/ppermute | solution.py:333
  42.7 20.8 %copy-start = (s32[64,512]{1,0:T(8,128)S(1)}, s32[64,512]{1,0:T(8,128)}, u32[]{:S(2)}) copy-start(s32[64,512]{1,0:T(8,128)} %onset_ref.3) | copy-start | bytes 393220
  42.7 1.7 %collective-permute-start.11 = (bf16[2,2,2,32,512]{4,3,2,1,0:T(8,128)(2,1)S(1)}, bf16[2,2,2,32,512]{4,3,2,1,0:T(8,128)(2,1)S(1)}, u32[]{:S(2)}, u32[]{:S(2)}) collective-permute-start(bf16[2,2,2,32,512]{4,3,2,1,0:T(8,128)(2,1)S(1)} %collective-permute-done.9.refs_1_), channel_id=1, source_target_pairs={{0,1},{1,0},{2,3},{3,2},{4,5},{5,4},{6,7},{7,6},{8,9},{9,8},{10,11... | collective-permute-start | bytes 786440 | tf_op jit(solution)/shard_map/ppermute | solution.py:333
  43.3 8.3 %collective-permute-start.8 = (bf16[2,2,2,32,512]{4,3,2,1,0:T(8,128)(2,1)S(1)}, bf16[2,2,2,32,512]{4,3,2,1,0:T(8,128)(2,1)S(1)}, u32[]{:S(2)}, u32[]{:S(2)}) collective-permute-start(bf16[2,2,2,32,512]{4,3,2,1,0:T(8,128)(2,1)S(1)} %stack.17.refs_4_.refs_0_), channel_id=1, source_target_pairs={{0,2},{1,3},{2,0},{3,1},{4,6},{5,7},{6,4},{7,5},{8,10},{9,11},{10,... | collective-permute-start | bytes 786440 | tf_op jit(solution)/shard_map/ppermute | solution.py:333
  43.5 11.8 %collective-permute-start.12 = (bf16[2,2,2,32,512]{4,3,2,1,0:T(8,128)(2,1)S(1)}, bf16[2,2,2,32,512]{4,3,2,1,0:T(8,128)(2,1)S(1)}, u32[]{:S(2)}, u32[]{:S(2)}) collective-permute-start(bf16[2,2,2,32,512]{4,3,2,1,0:T(8,128)(2,1)S(1)} %stack.17.refs_4_.refs_0_), channel_id=1, source_target_pairs={{0,1},{1,0},{2,3},{3,2},{4,5},{5,4},{6,7},{7,6},{8,9},{9,8},{10,11... | collective-permute-start | bytes 786440 | tf_op jit(solution)/shard_map/ppermute | solution.py:333
  51.6 3.6 %collective-permute-start.13 = (bf16[2,2,2,32,512]{4,3,2,1,0:T(8,128)(2,1)S(1)}, bf16[2,2,2,32,512]{4,3,2,1,0:T(8,128)(2,1)S(1)}, u32[]{:S(2)}, u32[]{:S(2)}) collective-permute-start(bf16[2,2,2,32,512]{4,3,2,1,0:T(8,128)(2,1)S(1)} %stack.18.refs_1_), channel_id=1, source_target_pairs={{0,1},{1,0},{2,3},{3,2},{4,5},{5,4},{6,7},{7,6},{8,9},{9,8},{10,11... | collective-permute-start | bytes 786440 | tf_op jit(solution)/shard_map/ppermute | solution.py:333
  51.7 11.2 %collective-permute-start.19 = (bf16[2,2,32,512]{3,2,1,0:T(8,128)(2,1)S(1)}, bf16[2,2,32,512]{3,2,1,0:T(8,128)(2,1)S(1)}, u32[]{:S(2)}, u32[]{:S(2)}) collective-permute-start(bf16[2,2,32,512]{3,2,1,0:T(8,128)(2,1)S(1)} %respond.2.refs_1_.refs_0_), channel_id=1, source_target_pairs={{0,24},{8,16},{16,8},{24,0},{1,25},{9,17},{17,9},{25,1},{2,26},{10... | collective-permute-start | bytes 393224 | tf_op jit(solution)/shard_map/ppermute | solution.py:333
  54.3 9.2 %collective-permute-start.18 = (bf16[2,2,32,512]{3,2,1,0:T(8,128)(2,1)S(1)}, bf16[2,2,32,512]{3,2,1,0:T(8,128)(2,1)S(1)}, u32[]{:S(2)}, u32[]{:S(2)}) collective-permute-start(bf16[2,2,32,512]{3,2,1,0:T(8,128)(2,1)S(1)} %respond.2.refs_1_.refs_0_), channel_id=1, source_target_pairs={{0,16},{8,24},{16,0},{24,8},{1,17},{9,25},{17,1},{25,9},{2,18},{10... | collective-permute-start | bytes 393224 | tf_op jit(solution)/shard_map/ppermute | solution.py:333
  54.7 8.7 %collective-permute-start.17 = (bf16[2,2,32,512]{3,2,1,0:T(8,128)(2,1)S(1)}, bf16[2,2,32,512]{3,2,1,0:T(8,128)(2,1)S(1)}, u32[]{:S(2)}, u32[]{:S(2)}) collective-permute-start(bf16[2,2,32,512]{3,2,1,0:T(8,128)(2,1)S(1)} %respond.2.refs_1_.refs_0_), channel_id=1, source_target_pairs={{0,8},{8,0},{16,24},{24,16},{1,9},{9,1},{17,25},{25,17},{2,10},{10... | collective-permute-start | bytes 393224 | tf_op jit(solution)/shard_map/ppermute | solution.py:333
  59.9 10.7 %collective-permute-start.16 = (bf16[2,2,32,512]{3,2,1,0:T(8,128)(2,1)S(1)}, bf16[2,2,32,512]{3,2,1,0:T(8,128)(2,1)S(1)}, u32[]{:S(2)}, u32[]{:S(2)}) collective-permute-start(bf16[2,2,32,512]{3,2,1,0:T(8,128)(2,1)S(1)} %respond.3.refs_0_), channel_id=1, source_target_pairs={{0,24},{8,16},{16,8},{24,0},{1,25},{9,17},{17,9},{25,1},{2,26},{10... | collective-permute-start | bytes 393224 | tf_op jit(solution)/shard_map/ppermute | solution.py:333
  62.5 8.2 %collective-permute-start.15 = (bf16[2,2,32,512]{3,2,1,0:T(8,128)(2,1)S(1)}, bf16[2,2,32,512]{3,2,1,0:T(8,128)(2,1)S(1)}, u32[]{:S(2)}, u32[]{:S(2)}) collective-permute-start(bf16[2,2,32,512]{3,2,1,0:T(8,128)(2,1)S(1)} %respond.3.refs_0_), channel_id=1, source_target_pairs={{0,16},{8,24},{16,0},{24,8},{1,17},{9,25},{17,1},{25,9},{2,18},{10... | collective-permute-start | bytes 393224 | tf_op jit(solution)/shard_map/ppermute | solution.py:333
  62.9 7.7 %collective-permute-start.14 = (bf16[2,2,32,512]{3,2,1,0:T(8,128)(2,1)S(1)}, bf16[2,2,32,512]{3,2,1,0:T(8,128)(2,1)S(1)}, u32[]{:S(2)}, u32[]{:S(2)}) collective-permute-start(bf16[2,2,32,512]{3,2,1,0:T(8,128)(2,1)S(1)} %respond.3.refs_0_), channel_id=1, source_target_pairs={{0,8},{8,0},{16,24},{24,16},{1,9},{9,1},{17,25},{25,17},{2,10},{10... | collective-permute-start | bytes 393224 | tf_op jit(solution)/shard_map/ppermute | solution.py:333

commit v4 on v3

--- a/solution.py
+++ b/solution.py
@@ -14,6 +14,7 @@
 F_SLOTS = 3
 I_TIMES = 128
 I_SLOTS = 3
+I_CUTS = 4
 MIB = 1024 * 1024
 F_VMEM = 40 * MIB
 R_VMEM = 12 * MIB
@@ -193,6 +194,56 @@
     )(reflection, *pieces, *earlier)
 
 
+def half_kernel(masks, last, reflection_ref, own_ref, other_ref, *refs):
+    out, spectra = refs[-2:]
+    bands, _, rows, _ = reflection_ref.shape
+    _, _, _, focal, width = own_ref.shape
+    me = lax.axis_index("mat")
+    for i in range(len(masks)):
+        for core, pieces in enumerate((own_ref, other_ref)):
+            start = pl.multiple_of((me % 2 ^ core) * width, width)
+            spectra[i, :, :, pl.ds(start, width)] = pieces[i].reshape(bands, 2 * focal, width)
+    for band in range(bands):
+        total = refs[0][band] if last else None
+        for i, mask in enumerate(masks):
+            start = pl.multiple_of((me ^ mask) // 2 * 2 * width, 2 * width)
+            part = lax.dot_general(
+                reflection_ref[band, :, :, pl.ds(start, 2 * width)].reshape(2 * rows, 2 * width),
+                spectra[i, band],
+                (((1,), (1,)), ((), ())),
+                preferred_element_type=jnp.float32,
+            )
+            total = part if total is None else total + part
+        if last:
+            product = total.T
+            out[band, 0] = (product[:focal, :rows] - product[focal:, rows:]).astype(out.dtype)
+            out[band, 1] = (product[focal:, :rows] + product[:focal, rows:]).astype(out.dtype)
+        else:
+            out[band] = total
+
+
+def respond_half(reflection, own, other, masks, before, earlier):
+    per_device, _, rows, sources = reflection.shape
+    focal, width = own.shape[3:]
+    whole = pl.BlockSpec(memory_space=pltpu.VMEM)
+    if before is None:
+        shape = jax.ShapeDtypeStruct((per_device, 2 * rows, 2 * focal), jnp.float32)
+        given = []
+    else:
+        shape = jax.ShapeDtypeStruct((per_device, 2, focal, rows), jnp.bfloat16)
+        given = [before]
+    return pl.pallas_call(
+        functools.partial(half_kernel, masks, before is not None),
+        in_specs=[whole] * (3 + len(given)) + [pl.BlockSpec(memory_space=pl.ANY)] * len(earlier),
+        out_specs=whole,
+        out_shape=shape,
+        scratch_shapes=[pltpu.VMEM((len(masks), per_device, 2 * focal, 2 * width), jnp.bfloat16)],
+        compiler_params=pltpu.CompilerParams(vmem_limit_bytes=R_VMEM),
+        cost_estimate=pl.CostEstimate(flops=0, bytes_accessed=1024, transcendentals=0),
+        name="respond_half",
+    )(reflection, own, other, *given, *earlier)
+
+
 def spread_kernel(table_ref, out):
     def store(i, block):
         out[pl.ds(i * ROWS, ROWS), :] = block
@@ -221,6 +272,8 @@
 def inverse_kernel(first, has_before, spread, onset_ref, *refs):
     pieces, (out, weights, slots, sems) = refs[: -4 - has_before], refs[-4:]
     depth, times, rows, width = slots.shape
+    cuts = sems.shape[1]
+    some = times // cuts
     focal = pieces[0].shape[2]
     local_times = out.shape[0]
     steps = local_times // times
@@ -228,10 +281,11 @@
     share = weights.shape[0] // len(pieces)
     begin = lax.axis_index("freq") * local_times
 
-    def send(i):
+    def send(i, cut):
         slot = lax.rem(i, depth)
-        target = out.at[pl.ds(lax.rem(i, steps) * times, times), pl.ds(first + i // steps * rows, rows), :]
-        return pltpu.make_async_copy(slots.at[slot], target, sems.at[slot])
+        start = lax.rem(i, steps) * times + cut * some
+        target = out.at[pl.ds(start, some), pl.ds(first + i // steps * rows, rows), :]
+        return pltpu.make_async_copy(slots.at[slot, pl.ds(cut * some, some)], target, sems.at[slot, cut])
 
     @pl.loop(0, count)
     def _(i):
@@ -241,23 +295,28 @@
 
         @pl.when(i >= depth)
         def _():
-            send(i - depth).wait()
+            for cut in range(cuts):
+                send(i - depth, cut).wait()
 
         @pl.when(step == 0)
         def _():
             for j, piece in enumerate(pieces):
                 weights[pl.ds(j * share, share), :] = piece[:, :, place, :].reshape(share, width)
 
-        lines = pl.ds(pl.multiple_of(step * times * rows, times * rows), times * rows)
-        signal = jnp.dot(spread[lines, :], weights[...], preferred_element_type=jnp.float32)
-        signal = signal.reshape(times, rows, width)
-        moment = begin + step * times + lax.broadcasted_iota(jnp.int32, (times, 1, 1), 0)
         onset = onset_ref[pl.ds(pl.multiple_of(first + i // steps * rows, rows), rows), :]
-        slots[slot] = jnp.where(moment < onset[None], signal, 0.0).astype(out.dtype)
-        send(i).start()
+        for cut in range(cuts):
+            start = step * times + cut * some
+            lines = pl.ds(pl.multiple_of(start * rows, some * rows), some * rows)
+            signal = jnp.dot(spread[lines, :], weights[...], preferred_element_type=jnp.float32)
+            signal = signal.reshape(some, rows, width)
+            moment = begin + start + lax.broadcasted_iota(jnp.int32, (some, 1, 1), 0)
+            windowed = jnp.where(moment < onset[None], signal, 0.0).astype(out.dtype)
+            slots[slot, pl.ds(cut * some, some)] = windowed
+            send(i, cut).start()
 
     for i in range(max(0, count - depth), count):
-        send(jnp.int32(i)).wait()
+        for cut in range(cuts):
+            send(jnp.int32(i), cut).wait()
 
 
 def invert(table, onset, pieces, before, first, shape):
@@ -276,7 +335,7 @@
         scratch_shapes=[
             pltpu.VMEM((table.shape[1], width), jnp.bfloat16),
             pltpu.VMEM((I_SLOTS, times, ROWS, width), jnp.bfloat16),
-            pltpu.SemaphoreType.DMA((I_SLOTS,)),
+            pltpu.SemaphoreType.DMA((I_SLOTS, I_CUTS)),
         ],
         input_output_aliases={len(operands) - 1: 0} if has_before else {},
         compiler_params=pltpu.CompilerParams(vmem_limit_bytes=I_VMEM),
@@ -344,28 +403,33 @@
 
     parts = [forward(table, traces, i * focal, focal, per_device, freq_devices) for i in range(CHUNKS)]
     spectra = []
+    inverse_spread = spread(table)
     for i, part in enumerate(parts):
         arrived = [swap(part[mask], "freq", mask) for mask in range(1, freq_devices)]
-        spectra.append(add([part[0], *arrived], [later[0] for later in parts[i + 1 :]]))
+        spectra.append(add([part[0], *arrived], [later[0] for later in parts[i + 1 :]] or [inverse_spread]))
     held, masks, tied = [], [0], []
     for block in spectra:
         for step in steps[:-1]:
             block = stack([block, swap(block, "mat", step)], tied or [spectra[-1]])
         if not tied:
-            tied = [spread(table), load(reflection, [block])]
+            tied = [load(reflection, [block])]
         held.append((block, swap(block, "mat", steps[-1])))
     for step in steps[:-1]:
         masks = masks + [mask ^ step for mask in masks]
     masks = [masks, [mask ^ steps[-1] for mask in masks]]
     masks += [[mask ^ 1 for mask in some] for some in masks]
 
-    inverse_spread, loaded = tied
+    loaded = tied[0]
     responses = []
     for i, (block, other) in enumerate(held):
+        beside = swap(block, "mat", 1)
         if responses:
-            other = stack([other], [responses[-1][0]])
-        pieces = [block, other, swap(block, "mat", 1), swap(other, "mat", 1)]
-        response = respond(loaded, pieces, masks, [later for later, _ in held[i + 1 :]])
+            half = respond_half(loaded, block, beside, masks[0], None, [responses[-1][0]])
+            other = stack([other], [half])
+            response = respond_half(loaded, other, swap(other, "mat", 1), masks[1], half, [])
+        else:
+            pieces = [block, other, beside, swap(other, "mat", 1)]
+            response = respond(loaded, pieces, masks, [later for later, _ in held[i + 1 :]])
         responses.append([response] + [swap(response, "freq", mask) for mask in range(1, freq_devices)])
     windowed = None
     for i, pieces in enumerate(responses):

time: 78 us -> 75.5 us (0.968)
  waiting for transfers between devices: 8.09 us -> 5.89 us
    pallas_call x0 -> x2, Pallas kernels: none -> 4.79 us  [respond_half(): pl.pallas_call(functools.partial(half_kernel, masks, before is not None),...]
    pallas_call x2 -> x1, Pallas kernels: 9.25 us -> 4.63 us  [respond(): pl.pallas_call(functools.partial(response_kernel, masks), in_specs=[whole...]
    ppermute x20, waiting for transfers between devices: 8.09 us -> 5.89 us  [swap(): lax.ppermute(array, axis, [(i, i ^ mask) for i in range(lax.axis_size(axi...]
  transfers between devices with their start and end apart: 20 -> 20, of which waited for: 4 -> 6; matrix products, arithmetic and copies ran while one was open for 0% -> 0% of each run, Pallas kernels for 39% -> 40%
where the time goes in v4:
time: 75.5 us; the launch traced here: 75.3 us
  Pallas kernels  45.4 us (60%)
  starting transfers between devices  23.5 us (31%)
  waiting for transfers between devices  5.89 us (8%)
    ppermute x20, starting transfers between devices, swap(): lax.ppermute(array, axis, [(i, i ^ mask) for i in range(lax.axis_size(axi...  23.5 us
    pallas_call x2, Pallas kernels, forward(): pl.pallas_call(functools.partial(forward_kernel, first, focal), in_specs=...  15.5 us
    pallas_call x2, Pallas kernels, invert(): pl.pallas_call(functools.partial(inverse_kernel, first, has_before), in_s...  13.7 us
    ppermute x20, waiting for transfers between devices, swap(): lax.ppermute(array, axis, [(i, i ^ mask) for i in range(lax.axis_size(axi...  5.89 us
    pallas_call x1, Pallas kernels, load(): pl.pallas_call(load_kernel, in_specs=[pl.BlockSpec(memory_space=pl.ANY)]...  5.78 us
    pallas_call x2, Pallas kernels, respond_half(): pl.pallas_call(functools.partial(half_kernel, masks, before is not None),...  4.79 us
    pallas_call x1, Pallas kernels, respond(): pl.pallas_call(functools.partial(response_kernel, masks), in_specs=[whole...  4.63 us
  transfers between devices with their start and end apart: 20, of which 6 were waited for; matrix products, arithmetic and copies ran while one was open for 0% of the time, Pallas kernels for 40%

profile of v4, /device:TPU:0, one launch (start us, length us, event | category | flops | bytes accessed | tf_op | source)
XLA Modules:
  0.0 75.3 jit_solution(7720796822643467489)
XLA Ops:
  0.5 7.9 %forward.2 = (f32[2,2,32,512]{3,2,1,0:T(8,128)S(1)}, bf16[2,2,32,512]{3,2,1,0:T(8,128)(2,1)S(1)}, bf16[2,2,32,512]{3,2,1,0:T(8,128)(2,1)S(1)}, bf16[2,2,32,512]{3,2,1,0:T(8,128)(2,1)S(1)}) custom-call(bf16[2,16,512]{2,1,0:T(8,128)(2,1)S(1)} %constant_dynamic-update-slice_fusion.table_ref, bf16[512,64,512]{2,1,0:T(8,128)(2,1)} %traces_ref.3), custom_call_target="tpu_custom_call" | custom-call | flops 4294967296 | bytes 16777216 | tf_op jit(solution)/shard_map/forward/pallas_call | solution.py:116
  8.4 3.0 %collective-permute-start = (bf16[2,2,32,512]{3,2,1,0:T(8,128)(2,1)S(1)}, bf16[2,2,32,512]{3,2,1,0:T(8,128)(2,1)S(1)}, u32[]{:S(2)}, u32[]{:S(2)}) collective-permute-start(bf16[2,2,32,512]{3,2,1,0:T(8,128)(2,1)S(1)} %get-tuple-element.14), channel_id=1, source_target_pairs={{0,8},{8,0},{16,24},{24,16},{1,9},{9,1},{17,25},{25,17},{2,10},{10... | collective-permute-start | bytes 393224 | tf_op jit(solution)/shard_map/ppermute | solution.py:392
  11.4 1.5 %collective-permute-start.1 = (bf16[2,2,32,512]{3,2,1,0:T(8,128)(2,1)S(1)}, bf16[2,2,32,512]{3,2,1,0:T(8,128)(2,1)S(1)}, u32[]{:S(2)}, u32[]{:S(2)}) collective-permute-start(bf16[2,2,32,512]{3,2,1,0:T(8,128)(2,1)S(1)} %get-tuple-element.15), channel_id=1, source_target_pairs={{0,16},{8,24},{16,0},{24,8},{1,17},{9,25},{17,1},{25,9},{2,18},{10... | collective-permute-start | bytes 393224 | tf_op jit(solution)/shard_map/ppermute | solution.py:392
  13.0 7.5 %forward.3 = (f32[2,2,32,512]{3,2,1,0:T(8,128)S(1)}, bf16[2,2,32,512]{3,2,1,0:T(8,128)(2,1)S(1)}, bf16[2,2,32,512]{3,2,1,0:T(8,128)(2,1)S(1)}, bf16[2,2,32,512]{3,2,1,0:T(8,128)(2,1)S(1)}) custom-call(bf16[2,16,512]{2,1,0:T(8,128)(2,1)S(1)} %constant_dynamic-update-slice_fusion.table_ref, bf16[512,64,512]{2,1,0:T(8,128)(2,1)} %traces_ref.3), custom_call_target="tpu_custom_call" | custom-call | flops 4294967296 | bytes 16777216 | tf_op jit(solution)/shard_map/forward/pallas_call | solution.py:116
  20.5 2.0 %collective-permute-start.4 = (bf16[2,2,32,512]{3,2,1,0:T(8,128)(2,1)S(1)}, bf16[2,2,32,512]{3,2,1,0:T(8,128)(2,1)S(1)}, u32[]{:S(2)}, u32[]{:S(2)}) collective-permute-start(bf16[2,2,32,512]{3,2,1,0:T(8,128)(2,1)S(1)} %get-tuple-element.18), channel_id=1, source_target_pairs={{0,8},{8,0},{16,24},{24,16},{1,9},{9,1},{17,25},{25,17},{2,10},{10... | collective-permute-start | bytes 393224 | tf_op jit(solution)/shard_map/ppermute | solution.py:392
  22.5 1.5 %collective-permute-start.5 = (bf16[2,2,32,512]{3,2,1,0:T(8,128)(2,1)S(1)}, bf16[2,2,32,512]{3,2,1,0:T(8,128)(2,1)S(1)}, u32[]{:S(2)}, u32[]{:S(2)}) collective-permute-start(bf16[2,2,32,512]{3,2,1,0:T(8,128)(2,1)S(1)} %get-tuple-element.19), channel_id=1, source_target_pairs={{0,16},{8,24},{16,0},{24,8},{1,17},{9,25},{17,1},{25,9},{2,18},{10... | collective-permute-start | bytes 393224 | tf_op jit(solution)/shard_map/ppermute | solution.py:392
  24.1 3.1 %collective-permute-start.3 = (bf16[1,2,2,32,512]{4,3,2,1,0:T(8,128)(2,1)S(1)}, bf16[1,2,2,32,512]{4,3,2,1,0:T(8,128)(2,1)S(1)}, u32[]{:S(2)}, u32[]{:S(2)}) collective-permute-start(bf16[1,2,2,32,512]{4,3,2,1,0:T(8,128)(2,1)S(1)} %add.81.refs_0_), channel_id=1, source_target_pairs={{0,4},{1,5},{2,6},{3,7},{4,0},{5,1},{6,2},{7,3},{8,12},{9,13},{10,... | collective-permute-start | bytes 393224 | tf_op jit(solution)/shard_map/ppermute | solution.py:392
  27.2 0.8 %spread.1.refs_4_ = bf16[8192,256]{1,0:T(8,128)(2,1)S(1)} custom-call(bf16[2,16,512]{2,1,0:T(8,128)(2,1)S(1)} %constant_dynamic-update-slice_fusion.table_ref), custom_call_target="tpu_custom_call" | custom-call | bytes 4194304 | tf_op jit(solution)/shard_map/spread/pallas_call | solution.py:261
  28.0 2.2 %collective-permute-done.5.refs_2_ = bf16[2,2,32,512]{3,2,1,0:T(8,128)(2,1)S(1)} collective-permute-done((bf16[2,2,32,512]{3,2,1,0:T(8,128)(2,1)S(1)}, bf16[2,2,32,512]{3,2,1,0:T(8,128)(2,1)S(1)}, u32[]{:S(2)}, u32[]{:S(2)}) %collective-permute-start.5) | collective-permute-done | bytes 131104 | tf_op jit(solution)/shard_map/ppermute | solution.py:392
  30.3 1.6 %collective-permute-done.3.refs_1_ = bf16[1,2,2,32,512]{4,3,2,1,0:T(8,128)(2,1)S(1)} collective-permute-done((bf16[1,2,2,32,512]{4,3,2,1,0:T(8,128)(2,1)S(1)}, bf16[1,2,2,32,512]{4,3,2,1,0:T(8,128)(2,1)S(1)}, u32[]{:S(2)}, u32[]{:S(2)}) %collective-permute-start.3) | collective-permute-done | bytes 131104 | tf_op jit(solution)/shard_map/ppermute | solution.py:392
  31.9 0.8 %collective-permute-start.10 = (bf16[2,2,2,32,512]{4,3,2,1,0:T(8,128)(2,1)S(1)}, bf16[2,2,2,32,512]{4,3,2,1,0:T(8,128)(2,1)S(1)}, u32[]{:S(2)}, u32[]{:S(2)}) collective-permute-start(bf16[2,2,2,32,512]{4,3,2,1,0:T(8,128)(2,1)S(1)} %stack.16.refs_0_), channel_id=1, source_target_pairs={{0,2},{1,3},{2,0},{3,1},{4,6},{5,7},{6,4},{7,5},{8,10},{9,11},{10,... | collective-permute-start | bytes 786440 | tf_op jit(solution)/shard_map/ppermute | solution.py:392
  32.7 3.4 %collective-permute-start.7 = (bf16[1,2,2,32,512]{4,3,2,1,0:T(8,128)(2,1)S(1)}, bf16[1,2,2,32,512]{4,3,2,1,0:T(8,128)(2,1)S(1)}, u32[]{:S(2)}, u32[]{:S(2)}) collective-permute-start(bf16[1,2,2,32,512]{4,3,2,1,0:T(8,128)(2,1)S(1)} %add.82.refs_2_.refs_0_), channel_id=1, source_target_pairs={{0,4},{1,5},{2,6},{3,7},{4,0},{5,1},{6,2},{7,3},{8,12},{9,13},{10,... | collective-permute-start | bytes 393224 | tf_op jit(solution)/shard_map/ppermute | solution.py:392
  36.1 5.8 %load.1.refs_2_.reflection_ref = bf16[2,2,512,4096]{3,2,1,0:T(8,128)(2,1)S(1)} custom-call(bf16[2,2,512,4096]{3,2,1,0:T(8,128)(2,1)} %reflection_ref.1, bf16[2,2,2,32,512]{4,3,2,1,0:T(8,128)(2,1)S(1)} %stack.16.refs_0_), custom_call_target="tpu_custom_call" | custom-call | tf_op jit(solution)/shard_map/load/pallas_call | solution.py:150
  41.9 0.6 collective-permute-start.12
  42.8 0.8 %collective-permute-done.12.refs_3_ = bf16[2,2,2,32,512]{4,3,2,1,0:T(8,128)(2,1)S(1)} collective-permute-done((bf16[2,2,2,32,512]{4,3,2,1,0:T(8,128)(2,1)S(1)}, bf16[2,2,2,32,512]{4,3,2,1,0:T(8,128)(2,1)S(1)}, u32[]{:S(2)}, u32[]{:S(2)}) %collective-permute-start.12) | collective-permute-done | bytes 262176 | tf_op jit(solution)/shard_map/ppermute | solution.py:392
  43.6 4.6 %respond.1.refs_0_ = bf16[2,2,32,512]{3,2,1,0:T(8,128)(2,1)S(1)} custom-call(bf16[2,2,512,4096]{3,2,1,0:T(8,128)(2,1)S(1)} %load.1.refs_2_.reflection_ref, bf16[2,2,2,32,512]{4,3,2,1,0:T(8,128)(2,1)S(1)} %stack.16.refs_0_, bf16[2,2,2,32,512]{4,3,2,1,0:T(8,128)(2,1)S(1)} %collective-permute-done.10.refs_1_, ...), custom_call_target="tpu_custom_call" | custom-call | bytes 1024 | tf_op jit(solution)/shard_map/respond/pallas_call | solution.py:185
  48.3 2.4 %respond_half.2.refs_1_.refs_0_ = f32[2,1024,64]{2,1,0:T(8,128)S(1)} custom-call(bf16[2,2,512,4096]{3,2,1,0:T(8,128)(2,1)S(1)} %load.1.refs_2_.reflection_ref, bf16[2,2,2,32,512]{4,3,2,1,0:T(8,128)(2,1)S(1)} %stack.17.refs_4_.own_ref, bf16[2,2,2,32,512]{4,3,2,1,0:T(8,128)(2,1)S(1)} %collective-permute-done.9.other_ref, ...), custom_call_target="tpu_custom_call" | custom-call | bytes 1024 | tf_op jit(solution)/shard_map/respond_half/pallas_call | solution.py:235
  50.6 0.7 collective-permute-done.8.refs_0_
  51.4 2.5 %collective-permute-start.19 = (bf16[2,2,32,512]{3,2,1,0:T(8,128)(2,1)S(1)}, bf16[2,2,32,512]{3,2,1,0:T(8,128)(2,1)S(1)}, u32[]{:S(2)}, u32[]{:S(2)}) collective-permute-start(bf16[2,2,32,512]{3,2,1,0:T(8,128)(2,1)S(1)} %respond.1.refs_0_), channel_id=1, source_target_pairs={{0,24},{8,16},{16,8},{24,0},{1,25},{9,17},{17,9},{25,1},{2,26},{10... | collective-permute-start | bytes 393224 | tf_op jit(solution)/shard_map/ppermute | solution.py:392
  54.9 2.4 %respond_half.3.refs_0_ = bf16[2,2,32,512]{3,2,1,0:T(8,128)(2,1)S(1)} custom-call(bf16[2,2,512,4096]{3,2,1,0:T(8,128)(2,1)S(1)} %load.1.refs_2_.reflection_ref, bf16[2,2,2,32,512]{4,3,2,1,0:T(8,128)(2,1)S(1)} %stack.18.own_ref, bf16[2,2,2,32,512]{4,3,2,1,0:T(8,128)(2,1)S(1)} %collective-permute-done.13.other_ref, f32[2,1024,64]{2,1,0:T(8,128)S(1)} %respond_half.2.refs_1_.refs_0_), custom_call_target="tpu_custom_call" | custom-call | bytes 1024 | tf_op jit(solution)/shard_map/respond_half/pallas_call | solution.py:235
  57.4 2.5 %collective-permute-start.16 = (bf16[2,2,32,512]{3,2,1,0:T(8,128)(2,1)S(1)}, bf16[2,2,32,512]{3,2,1,0:T(8,128)(2,1)S(1)}, u32[]{:S(2)}, u32[]{:S(2)}) collective-permute-start(bf16[2,2,32,512]{3,2,1,0:T(8,128)(2,1)S(1)} %respond_half.3.refs_0_), channel_id=1, source_target_pairs={{0,24},{8,16},{16,8},{24,0},{1,25},{9,17},{17,9},{25,1},{2,26},{10... | collective-permute-start | bytes 393224 | tf_op jit(solution)/shard_map/ppermute | solution.py:392
  60.4 0.5 collective-permute-start.14
  61.6 6.8 %invert.2.refs_4_ = bf16[512,64,512]{2,1,0:T(8,128)(2,1)} custom-call(bf16[8192,256]{1,0:T(8,128)(2,1)S(1)} %spread.1.refs_4_, s32[64,512]{1,0:T(8,128)S(1)} %copy-done, bf16[2,2,32,512]{3,2,1,0:T(8,128)(2,1)S(1)} %respond.1.refs_0_, bf16[2,2,32,512]{3,2,1,0:T(8,128)(2,1)S(1)} %collective-permute-done.17.refs_1_, ...), custom_call_target="tpu_custom_call" | custom-call | flops 4294967296 | bytes 16777216 | tf_op jit(solution)/shard_map/invert/pallas_call | solution.py:330
  68.4 6.9 %invert.3 = bf16[512,64,512]{2,1,0:T(8,128)(2,1)} custom-call(bf16[8192,256]{1,0:T(8,128)(2,1)S(1)} %spread.1.refs_4_, s32[64,512]{1,0:T(8,128)S(1)} %copy-done, bf16[2,2,32,512]{3,2,1,0:T(8,128)(2,1)S(1)} %respond_half.3.refs_0_, bf16[2,2,32,512]{3,2,1,0:T(8,128)(2,1)S(1)} %collective-permute-done.14.refs_1_, ...), custom_call_target="tpu_custom_call", output_to_operand_aliasing={{}: (6, {})} | custom-call | flops 4294967296 | bytes 16777216 | tf_op jit(solution)/shard_map/invert/pallas_call | solution.py:330
  (44 shorter events, 3.2 us)
Async XLA Ops:
  8.4 15.6 %collective-permute-start = (bf16[2,2,32,512]{3,2,1,0:T(8,128)(2,1)S(1)}, bf16[2,2,32,512]{3,2,1,0:T(8,128)(2,1)S(1)}, u32[]{:S(2)}, u32[]{:S(2)}) collective-permute-start(bf16[2,2,32,512]{3,2,1,0:T(8,128)(2,1)S(1)} %get-tuple-element.14), channel_id=1, source_target_pairs={{0,8},{8,0},{16,24},{24,16},{1,9},{9,1},{17,25},{25,17},{2,10},{10... | collective-permute-start | bytes 393224 | tf_op jit(solution)/shard_map/ppermute | solution.py:392
  11.4 12.7 %collective-permute-start.1 = (bf16[2,2,32,512]{3,2,1,0:T(8,128)(2,1)S(1)}, bf16[2,2,32,512]{3,2,1,0:T(8,128)(2,1)S(1)}, u32[]{:S(2)}, u32[]{:S(2)}) collective-permute-start(bf16[2,2,32,512]{3,2,1,0:T(8,128)(2,1)S(1)} %get-tuple-element.15), channel_id=1, source_target_pairs={{0,16},{8,24},{16,0},{24,8},{1,17},{9,25},{17,1},{25,9},{2,18},{10... | collective-permute-start | bytes 393224 | tf_op jit(solution)/shard_map/ppermute | solution.py:392
  12.9 11.1 %collective-permute-start.2 = (bf16[2,2,32,512]{3,2,1,0:T(8,128)(2,1)S(1)}, bf16[2,2,32,512]{3,2,1,0:T(8,128)(2,1)S(1)}, u32[]{:S(2)}, u32[]{:S(2)}) collective-permute-start(bf16[2,2,32,512]{3,2,1,0:T(8,128)(2,1)S(1)} %get-tuple-element.16), channel_id=1, source_target_pairs={{0,24},{8,16},{16,8},{24,0},{1,25},{9,17},{17,9},{25,1},{2,26},{10... | collective-permute-start | bytes 393224 | tf_op jit(solution)/shard_map/ppermute | solution.py:392
  20.5 7.5 %collective-permute-start.4 = (bf16[2,2,32,512]{3,2,1,0:T(8,128)(2,1)S(1)}, bf16[2,2,32,512]{3,2,1,0:T(8,128)(2,1)S(1)}, u32[]{:S(2)}, u32[]{:S(2)}) collective-permute-start(bf16[2,2,32,512]{3,2,1,0:T(8,128)(2,1)S(1)} %get-tuple-element.18), channel_id=1, source_target_pairs={{0,8},{8,0},{16,24},{24,16},{1,9},{9,1},{17,25},{25,17},{2,10},{10... | collective-permute-start | bytes 393224 | tf_op jit(solution)/shard_map/ppermute | solution.py:392
  22.5 7.7 %collective-permute-start.5 = (bf16[2,2,32,512]{3,2,1,0:T(8,128)(2,1)S(1)}, bf16[2,2,32,512]{3,2,1,0:T(8,128)(2,1)S(1)}, u32[]{:S(2)}, u32[]{:S(2)}) collective-permute-start(bf16[2,2,32,512]{3,2,1,0:T(8,128)(2,1)S(1)} %get-tuple-element.19), channel_id=1, source_target_pairs={{0,16},{8,24},{16,0},{24,8},{1,17},{9,25},{17,1},{25,9},{2,18},{10... | collective-permute-start | bytes 393224 | tf_op jit(solution)/shard_map/ppermute | solution.py:392
  24.0 6.2 %collective-permute-start.6 = (bf16[2,2,32,512]{3,2,1,0:T(8,128)(2,1)S(1)}, bf16[2,2,32,512]{3,2,1,0:T(8,128)(2,1)S(1)}, u32[]{:S(2)}, u32[]{:S(2)}) collective-permute-start(bf16[2,2,32,512]{3,2,1,0:T(8,128)(2,1)S(1)} %get-tuple-element.20), channel_id=1, source_target_pairs={{0,24},{8,16},{16,8},{24,0},{1,25},{9,17},{17,9},{25,1},{2,26},{10... | collective-permute-start | bytes 393224 | tf_op jit(solution)/shard_map/ppermute | solution.py:392
  24.1 7.7 %collective-permute-start.3 = (bf16[1,2,2,32,512]{4,3,2,1,0:T(8,128)(2,1)S(1)}, bf16[1,2,2,32,512]{4,3,2,1,0:T(8,128)(2,1)S(1)}, u32[]{:S(2)}, u32[]{:S(2)}) collective-permute-start(bf16[1,2,2,32,512]{4,3,2,1,0:T(8,128)(2,1)S(1)} %add.81.refs_0_), channel_id=1, source_target_pairs={{0,4},{1,5},{2,6},{3,7},{4,0},{5,1},{6,2},{7,3},{8,12},{9,13},{10,... | collective-permute-start | bytes 393224 | tf_op jit(solution)/shard_map/ppermute | solution.py:392
  31.9 10.0 %collective-permute-start.10 = (bf16[2,2,2,32,512]{4,3,2,1,0:T(8,128)(2,1)S(1)}, bf16[2,2,2,32,512]{4,3,2,1,0:T(8,128)(2,1)S(1)}, u32[]{:S(2)}, u32[]{:S(2)}) collective-permute-start(bf16[2,2,2,32,512]{4,3,2,1,0:T(8,128)(2,1)S(1)} %stack.16.refs_0_), channel_id=1, source_target_pairs={{0,2},{1,3},{2,0},{3,1},{4,6},{5,7},{6,4},{7,5},{8,10},{9,11},{10,... | collective-permute-start | bytes 786440 | tf_op jit(solution)/shard_map/ppermute | solution.py:392
  32.7 9.8 %collective-permute-start.7 = (bf16[1,2,2,32,512]{4,3,2,1,0:T(8,128)(2,1)S(1)}, bf16[1,2,2,32,512]{4,3,2,1,0:T(8,128)(2,1)S(1)}, u32[]{:S(2)}, u32[]{:S(2)}) collective-permute-start(bf16[1,2,2,32,512]{4,3,2,1,0:T(8,128)(2,1)S(1)} %add.82.refs_2_.refs_0_), channel_id=1, source_target_pairs={{0,4},{1,5},{2,6},{3,7},{4,0},{5,1},{6,2},{7,3},{8,12},{9,13},{10,... | collective-permute-start | bytes 393224 | tf_op jit(solution)/shard_map/ppermute | solution.py:392
  36.1 6.7 %collective-permute-start.11 = (bf16[2,2,2,32,512]{4,3,2,1,0:T(8,128)(2,1)S(1)}, bf16[2,2,2,32,512]{4,3,2,1,0:T(8,128)(2,1)S(1)}, u32[]{:S(2)}, u32[]{:S(2)}) collective-permute-start(bf16[2,2,2,32,512]{4,3,2,1,0:T(8,128)(2,1)S(1)} %stack.16.refs_0_), channel_id=1, source_target_pairs={{0,1},{1,0},{2,3},{3,2},{4,5},{5,4},{6,7},{7,6},{8,9},{9,8},{10,11... | collective-permute-start | bytes 786440 | tf_op jit(solution)/shard_map/ppermute | solution.py:392
  41.9 19.7 %copy-start = (s32[64,512]{1,0:T(8,128)S(1)}, s32[64,512]{1,0:T(8,128)}, u32[]{:S(2)}) copy-start(s32[64,512]{1,0:T(8,128)} %onset_ref.3) | copy-start | bytes 393220
  41.9 1.7 %collective-permute-start.12 = (bf16[2,2,2,32,512]{4,3,2,1,0:T(8,128)(2,1)S(1)}, bf16[2,2,2,32,512]{4,3,2,1,0:T(8,128)(2,1)S(1)}, u32[]{:S(2)}, u32[]{:S(2)}) collective-permute-start(bf16[2,2,2,32,512]{4,3,2,1,0:T(8,128)(2,1)S(1)} %collective-permute-done.10.refs_1_), channel_id=1, source_target_pairs={{0,1},{1,0},{2,3},{3,2},{4,5},{5,4},{6,7},{7,6},{8,9},{9,8},{10,11... | collective-permute-start | bytes 786440 | tf_op jit(solution)/shard_map/ppermute | solution.py:392
  42.5 5.8 %collective-permute-start.9 = (bf16[2,2,2,32,512]{4,3,2,1,0:T(8,128)(2,1)S(1)}, bf16[2,2,2,32,512]{4,3,2,1,0:T(8,128)(2,1)S(1)}, u32[]{:S(2)}, u32[]{:S(2)}) collective-permute-start(bf16[2,2,2,32,512]{4,3,2,1,0:T(8,128)(2,1)S(1)} %stack.17.refs_4_.own_ref), channel_id=1, source_target_pairs={{0,1},{1,0},{2,3},{3,2},{4,5},{5,4},{6,7},{7,6},{8,9},{9,8},{10,11... | collective-permute-start | bytes 786440 | tf_op jit(solution)/shard_map/ppermute | solution.py:392
  42.6 8.7 %collective-permute-start.8 = (bf16[2,2,2,32,512]{4,3,2,1,0:T(8,128)(2,1)S(1)}, bf16[2,2,2,32,512]{4,3,2,1,0:T(8,128)(2,1)S(1)}, u32[]{:S(2)}, u32[]{:S(2)}) collective-permute-start(bf16[2,2,2,32,512]{4,3,2,1,0:T(8,128)(2,1)S(1)} %stack.17.refs_4_.own_ref), channel_id=1, source_target_pairs={{0,2},{1,3},{2,0},{3,1},{4,6},{5,7},{6,4},{7,5},{8,10},{9,11},{10,... | collective-permute-start | bytes 786440 | tf_op jit(solution)/shard_map/ppermute | solution.py:392
  51.3 3.6 %collective-permute-start.13 = (bf16[2,2,2,32,512]{4,3,2,1,0:T(8,128)(2,1)S(1)}, bf16[2,2,2,32,512]{4,3,2,1,0:T(8,128)(2,1)S(1)}, u32[]{:S(2)}, u32[]{:S(2)}) collective-permute-start(bf16[2,2,2,32,512]{4,3,2,1,0:T(8,128)(2,1)S(1)} %stack.18.own_ref), channel_id=1, source_target_pairs={{0,1},{1,0},{2,3},{3,2},{4,5},{5,4},{6,7},{7,6},{8,9},{9,8},{10,11... | collective-permute-start | bytes 786440 | tf_op jit(solution)/shard_map/ppermute | solution.py:392
  51.4 9.0 %collective-permute-start.19 = (bf16[2,2,32,512]{3,2,1,0:T(8,128)(2,1)S(1)}, bf16[2,2,32,512]{3,2,1,0:T(8,128)(2,1)S(1)}, u32[]{:S(2)}, u32[]{:S(2)}) collective-permute-start(bf16[2,2,32,512]{3,2,1,0:T(8,128)(2,1)S(1)} %respond.1.refs_0_), channel_id=1, source_target_pairs={{0,24},{8,16},{16,8},{24,0},{1,25},{9,17},{17,9},{25,1},{2,26},{10... | collective-permute-start | bytes 393224 | tf_op jit(solution)/shard_map/ppermute | solution.py:392
  53.9 7.5 %collective-permute-start.18 = (bf16[2,2,32,512]{3,2,1,0:T(8,128)(2,1)S(1)}, bf16[2,2,32,512]{3,2,1,0:T(8,128)(2,1)S(1)}, u32[]{:S(2)}, u32[]{:S(2)}) collective-permute-start(bf16[2,2,32,512]{3,2,1,0:T(8,128)(2,1)S(1)} %respond.1.refs_0_), channel_id=1, source_target_pairs={{0,16},{8,24},{16,0},{24,8},{1,17},{9,25},{17,1},{25,9},{2,18},{10... | collective-permute-start | bytes 393224 | tf_op jit(solution)/shard_map/ppermute | solution.py:392
  54.4 7.2 %collective-permute-start.17 = (bf16[2,2,32,512]{3,2,1,0:T(8,128)(2,1)S(1)}, bf16[2,2,32,512]{3,2,1,0:T(8,128)(2,1)S(1)}, u32[]{:S(2)}, u32[]{:S(2)}) collective-permute-start(bf16[2,2,32,512]{3,2,1,0:T(8,128)(2,1)S(1)} %respond.1.refs_0_), channel_id=1, source_target_pairs={{0,8},{8,0},{16,24},{24,16},{1,9},{9,1},{17,25},{25,17},{2,10},{10... | collective-permute-start | bytes 393224 | tf_op jit(solution)/shard_map/ppermute | solution.py:392
  57.4 11.0 %collective-permute-start.16 = (bf16[2,2,32,512]{3,2,1,0:T(8,128)(2,1)S(1)}, bf16[2,2,32,512]{3,2,1,0:T(8,128)(2,1)S(1)}, u32[]{:S(2)}, u32[]{:S(2)}) collective-permute-start(bf16[2,2,32,512]{3,2,1,0:T(8,128)(2,1)S(1)} %respond_half.3.refs_0_), channel_id=1, source_target_pairs={{0,24},{8,16},{16,8},{24,0},{1,25},{9,17},{17,9},{25,1},{2,26},{10... | collective-permute-start | bytes 393224 | tf_op jit(solution)/shard_map/ppermute | solution.py:392
  59.9 8.5 %collective-permute-start.15 = (bf16[2,2,32,512]{3,2,1,0:T(8,128)(2,1)S(1)}, bf16[2,2,32,512]{3,2,1,0:T(8,128)(2,1)S(1)}, u32[]{:S(2)}, u32[]{:S(2)}) collective-permute-start(bf16[2,2,32,512]{3,2,1,0:T(8,128)(2,1)S(1)} %respond_half.3.refs_0_), channel_id=1, source_target_pairs={{0,16},{8,24},{16,0},{24,8},{1,17},{9,25},{17,1},{25,9},{2,18},{10... | collective-permute-start | bytes 393224 | tf_op jit(solution)/shard_map/ppermute | solution.py:392
  60.4 8.0 %collective-permute-start.14 = (bf16[2,2,32,512]{3,2,1,0:T(8,128)(2,1)S(1)}, bf16[2,2,32,512]{3,2,1,0:T(8,128)(2,1)S(1)}, u32[]{:S(2)}, u32[]{:S(2)}) collective-permute-start(bf16[2,2,32,512]{3,2,1,0:T(8,128)(2,1)S(1)} %respond_half.3.refs_0_), channel_id=1, source_target_pairs={{0,8},{8,0},{16,24},{24,16},{1,9},{9,1},{17,25},{25,17},{2,10},{10... | collective-permute-start | bytes 393224 | tf_op jit(solution)/shard_map/ppermute | solution.py:392

commit v5 on v4

--- a/solution.py
+++ b/solution.py
@@ -134,34 +134,38 @@
     )(table, traces)
 
 
-def load_kernel(reflection_ref, *refs):
+def load_kernel(first, reflection_ref, *refs):
     out, sems = refs[-2:]
-
-    def fetch(i):
-        return pltpu.make_async_copy(reflection_ref.at[i], out.at[i], sems.at[i])
-
-    for i in range(out.shape[0]):
-        fetch(i).start()
-    for i in range(out.shape[0]):
-        fetch(i).wait()
-
-
-def load(reflection, earlier):
-    return pl.pallas_call(
-        load_kernel,
+    bands, parts = out.shape[:2]
+
+    def fetch(band, part):
+        return pltpu.make_async_copy(reflection_ref.at[first + band, part], out.at[band, part], sems.at[band, part])
+
+    for band in range(bands):
+        for part in range(parts):
+            fetch(band, part).start()
+    for band in range(bands):
+        for part in range(parts):
+            fetch(band, part).wait()
+
+
+def load(reflection, first, bands, earlier):
+    return pl.pallas_call(
+        functools.partial(load_kernel, first),
         in_specs=[pl.BlockSpec(memory_space=pl.ANY)] * (1 + len(earlier)),
         out_specs=pl.BlockSpec(memory_space=pltpu.VMEM),
-        out_shape=jax.ShapeDtypeStruct(reflection.shape, reflection.dtype),
-        scratch_shapes=[pltpu.SemaphoreType.DMA((reflection.shape[0],))],
+        out_shape=jax.ShapeDtypeStruct((bands, *reflection.shape[1:]), reflection.dtype),
+        scratch_shapes=[pltpu.SemaphoreType.DMA((bands, reflection.shape[1]))],
         compiler_params=pltpu.CompilerParams(vmem_limit_bytes=L_VMEM),
         name="load",
     )(reflection, *earlier)
 
 
-def response_kernel(masks, reflection_ref, *refs):
+def response_kernel(masks, loads, *refs):
+    kept, refs = refs[:loads], refs[loads:]
     out, spectra = refs[-2:]
-    bands, _, rows, sources = reflection_ref.shape
-    _, _, _, focal, width = refs[0].shape
+    share, _, rows, sources = kept[0].shape
+    _, bands, _, focal, width = refs[0].shape
     me = lax.axis_index("mat")
     for pieces, origins in zip(refs, masks):
         for i, mask in enumerate(origins):
@@ -169,7 +173,7 @@
             spectra[:, :, pl.ds(start, width)] = pieces[i].reshape(bands, 2 * focal, width)
     for band in range(bands):
         product = lax.dot_general(
-            reflection_ref[band].reshape(2 * rows, sources),
+            kept[band // share][band % share].reshape(2 * rows, sources),
             spectra[band],
             (((1,), (1,)), ((), ())),
             preferred_element_type=jnp.float32,
@@ -178,26 +182,26 @@
         out[band, 1] = (product[focal:, :rows] + product[:focal, rows:]).astype(out.dtype)
 
 
-def respond(reflection, pieces, masks, earlier):
-    per_device, _, rows, sources = reflection.shape
-    focal, width = pieces[0].shape[3:]
-    whole = pl.BlockSpec(memory_space=pltpu.VMEM)
-    return pl.pallas_call(
-        functools.partial(response_kernel, masks),
-        in_specs=[whole] * (1 + len(pieces)) + [pl.BlockSpec(memory_space=pl.ANY)] * len(earlier),
+def respond(kept, pieces, masks, earlier):
+    _, _, rows, sources = kept[0].shape
+    _, per_device, _, focal, width = pieces[0].shape
+    whole = pl.BlockSpec(memory_space=pltpu.VMEM)
+    return pl.pallas_call(
+        functools.partial(response_kernel, masks, len(kept)),
+        in_specs=[whole] * (len(kept) + len(pieces)) + [pl.BlockSpec(memory_space=pl.ANY)] * len(earlier),
         out_specs=whole,
         out_shape=jax.ShapeDtypeStruct((per_device, 2, focal, rows), jnp.bfloat16),
         scratch_shapes=[pltpu.VMEM((per_device, 2 * focal, sources), jnp.bfloat16)],
         compiler_params=pltpu.CompilerParams(vmem_limit_bytes=R_VMEM),
         cost_estimate=pl.CostEstimate(flops=0, bytes_accessed=1024, transcendentals=0),
         name="respond",
-    )(reflection, *pieces, *earlier)
-
-
-def half_kernel(masks, last, reflection_ref, own_ref, other_ref, *refs):
-    out, spectra = refs[-2:]
-    bands, _, rows, _ = reflection_ref.shape
-    _, _, _, focal, width = own_ref.shape
+    )(*kept, *pieces, *earlier)
+
+
+def half_kernel(masks, last, loads, own_ref, other_ref, *refs):
+    kept, (out, spectra) = refs[last : last + loads], refs[-2:]
+    share, _, rows, _ = kept[0].shape
+    _, bands, _, focal, width = own_ref.shape
     me = lax.axis_index("mat")
     for i in range(len(masks)):
         for core, pieces in enumerate((own_ref, other_ref)):
@@ -208,7 +212,7 @@
         for i, mask in enumerate(masks):
             start = pl.multiple_of((me ^ mask) // 2 * 2 * width, 2 * width)
             part = lax.dot_general(
-                reflection_ref[band, :, :, pl.ds(start, 2 * width)].reshape(2 * rows, 2 * width),
+                kept[band // share][band % share, :, :, pl.ds(start, 2 * width)].reshape(2 * rows, 2 * width),
                 spectra[i, band],
                 (((1,), (1,)), ((), ())),
                 preferred_element_type=jnp.float32,
@@ -222,9 +226,9 @@
             out[band] = total
 
 
-def respond_half(reflection, own, other, masks, before, earlier):
-    per_device, _, rows, sources = reflection.shape
-    focal, width = own.shape[3:]
+def respond_half(kept, own, other, masks, before, earlier):
+    _, _, rows, _ = kept[0].shape
+    _, per_device, _, focal, width = own.shape
     whole = pl.BlockSpec(memory_space=pltpu.VMEM)
     if before is None:
         shape = jax.ShapeDtypeStruct((per_device, 2 * rows, 2 * focal), jnp.float32)
@@ -233,15 +237,15 @@
         shape = jax.ShapeDtypeStruct((per_device, 2, focal, rows), jnp.bfloat16)
         given = [before]
     return pl.pallas_call(
-        functools.partial(half_kernel, masks, before is not None),
-        in_specs=[whole] * (3 + len(given)) + [pl.BlockSpec(memory_space=pl.ANY)] * len(earlier),
+        functools.partial(half_kernel, masks, before is not None, len(kept)),
+        in_specs=[whole] * (2 + len(given) + len(kept)) + [pl.BlockSpec(memory_space=pl.ANY)] * len(earlier),
         out_specs=whole,
         out_shape=shape,
         scratch_shapes=[pltpu.VMEM((len(masks), per_device, 2 * focal, 2 * width), jnp.bfloat16)],
         compiler_params=pltpu.CompilerParams(vmem_limit_bytes=R_VMEM),
         cost_estimate=pl.CostEstimate(flops=0, bytes_accessed=1024, transcendentals=0),
         name="respond_half",
-    )(reflection, own, other, *given, *earlier)
+    )(own, other, *given, *kept, *earlier)
 
 
 def spread_kernel(table_ref, out):
@@ -404,32 +408,36 @@
     parts = [forward(table, traces, i * focal, focal, per_device, freq_devices) for i in range(CHUNKS)]
     spectra = []
     inverse_spread = spread(table)
+    some = max(1, per_device // 2)
+    kept = []
     for i, part in enumerate(parts):
         arrived = [swap(part[mask], "freq", mask) for mask in range(1, freq_devices)]
-        spectra.append(add([part[0], *arrived], [later[0] for later in parts[i + 1 :]] or [inverse_spread]))
+        if spectra:
+            kept.append(load(reflection, 0, some, [spectra[0]]))
+        spectra.append(add([part[0], *arrived], [later[0] for later in parts[i + 1 :]] or [inverse_spread, *kept]))
     held, masks, tied = [], [0], []
     for block in spectra:
         for step in steps[:-1]:
             block = stack([block, swap(block, "mat", step)], tied or [spectra[-1]])
         if not tied:
-            tied = [load(reflection, [block])]
+            tied = [load(reflection, some, per_device - some, [spectra[-1]])]
         held.append((block, swap(block, "mat", steps[-1])))
     for step in steps[:-1]:
         masks = masks + [mask ^ step for mask in masks]
     masks = [masks, [mask ^ steps[-1] for mask in masks]]
     masks += [[mask ^ 1 for mask in some] for some in masks]
 
-    loaded = tied[0]
+    kept += tied
     responses = []
     for i, (block, other) in enumerate(held):
         beside = swap(block, "mat", 1)
         if responses:
-            half = respond_half(loaded, block, beside, masks[0], None, [responses[-1][0]])
+            half = respond_half(kept, block, beside, masks[0], None, [responses[-1][0]])
             other = stack([other], [half])
-            response = respond_half(loaded, other, swap(other, "mat", 1), masks[1], half, [])
+            response = respond_half(kept, other, swap(other, "mat", 1), masks[1], half, [])
         else:
             pieces = [block, other, beside, swap(other, "mat", 1)]
-            response = respond(loaded, pieces, masks, [later for later, _ in held[i + 1 :]])
+            response = respond(kept, pieces, masks, [later for later, _ in held[i + 1 :]])
         responses.append([response] + [swap(response, "freq", mask) for mask in range(1, freq_devices)])
     windowed = None
     for i, pieces in enumerate(responses):

time: 75.5 us -> 73.9 us (0.979)
  waiting for transfers between devices: 5.89 us -> 1.65 us
  starting transfers between devices: 23.5 us -> 24.9 us
  Pallas kernels: 45.4 us -> 46.5 us
    ppermute x20, waiting for transfers between devices: 5.89 us -> 1.65 us  [swap(): lax.ppermute(array, axis, [(i, i ^ mask) for i in range(lax.axis_size(axi...]
    ppermute x20, starting transfers between devices: 23.5 us -> 24.9 us  [swap(): lax.ppermute(array, axis, [(i, i ^ mask) for i in range(lax.axis_size(axi...]
    pallas_call x4 -> x5, Pallas kernels: 15.2 us -> 16.4 us  [the longest x2 6.97 us: load(): pl.pallas_call(functools.partial(load_kernel, first), in_specs=[pl.BlockS...]
  transfers between devices with their start and end apart: 20 -> 20, of which waited for: 6 -> 3; matrix products, arithmetic and copies ran while one was open for 0% -> 0% of each run, Pallas kernels for 40% -> 43%
where the time goes in v5:
time: 73.9 us; the launch traced here: 73.7 us
  Pallas kernels  46.5 us (63%)
  starting transfers between devices  24.9 us (34%)
  waiting for transfers between devices  1.65 us (2%)
    ppermute x20, starting transfers between devices, swap(): lax.ppermute(array, axis, [(i, i ^ mask) for i in range(lax.axis_size(axi...  24.9 us
    pallas_call x2, Pallas kernels, forward(): pl.pallas_call(functools.partial(forward_kernel, first, focal), in_specs=...  15.5 us
    pallas_call x2, Pallas kernels, invert(): pl.pallas_call(functools.partial(inverse_kernel, first, has_before), in_s...  13.7 us
    pallas_call x2, Pallas kernels, load(): pl.pallas_call(functools.partial(load_kernel, first), in_specs=[pl.BlockS...  6.97 us
    pallas_call x2, Pallas kernels, respond_half(): pl.pallas_call(functools.partial(half_kernel, masks, before is not None,...  4.79 us
    pallas_call x1, Pallas kernels, respond(): pl.pallas_call(functools.partial(response_kernel, masks, len(kept)), in_s...  4.63 us
    ppermute x20, waiting for transfers between devices, swap(): lax.ppermute(array, axis, [(i, i ^ mask) for i in range(lax.axis_size(axi...  1.65 us
  transfers between devices with their start and end apart: 20, of which 3 were waited for; matrix products, arithmetic and copies ran while one was open for 0% of the time, Pallas kernels for 43%

profile of v5, /device:TPU:0, one launch (start us, length us, event | category | flops | bytes accessed | tf_op | source)
XLA Modules:
  0.0 73.7 jit_solution(16873950323462534425)
XLA Ops:
  0.5 7.9 %forward.3 = (f32[2,2,32,512]{3,2,1,0:T(8,128)S(1)}, bf16[2,2,32,512]{3,2,1,0:T(8,128)(2,1)S(1)}, bf16[2,2,32,512]{3,2,1,0:T(8,128)(2,1)S(1)}, bf16[2,2,32,512]{3,2,1,0:T(8,128)(2,1)S(1)}) custom-call(bf16[2,16,512]{2,1,0:T(8,128)(2,1)S(1)} %constant_dynamic-update-slice_fusion.table_ref, bf16[512,64,512]{2,1,0:T(8,128)(2,1)} %traces_ref.3), custom_call_target="tpu_custom_call" | custom-call | flops 4294967296 | bytes 16777216 | tf_op jit(solution)/shard_map/forward/pallas_call | solution.py:116
  8.4 3.0 %collective-permute-start.3 = (bf16[2,2,32,512]{3,2,1,0:T(8,128)(2,1)S(1)}, bf16[2,2,32,512]{3,2,1,0:T(8,128)(2,1)S(1)}, u32[]{:S(2)}, u32[]{:S(2)}) collective-permute-start(bf16[2,2,32,512]{3,2,1,0:T(8,128)(2,1)S(1)} %get-tuple-element.18), channel_id=1, source_target_pairs={{0,8},{8,0},{16,24},{24,16},{1,9},{9,1},{17,25},{25,17},{2,10},{10... | collective-permute-start | bytes 393224 | tf_op jit(solution)/shard_map/ppermute | solution.py:396
  11.4 1.5 %collective-permute-start.4 = (bf16[2,2,32,512]{3,2,1,0:T(8,128)(2,1)S(1)}, bf16[2,2,32,512]{3,2,1,0:T(8,128)(2,1)S(1)}, u32[]{:S(2)}, u32[]{:S(2)}) collective-permute-start(bf16[2,2,32,512]{3,2,1,0:T(8,128)(2,1)S(1)} %get-tuple-element.19), channel_id=1, source_target_pairs={{0,16},{8,24},{16,0},{24,8},{1,17},{9,25},{17,1},{25,9},{2,18},{10... | collective-permute-start | bytes 393224 | tf_op jit(solution)/shard_map/ppermute | solution.py:396
  13.0 7.5 %forward.2 = (f32[2,2,32,512]{3,2,1,0:T(8,128)S(1)}, bf16[2,2,32,512]{3,2,1,0:T(8,128)(2,1)S(1)}, bf16[2,2,32,512]{3,2,1,0:T(8,128)(2,1)S(1)}, bf16[2,2,32,512]{3,2,1,0:T(8,128)(2,1)S(1)}) custom-call(bf16[2,16,512]{2,1,0:T(8,128)(2,1)S(1)} %constant_dynamic-update-slice_fusion.table_ref, bf16[512,64,512]{2,1,0:T(8,128)(2,1)} %traces_ref.3), custom_call_target="tpu_custom_call" | custom-call | flops 4294967296 | bytes 16777216 | tf_op jit(solution)/shard_map/forward/pallas_call | solution.py:116
  20.5 2.0 %collective-permute-start = (bf16[2,2,32,512]{3,2,1,0:T(8,128)(2,1)S(1)}, bf16[2,2,32,512]{3,2,1,0:T(8,128)(2,1)S(1)}, u32[]{:S(2)}, u32[]{:S(2)}) collective-permute-start(bf16[2,2,32,512]{3,2,1,0:T(8,128)(2,1)S(1)} %get-tuple-element.14), channel_id=1, source_target_pairs={{0,8},{8,0},{16,24},{24,16},{1,9},{9,1},{17,25},{25,17},{2,10},{10... | collective-permute-start | bytes 393224 | tf_op jit(solution)/shard_map/ppermute | solution.py:396
  22.5 1.5 %collective-permute-start.1 = (bf16[2,2,32,512]{3,2,1,0:T(8,128)(2,1)S(1)}, bf16[2,2,32,512]{3,2,1,0:T(8,128)(2,1)S(1)}, u32[]{:S(2)}, u32[]{:S(2)}) collective-permute-start(bf16[2,2,32,512]{3,2,1,0:T(8,128)(2,1)S(1)} %get-tuple-element.15), channel_id=1, source_target_pairs={{0,16},{8,24},{16,0},{24,8},{1,17},{9,25},{17,1},{25,9},{2,18},{10... | collective-permute-start | bytes 393224 | tf_op jit(solution)/shard_map/ppermute | solution.py:396
  24.1 3.1 %collective-permute-start.9 = (bf16[1,2,2,32,512]{4,3,2,1,0:T(8,128)(2,1)S(1)}, bf16[1,2,2,32,512]{4,3,2,1,0:T(8,128)(2,1)S(1)}, u32[]{:S(2)}, u32[]{:S(2)}) collective-permute-start(bf16[1,2,2,32,512]{4,3,2,1,0:T(8,128)(2,1)S(1)} %add.81.refs_0_), channel_id=1, source_target_pairs={{0,4},{1,5},{2,6},{3,7},{4,0},{5,1},{6,2},{7,3},{8,12},{9,13},{10,... | collective-permute-start | bytes 393224 | tf_op jit(solution)/shard_map/ppermute | solution.py:396
  27.2 0.8 %spread.1.refs_4_ = bf16[8192,256]{1,0:T(8,128)(2,1)S(1)} custom-call(bf16[2,16,512]{2,1,0:T(8,128)(2,1)S(1)} %constant_dynamic-update-slice_fusion.table_ref), custom_call_target="tpu_custom_call" | custom-call | bytes 4194304 | tf_op jit(solution)/shard_map/spread/pallas_call | solution.py:265
  28.0 3.5 %load.2.refs_5_.refs_0_.refs_1_ = bf16[1,2,512,4096]{3,2,1,0:T(8,128)(2,1)S(1)} custom-call(bf16[2,2,512,4096]{3,2,1,0:T(8,128)(2,1)} %reflection_ref.3, bf16[1,2,2,32,512]{4,3,2,1,0:T(8,128)(2,1)S(1)} %add.81.refs_0_), custom_call_target="tpu_custom_call" | custom-call | tf_op jit(solution)/shard_map/load/pallas_call | solution.py:153
  31.9 1.4 %collective-permute-start.10 = (bf16[2,2,2,32,512]{4,3,2,1,0:T(8,128)(2,1)S(1)}, bf16[2,2,2,32,512]{4,3,2,1,0:T(8,128)(2,1)S(1)}, u32[]{:S(2)}, u32[]{:S(2)}) collective-permute-start(bf16[2,2,2,32,512]{4,3,2,1,0:T(8,128)(2,1)S(1)} %stack.17.refs_2_), channel_id=1, source_target_pairs={{0,2},{1,3},{2,0},{3,1},{4,6},{5,7},{6,4},{7,5},{8,10},{9,11},{10,... | collective-permute-start | bytes 786440 | tf_op jit(solution)/shard_map/ppermute | solution.py:396
  33.3 2.8 %collective-permute-start.6 = (bf16[1,2,2,32,512]{4,3,2,1,0:T(8,128)(2,1)S(1)}, bf16[1,2,2,32,512]{4,3,2,1,0:T(8,128)(2,1)S(1)}, u32[]{:S(2)}, u32[]{:S(2)}) collective-permute-start(bf16[1,2,2,32,512]{4,3,2,1,0:T(8,128)(2,1)S(1)} %add.82.refs_0_.refs_2_), channel_id=1, source_target_pairs={{0,4},{1,5},{2,6},{3,7},{4,0},{5,1},{6,2},{7,3},{8,12},{9,13},{10,... | collective-permute-start | bytes 393224 | tf_op jit(solution)/shard_map/ppermute | solution.py:396
  36.1 3.5 %load.3.refs_2_.refs_1_ = bf16[1,2,512,4096]{3,2,1,0:T(8,128)(2,1)S(1)} custom-call(bf16[2,2,512,4096]{3,2,1,0:T(8,128)(2,1)} %reflection_ref.3, bf16[1,2,2,32,512]{4,3,2,1,0:T(8,128)(2,1)S(1)} %add.82.refs_0_.refs_2_), custom_call_target="tpu_custom_call" | custom-call | tf_op jit(solution)/shard_map/load/pallas_call | solution.py:153
  39.6 1.0 %collective-permute-done.10.refs_3_ = bf16[2,2,2,32,512]{4,3,2,1,0:T(8,128)(2,1)S(1)} collective-permute-done((bf16[2,2,2,32,512]{4,3,2,1,0:T(8,128)(2,1)S(1)}, bf16[2,2,2,32,512]{4,3,2,1,0:T(8,128)(2,1)S(1)}, u32[]{:S(2)}, u32[]{:S(2)}) %collective-permute-start.10) | collective-permute-done | bytes 262176 | tf_op jit(solution)/shard_map/ppermute | solution.py:396
  40.6 0.6 collective-permute-start.8
  41.2 1.6 %collective-permute-start.7 = (bf16[2,2,2,32,512]{4,3,2,1,0:T(8,128)(2,1)S(1)}, bf16[2,2,2,32,512]{4,3,2,1,0:T(8,128)(2,1)S(1)}, u32[]{:S(2)}, u32[]{:S(2)}) collective-permute-start(bf16[2,2,2,32,512]{4,3,2,1,0:T(8,128)(2,1)S(1)} %stack.16.refs_6_.own_ref), channel_id=1, source_target_pairs={{0,2},{1,3},{2,0},{3,1},{4,6},{5,7},{6,4},{7,5},{8,10},{9,11},{10,... | collective-permute-start | bytes 786440 | tf_op jit(solution)/shard_map/ppermute | solution.py:396
  42.8 4.6 %respond.1.refs_2_.refs_0_ = bf16[2,2,32,512]{3,2,1,0:T(8,128)(2,1)S(1)} custom-call(bf16[1,2,512,4096]{3,2,1,0:T(8,128)(2,1)S(1)} %load.2.refs_5_.refs_0_.refs_1_, bf16[1,2,512,4096]{3,2,1,0:T(8,128)(2,1)S(1)} %load.3.refs_2_.refs_1_, bf16[2,2,2,32,512]{4,3,2,1,0:T(8,128)(2,1)S(1)} %stack.17.refs_2_, ...), custom_call_target="tpu_custom_call" | custom-call | bytes 1024 | tf_op jit(solution)/shard_map/respond/pallas_call | solution.py:189
  47.5 2.4 %respond_half.2.refs_1_.refs_0_ = f32[2,1024,64]{2,1,0:T(8,128)S(1)} custom-call(bf16[2,2,2,32,512]{4,3,2,1,0:T(8,128)(2,1)S(1)} %stack.16.refs_6_.own_ref, bf16[2,2,2,32,512]{4,3,2,1,0:T(8,128)(2,1)S(1)} %collective-permute-done.8.other_ref, bf16[1,2,512,4096]{3,2,1,0:T(8,128)(2,1)S(1)} %load.2.refs_5_.refs_0_.refs_1_, ...), custom_call_target="tpu_custom_call" | custom-call | bytes 1024 | tf_op jit(solution)/shard_map/respond_half/pallas_call | solution.py:239
  50.1 2.1 %collective-permute-start.19 = (bf16[2,2,32,512]{3,2,1,0:T(8,128)(2,1)S(1)}, bf16[2,2,32,512]{3,2,1,0:T(8,128)(2,1)S(1)}, u32[]{:S(2)}, u32[]{:S(2)}) collective-permute-start(bf16[2,2,32,512]{3,2,1,0:T(8,128)(2,1)S(1)} %respond.1.refs_2_.refs_0_), channel_id=1, source_target_pairs={{0,24},{8,16},{16,8},{24,0},{1,25},{9,17},{17,9},{25,1},{2,26},{10... | collective-permute-start | bytes 393224 | tf_op jit(solution)/shard_map/ppermute | solution.py:396
  52.3 0.8 %collective-permute-start.18 = (bf16[2,2,32,512]{3,2,1,0:T(8,128)(2,1)S(1)}, bf16[2,2,32,512]{3,2,1,0:T(8,128)(2,1)S(1)}, u32[]{:S(2)}, u32[]{:S(2)}) collective-permute-start(bf16[2,2,32,512]{3,2,1,0:T(8,128)(2,1)S(1)} %respond.1.refs_2_.refs_0_), channel_id=1, source_target_pairs={{0,16},{8,24},{16,0},{24,8},{1,17},{9,25},{17,1},{25,9},{2,18},{10... | collective-permute-start | bytes 393224 | tf_op jit(solution)/shard_map/ppermute | solution.py:396
  53.6 2.4 %respond_half.3.refs_0_ = bf16[2,2,32,512]{3,2,1,0:T(8,128)(2,1)S(1)} custom-call(bf16[2,2,2,32,512]{4,3,2,1,0:T(8,128)(2,1)S(1)} %stack.18.own_ref, bf16[2,2,2,32,512]{4,3,2,1,0:T(8,128)(2,1)S(1)} %collective-permute-done.13.other_ref, f32[2,1024,64]{2,1,0:T(8,128)S(1)} %respond_half.2.refs_1_.refs_0_, ...), custom_call_target="tpu_custom_call" | custom-call | bytes 1024 | tf_op jit(solution)/shard_map/respond_half/pallas_call | solution.py:239
  56.0 2.2 %collective-permute-start.16 = (bf16[2,2,32,512]{3,2,1,0:T(8,128)(2,1)S(1)}, bf16[2,2,32,512]{3,2,1,0:T(8,128)(2,1)S(1)}, u32[]{:S(2)}, u32[]{:S(2)}) collective-permute-start(bf16[2,2,32,512]{3,2,1,0:T(8,128)(2,1)S(1)} %respond_half.3.refs_0_), channel_id=1, source_target_pairs={{0,24},{8,16},{16,8},{24,0},{1,25},{9,17},{17,9},{25,1},{2,26},{10... | collective-permute-start | bytes 393224 | tf_op jit(solution)/shard_map/ppermute | solution.py:396
  58.3 0.8 %collective-permute-start.15 = (bf16[2,2,32,512]{3,2,1,0:T(8,128)(2,1)S(1)}, bf16[2,2,32,512]{3,2,1,0:T(8,128)(2,1)S(1)}, u32[]{:S(2)}, u32[]{:S(2)}) collective-permute-start(bf16[2,2,32,512]{3,2,1,0:T(8,128)(2,1)S(1)} %respond_half.3.refs_0_), channel_id=1, source_target_pairs={{0,16},{8,24},{16,0},{24,8},{1,17},{9,25},{17,1},{25,9},{2,18},{10... | collective-permute-start | bytes 393224 | tf_op jit(solution)/shard_map/ppermute | solution.py:396
  60.0 6.8 %invert.2.refs_4_ = bf16[512,64,512]{2,1,0:T(8,128)(2,1)} custom-call(bf16[8192,256]{1,0:T(8,128)(2,1)S(1)} %spread.1.refs_4_, s32[64,512]{1,0:T(8,128)S(1)} %copy-done, bf16[2,2,32,512]{3,2,1,0:T(8,128)(2,1)S(1)} %respond.1.refs_2_.refs_0_, bf16[2,2,32,512]{3,2,1,0:T(8,128)(2,1)S(1)} %collective-permute-done.17.refs_1_, ...), custom_call_target="tpu_custom_call" | custom-call | flops 4294967296 | bytes 16777216 | tf_op jit(solution)/shard_map/invert/pallas_call | solution.py:334
  66.9 6.9 %invert.3 = bf16[512,64,512]{2,1,0:T(8,128)(2,1)} custom-call(bf16[8192,256]{1,0:T(8,128)(2,1)S(1)} %spread.1.refs_4_, s32[64,512]{1,0:T(8,128)S(1)} %copy-done, bf16[2,2,32,512]{3,2,1,0:T(8,128)(2,1)S(1)} %respond_half.3.refs_0_, bf16[2,2,32,512]{3,2,1,0:T(8,128)(2,1)S(1)} %collective-permute-done.14.refs_1_, ...), custom_call_target="tpu_custom_call", output_to_operand_aliasing={{}: (6, {})} | custom-call | flops 4294967296 | bytes 16777216 | tf_op jit(solution)/shard_map/invert/pallas_call | solution.py:334
  (45 shorter events, 2.7 us)
Async XLA Ops:
  8.4 15.6 %collective-permute-start.3 = (bf16[2,2,32,512]{3,2,1,0:T(8,128)(2,1)S(1)}, bf16[2,2,32,512]{3,2,1,0:T(8,128)(2,1)S(1)}, u32[]{:S(2)}, u32[]{:S(2)}) collective-permute-start(bf16[2,2,32,512]{3,2,1,0:T(8,128)(2,1)S(1)} %get-tuple-element.18), channel_id=1, source_target_pairs={{0,8},{8,0},{16,24},{24,16},{1,9},{9,1},{17,25},{25,17},{2,10},{10... | collective-permute-start | bytes 393224 | tf_op jit(solution)/shard_map/ppermute | solution.py:396
  11.4 12.7 %collective-permute-start.4 = (bf16[2,2,32,512]{3,2,1,0:T(8,128)(2,1)S(1)}, bf16[2,2,32,512]{3,2,1,0:T(8,128)(2,1)S(1)}, u32[]{:S(2)}, u32[]{:S(2)}) collective-permute-start(bf16[2,2,32,512]{3,2,1,0:T(8,128)(2,1)S(1)} %get-tuple-element.19), channel_id=1, source_target_pairs={{0,16},{8,24},{16,0},{24,8},{1,17},{9,25},{17,1},{25,9},{2,18},{10... | collective-permute-start | bytes 393224 | tf_op jit(solution)/shard_map/ppermute | solution.py:396
  12.9 11.1 %collective-permute-start.5 = (bf16[2,2,32,512]{3,2,1,0:T(8,128)(2,1)S(1)}, bf16[2,2,32,512]{3,2,1,0:T(8,128)(2,1)S(1)}, u32[]{:S(2)}, u32[]{:S(2)}) collective-permute-start(bf16[2,2,32,512]{3,2,1,0:T(8,128)(2,1)S(1)} %get-tuple-element.20), channel_id=1, source_target_pairs={{0,24},{8,16},{16,8},{24,0},{1,25},{9,17},{17,9},{25,1},{2,26},{10... | collective-permute-start | bytes 393224 | tf_op jit(solution)/shard_map/ppermute | solution.py:396
  20.5 11.0 %collective-permute-start = (bf16[2,2,32,512]{3,2,1,0:T(8,128)(2,1)S(1)}, bf16[2,2,32,512]{3,2,1,0:T(8,128)(2,1)S(1)}, u32[]{:S(2)}, u32[]{:S(2)}) collective-permute-start(bf16[2,2,32,512]{3,2,1,0:T(8,128)(2,1)S(1)} %get-tuple-element.14), channel_id=1, source_target_pairs={{0,8},{8,0},{16,24},{24,16},{1,9},{9,1},{17,25},{25,17},{2,10},{10... | collective-permute-start | bytes 393224 | tf_op jit(solution)/shard_map/ppermute | solution.py:396
  22.5 9.0 %collective-permute-start.1 = (bf16[2,2,32,512]{3,2,1,0:T(8,128)(2,1)S(1)}, bf16[2,2,32,512]{3,2,1,0:T(8,128)(2,1)S(1)}, u32[]{:S(2)}, u32[]{:S(2)}) collective-permute-start(bf16[2,2,32,512]{3,2,1,0:T(8,128)(2,1)S(1)} %get-tuple-element.15), channel_id=1, source_target_pairs={{0,16},{8,24},{16,0},{24,8},{1,17},{9,25},{17,1},{25,9},{2,18},{10... | collective-permute-start | bytes 393224 | tf_op jit(solution)/shard_map/ppermute | solution.py:396
  24.0 7.5 %collective-permute-start.2 = (bf16[2,2,32,512]{3,2,1,0:T(8,128)(2,1)S(1)}, bf16[2,2,32,512]{3,2,1,0:T(8,128)(2,1)S(1)}, u32[]{:S(2)}, u32[]{:S(2)}) collective-permute-start(bf16[2,2,32,512]{3,2,1,0:T(8,128)(2,1)S(1)} %get-tuple-element.16), channel_id=1, source_target_pairs={{0,24},{8,16},{16,8},{24,0},{1,25},{9,17},{17,9},{25,1},{2,26},{10... | collective-permute-start | bytes 393224 | tf_op jit(solution)/shard_map/ppermute | solution.py:396
  24.1 7.7 %collective-permute-start.9 = (bf16[1,2,2,32,512]{4,3,2,1,0:T(8,128)(2,1)S(1)}, bf16[1,2,2,32,512]{4,3,2,1,0:T(8,128)(2,1)S(1)}, u32[]{:S(2)}, u32[]{:S(2)}) collective-permute-start(bf16[1,2,2,32,512]{4,3,2,1,0:T(8,128)(2,1)S(1)} %add.81.refs_0_), channel_id=1, source_target_pairs={{0,4},{1,5},{2,6},{3,7},{4,0},{5,1},{6,2},{7,3},{8,12},{9,13},{10,... | collective-permute-start | bytes 393224 | tf_op jit(solution)/shard_map/ppermute | solution.py:396
  31.9 8.7 %collective-permute-start.10 = (bf16[2,2,2,32,512]{4,3,2,1,0:T(8,128)(2,1)S(1)}, bf16[2,2,2,32,512]{4,3,2,1,0:T(8,128)(2,1)S(1)}, u32[]{:S(2)}, u32[]{:S(2)}) collective-permute-start(bf16[2,2,2,32,512]{4,3,2,1,0:T(8,128)(2,1)S(1)} %stack.17.refs_2_), channel_id=1, source_target_pairs={{0,2},{1,3},{2,0},{3,1},{4,6},{5,7},{6,4},{7,5},{8,10},{9,11},{10,... | collective-permute-start | bytes 786440 | tf_op jit(solution)/shard_map/ppermute | solution.py:396
  33.3 7.3 %collective-permute-start.6 = (bf16[1,2,2,32,512]{4,3,2,1,0:T(8,128)(2,1)S(1)}, bf16[1,2,2,32,512]{4,3,2,1,0:T(8,128)(2,1)S(1)}, u32[]{:S(2)}, u32[]{:S(2)}) collective-permute-start(bf16[1,2,2,32,512]{4,3,2,1,0:T(8,128)(2,1)S(1)} %add.82.refs_0_.refs_2_), channel_id=1, source_target_pairs={{0,4},{1,5},{2,6},{3,7},{4,0},{5,1},{6,2},{7,3},{8,12},{9,13},{10,... | collective-permute-start | bytes 393224 | tf_op jit(solution)/shard_map/ppermute | solution.py:396
  39.5 3.3 %collective-permute-start.11 = (bf16[2,2,2,32,512]{4,3,2,1,0:T(8,128)(2,1)S(1)}, bf16[2,2,2,32,512]{4,3,2,1,0:T(8,128)(2,1)S(1)}, u32[]{:S(2)}, u32[]{:S(2)}) collective-permute-start(bf16[2,2,2,32,512]{4,3,2,1,0:T(8,128)(2,1)S(1)} %stack.17.refs_2_), channel_id=1, source_target_pairs={{0,1},{1,0},{2,3},{3,2},{4,5},{5,4},{6,7},{7,6},{8,9},{9,8},{10,11... | collective-permute-start | bytes 786440 | tf_op jit(solution)/shard_map/ppermute | solution.py:396
  40.6 2.2 %collective-permute-start.12 = (bf16[2,2,2,32,512]{4,3,2,1,0:T(8,128)(2,1)S(1)}, bf16[2,2,2,32,512]{4,3,2,1,0:T(8,128)(2,1)S(1)}, u32[]{:S(2)}, u32[]{:S(2)}) collective-permute-start(bf16[2,2,2,32,512]{4,3,2,1,0:T(8,128)(2,1)S(1)} %collective-permute-done.10.refs_3_), channel_id=1, source_target_pairs={{0,1},{1,0},{2,3},{3,2},{4,5},{5,4},{6,7},{7,6},{8,9},{9,8},{10,11... | collective-permute-start | bytes 786440 | tf_op jit(solution)/shard_map/ppermute | solution.py:396
  40.6 6.8 %collective-permute-start.8 = (bf16[2,2,2,32,512]{4,3,2,1,0:T(8,128)(2,1)S(1)}, bf16[2,2,2,32,512]{4,3,2,1,0:T(8,128)(2,1)S(1)}, u32[]{:S(2)}, u32[]{:S(2)}) collective-permute-start(bf16[2,2,2,32,512]{4,3,2,1,0:T(8,128)(2,1)S(1)} %stack.16.refs_6_.own_ref), channel_id=1, source_target_pairs={{0,1},{1,0},{2,3},{3,2},{4,5},{5,4},{6,7},{7,6},{8,9},{9,8},{10,11... | collective-permute-start | bytes 786440 | tf_op jit(solution)/shard_map/ppermute | solution.py:396
  41.2 8.6 %collective-permute-start.7 = (bf16[2,2,2,32,512]{4,3,2,1,0:T(8,128)(2,1)S(1)}, bf16[2,2,2,32,512]{4,3,2,1,0:T(8,128)(2,1)S(1)}, u32[]{:S(2)}, u32[]{:S(2)}) collective-permute-start(bf16[2,2,2,32,512]{4,3,2,1,0:T(8,128)(2,1)S(1)} %stack.16.refs_6_.own_ref), channel_id=1, source_target_pairs={{0,2},{1,3},{2,0},{3,1},{4,6},{5,7},{6,4},{7,5},{8,10},{9,11},{10,... | collective-permute-start | bytes 786440 | tf_op jit(solution)/shard_map/ppermute | solution.py:396
  47.4 12.5 %copy-start = (s32[64,512]{1,0:T(8,128)S(1)}, s32[64,512]{1,0:T(8,128)}, u32[]{:S(2)}) copy-start(s32[64,512]{1,0:T(8,128)} %onset_ref.3) | copy-start | bytes 393220
  49.9 3.7 %collective-permute-start.13 = (bf16[2,2,2,32,512]{4,3,2,1,0:T(8,128)(2,1)S(1)}, bf16[2,2,2,32,512]{4,3,2,1,0:T(8,128)(2,1)S(1)}, u32[]{:S(2)}, u32[]{:S(2)}) collective-permute-start(bf16[2,2,2,32,512]{4,3,2,1,0:T(8,128)(2,1)S(1)} %stack.18.own_ref), channel_id=1, source_target_pairs={{0,1},{1,0},{2,3},{3,2},{4,5},{5,4},{6,7},{7,6},{8,9},{9,8},{10,11... | collective-permute-start | bytes 786440 | tf_op jit(solution)/shard_map/ppermute | solution.py:396
  50.1 9.0 %collective-permute-start.19 = (bf16[2,2,32,512]{3,2,1,0:T(8,128)(2,1)S(1)}, bf16[2,2,32,512]{3,2,1,0:T(8,128)(2,1)S(1)}, u32[]{:S(2)}, u32[]{:S(2)}) collective-permute-start(bf16[2,2,32,512]{3,2,1,0:T(8,128)(2,1)S(1)} %respond.1.refs_2_.refs_0_), channel_id=1, source_target_pairs={{0,24},{8,16},{16,8},{24,0},{1,25},{9,17},{17,9},{25,1},{2,26},{10... | collective-permute-start | bytes 393224 | tf_op jit(solution)/shard_map/ppermute | solution.py:396
  52.3 7.7 %collective-permute-start.18 = (bf16[2,2,32,512]{3,2,1,0:T(8,128)(2,1)S(1)}, bf16[2,2,32,512]{3,2,1,0:T(8,128)(2,1)S(1)}, u32[]{:S(2)}, u32[]{:S(2)}) collective-permute-start(bf16[2,2,32,512]{3,2,1,0:T(8,128)(2,1)S(1)} %respond.1.refs_2_.refs_0_), channel_id=1, source_target_pairs={{0,16},{8,24},{16,0},{24,8},{1,17},{9,25},{17,1},{25,9},{2,18},{10... | collective-permute-start | bytes 393224 | tf_op jit(solution)/shard_map/ppermute | solution.py:396
  53.1 6.9 %collective-permute-start.17 = (bf16[2,2,32,512]{3,2,1,0:T(8,128)(2,1)S(1)}, bf16[2,2,32,512]{3,2,1,0:T(8,128)(2,1)S(1)}, u32[]{:S(2)}, u32[]{:S(2)}) collective-permute-start(bf16[2,2,32,512]{3,2,1,0:T(8,128)(2,1)S(1)} %respond.1.refs_2_.refs_0_), channel_id=1, source_target_pairs={{0,8},{8,0},{16,24},{24,16},{1,9},{9,1},{17,25},{25,17},{2,10},{10... | collective-permute-start | bytes 393224 | tf_op jit(solution)/shard_map/ppermute | solution.py:396
  56.0 10.8 %collective-permute-start.16 = (bf16[2,2,32,512]{3,2,1,0:T(8,128)(2,1)S(1)}, bf16[2,2,32,512]{3,2,1,0:T(8,128)(2,1)S(1)}, u32[]{:S(2)}, u32[]{:S(2)}) collective-permute-start(bf16[2,2,32,512]{3,2,1,0:T(8,128)(2,1)S(1)} %respond_half.3.refs_0_), channel_id=1, source_target_pairs={{0,24},{8,16},{16,8},{24,0},{1,25},{9,17},{17,9},{25,1},{2,26},{10... | collective-permute-start | bytes 393224 | tf_op jit(solution)/shard_map/ppermute | solution.py:396
  58.3 8.6 %collective-permute-start.15 = (bf16[2,2,32,512]{3,2,1,0:T(8,128)(2,1)S(1)}, bf16[2,2,32,512]{3,2,1,0:T(8,128)(2,1)S(1)}, u32[]{:S(2)}, u32[]{:S(2)}) collective-permute-start(bf16[2,2,32,512]{3,2,1,0:T(8,128)(2,1)S(1)} %respond_half.3.refs_0_), channel_id=1, source_target_pairs={{0,16},{8,24},{16,0},{24,8},{1,17},{9,25},{17,1},{25,9},{2,18},{10... | collective-permute-start | bytes 393224 | tf_op jit(solution)/shard_map/ppermute | solution.py:396
  59.1 7.8 %collective-permute-start.14 = (bf16[2,2,32,512]{3,2,1,0:T(8,128)(2,1)S(1)}, bf16[2,2,32,512]{3,2,1,0:T(8,128)(2,1)S(1)}, u32[]{:S(2)}, u32[]{:S(2)}) collective-permute-start(bf16[2,2,32,512]{3,2,1,0:T(8,128)(2,1)S(1)} %respond_half.3.refs_0_), channel_id=1, source_target_pairs={{0,8},{8,0},{16,24},{24,16},{1,9},{9,1},{17,25},{25,17},{2,10},{10... | collective-permute-start | bytes 393224 | tf_op jit(solution)/shard_map/ppermute | solution.py:396

commit v6 on v5

--- a/solution.py
+++ b/solution.py
@@ -12,9 +12,9 @@
 CHUNKS = 2
 F_TIMES = 256
 F_SLOTS = 3
-I_TIMES = 128
-I_SLOTS = 3
-I_CUTS = 4
+I_TIMES = 256
+I_SLOTS = 2
+I_CUTS = 8
 MIB = 1024 * 1024
 F_VMEM = 40 * MIB
 R_VMEM = 12 * MIB
@@ -60,14 +60,11 @@
     count = steps * (focal // rows)
 
     def fetch(i):
-        slot = lax.rem(i, depth)
-        source = traces_ref.at[
-            pl.ds(lax.rem(i, steps) * times, times), pl.ds(first + i // steps * rows, rows), :
-        ]
-        return pltpu.make_async_copy(source, slots.at[slot], sems.at[slot])
+        source = traces_ref.at[pl.ds(i % steps * times, times), pl.ds(first + i // steps * rows, rows), :]
+        return pltpu.make_async_copy(source, slots.at[i % depth], sems.at[i % depth])
 
     for i in range(min(depth - 1, count)):
-        fetch(jnp.int32(i)).start()
+        fetch(i).start()
 
     for step in range(steps):
 
@@ -77,33 +74,23 @@
         some = table_ref[0, :, pl.ds(step * times, times)]
         spread_rows(store, jnp.dot(some, repeats(times), preferred_element_type=jnp.float32))
 
-    @pl.loop(0, count)
-    def _(i):
-        step = lax.rem(i, steps)
-
-        @pl.when(i + depth - 1 < count)
-        def _():
+    for i in range(count):
+        if i + depth - 1 < count:
             fetch(i + depth - 1).start()
-
         fetch(i).wait()
-        block = slots[lax.rem(i, depth)].reshape(times * rows, width)
+        step = i % steps
+        block = slots[i % depth].reshape(times * rows, width)
         part = jnp.dot(spread[step], block, preferred_element_type=jnp.float32)
-
-        @pl.when(step == 0)
-        def _():
+        if step > 0:
+            part = total[...] + part
+        if step < steps - 1:
             total[...] = part
-
-        @pl.when(step > 0)
-        def _():
-            total[...] += part
-
-        @pl.when(step == steps - 1)
-        def _():
-            share = total.shape[0] // len(outs)
-            place = pl.ds(pl.multiple_of(i // steps * rows, rows), rows)
-            for j, out in enumerate(outs):
-                value = total[pl.ds(j * share, share), :].reshape(*out.shape[:2], rows, width)
-                out[:, :, place, :] = value.astype(out.dtype)
+            continue
+        share = total.shape[0] // len(outs)
+        place = pl.ds(i // steps * rows, rows)
+        for j, out in enumerate(outs):
+            value = part[j * share : (j + 1) * share].reshape(*out.shape[:2], rows, width)
+            out[:, :, place, :] = value.astype(out.dtype)
 
 
 def forward(table, traces, first, focal, per_device, freq_devices):
@@ -414,20 +401,20 @@
         arrived = [swap(part[mask], "freq", mask) for mask in range(1, freq_devices)]
         if spectra:
             kept.append(load(reflection, 0, some, [spectra[0]]))
-        spectra.append(add([part[0], *arrived], [later[0] for later in parts[i + 1 :]] or [inverse_spread, *kept]))
+        spectra.append(add([part[0], *arrived], [later[0] for later in parts[i + 1 :]] or kept))
     held, masks, tied = [], [0], []
     for block in spectra:
         for step in steps[:-1]:
             block = stack([block, swap(block, "mat", step)], tied or [spectra[-1]])
         if not tied:
-            tied = [load(reflection, some, per_device - some, [spectra[-1]])]
+            tied = [load(reflection, some, per_device - some, [spectra[-1]]), inverse_spread]
         held.append((block, swap(block, "mat", steps[-1])))
     for step in steps[:-1]:
         masks = masks + [mask ^ step for mask in masks]
     masks = [masks, [mask ^ steps[-1] for mask in masks]]
     masks += [[mask ^ 1 for mask in some] for some in masks]
 
-    kept += tied
+    kept += tied[:1]
     responses = []
     for i, (block, other) in enumerate(held):
         beside = swap(block, "mat", 1)

time: 73.9 us -> 72.6 us (0.982)
  Pallas kernels: 46.5 us -> 45.1 us
    pallas_call x2, Pallas kernels: 13.7 us -> 12.5 us  [invert(): pl.pallas_call(functools.partial(inverse_kernel, first, has_before), in_s...]
  transfers between devices with their start and end apart: 20 -> 20, of which waited for: 3 -> 2; matrix products, arithmetic and copies ran while one was open for 0% -> 0% of each run, Pallas kernels for 43% -> 43%
where the time goes in v6:
time: 72.6 us; the launch traced here: 72.4 us
  Pallas kernels  45.1 us (62%)
  starting transfers between devices  25.1 us (35%)
  waiting for transfers between devices  1.5 us (2%)
    ppermute x20, starting transfers between devices, swap(): lax.ppermute(array, axis, [(i, i ^ mask) for i in range(lax.axis_size(axi...  25.1 us
    pallas_call x2, Pallas kernels, forward(): pl.pallas_call(functools.partial(forward_kernel, first, focal), in_specs=...  15 us
    pallas_call x2, Pallas kernels, invert(): pl.pallas_call(functools.partial(inverse_kernel, first, has_before), in_s...  12.5 us
    pallas_call x2, Pallas kernels, load(): pl.pallas_call(functools.partial(load_kernel, first), in_specs=[pl.BlockS...  6.97 us
    pallas_call x1, Pallas kernels, respond(): pl.pallas_call(functools.partial(response_kernel, masks, len(kept)), in_s...  4.81 us
    pallas_call x2, Pallas kernels, respond_half(): pl.pallas_call(functools.partial(half_kernel, masks, before is not None,...  4.79 us
    ppermute x20, waiting for transfers between devices, swap(): lax.ppermute(array, axis, [(i, i ^ mask) for i in range(lax.axis_size(axi...  1.5 us
  transfers between devices with their start and end apart: 20, of which 2 were waited for; matrix products, arithmetic and copies ran while one was open for 0% of the time, Pallas kernels for 43%

profile of v6, /device:TPU:0, one launch (start us, length us, event | category | flops | bytes accessed | tf_op | source)
XLA Modules:
  0.0 72.4 jit_solution(13171545640092914974)
XLA Ops:
  0.5 7.6 %forward.3 = (f32[2,2,32,512]{3,2,1,0:T(8,128)S(1)}, bf16[2,2,32,512]{3,2,1,0:T(8,128)(2,1)S(1)}, bf16[2,2,32,512]{3,2,1,0:T(8,128)(2,1)S(1)}, bf16[2,2,32,512]{3,2,1,0:T(8,128)(2,1)S(1)}) custom-call(bf16[2,16,512]{2,1,0:T(8,128)(2,1)S(1)} %constant_dynamic-update-slice_fusion.table_ref, bf16[512,64,512]{2,1,0:T(8,128)(2,1)} %traces_ref.3), custom_call_target="tpu_custom_call" | custom-call | flops 4294967296 | bytes 16777216 | tf_op jit(solution)/shard_map/forward/pallas_call | solution.py:103
  8.1 3.0 %collective-permute-start.3 = (bf16[2,2,32,512]{3,2,1,0:T(8,128)(2,1)S(1)}, bf16[2,2,32,512]{3,2,1,0:T(8,128)(2,1)S(1)}, u32[]{:S(2)}, u32[]{:S(2)}) collective-permute-start(bf16[2,2,32,512]{3,2,1,0:T(8,128)(2,1)S(1)} %get-tuple-element.18), channel_id=1, source_target_pairs={{0,8},{8,0},{16,24},{24,16},{1,9},{9,1},{17,25},{25,17},{2,10},{10... | collective-permute-start | bytes 393224 | tf_op jit(solution)/shard_map/ppermute | solution.py:383
  11.1 1.5 %collective-permute-start.4 = (bf16[2,2,32,512]{3,2,1,0:T(8,128)(2,1)S(1)}, bf16[2,2,32,512]{3,2,1,0:T(8,128)(2,1)S(1)}, u32[]{:S(2)}, u32[]{:S(2)}) collective-permute-start(bf16[2,2,32,512]{3,2,1,0:T(8,128)(2,1)S(1)} %get-tuple-element.19), channel_id=1, source_target_pairs={{0,16},{8,24},{16,0},{24,8},{1,17},{9,25},{17,1},{25,9},{2,18},{10... | collective-permute-start | bytes 393224 | tf_op jit(solution)/shard_map/ppermute | solution.py:383
  12.6 7.4 %forward.2 = (f32[2,2,32,512]{3,2,1,0:T(8,128)S(1)}, bf16[2,2,32,512]{3,2,1,0:T(8,128)(2,1)S(1)}, bf16[2,2,32,512]{3,2,1,0:T(8,128)(2,1)S(1)}, bf16[2,2,32,512]{3,2,1,0:T(8,128)(2,1)S(1)}) custom-call(bf16[2,16,512]{2,1,0:T(8,128)(2,1)S(1)} %constant_dynamic-update-slice_fusion.table_ref, bf16[512,64,512]{2,1,0:T(8,128)(2,1)} %traces_ref.3), custom_call_target="tpu_custom_call" | custom-call | flops 4294967296 | bytes 16777216 | tf_op jit(solution)/shard_map/forward/pallas_call | solution.py:103
  20.0 2.0 %collective-permute-start = (bf16[2,2,32,512]{3,2,1,0:T(8,128)(2,1)S(1)}, bf16[2,2,32,512]{3,2,1,0:T(8,128)(2,1)S(1)}, u32[]{:S(2)}, u32[]{:S(2)}) collective-permute-start(bf16[2,2,32,512]{3,2,1,0:T(8,128)(2,1)S(1)} %get-tuple-element.14), channel_id=1, source_target_pairs={{0,8},{8,0},{16,24},{24,16},{1,9},{9,1},{17,25},{25,17},{2,10},{10... | collective-permute-start | bytes 393224 | tf_op jit(solution)/shard_map/ppermute | solution.py:383
  22.0 1.5 %collective-permute-start.1 = (bf16[2,2,32,512]{3,2,1,0:T(8,128)(2,1)S(1)}, bf16[2,2,32,512]{3,2,1,0:T(8,128)(2,1)S(1)}, u32[]{:S(2)}, u32[]{:S(2)}) collective-permute-start(bf16[2,2,32,512]{3,2,1,0:T(8,128)(2,1)S(1)} %get-tuple-element.15), channel_id=1, source_target_pairs={{0,16},{8,24},{16,0},{24,8},{1,17},{9,25},{17,1},{25,9},{2,18},{10... | collective-permute-start | bytes 393224 | tf_op jit(solution)/shard_map/ppermute | solution.py:383
  23.6 3.1 %collective-permute-start.9 = (bf16[1,2,2,32,512]{4,3,2,1,0:T(8,128)(2,1)S(1)}, bf16[1,2,2,32,512]{4,3,2,1,0:T(8,128)(2,1)S(1)}, u32[]{:S(2)}, u32[]{:S(2)}) collective-permute-start(bf16[1,2,2,32,512]{4,3,2,1,0:T(8,128)(2,1)S(1)} %add.81.refs_0_), channel_id=1, source_target_pairs={{0,4},{1,5},{2,6},{3,7},{4,0},{5,1},{6,2},{7,3},{8,12},{9,13},{10,... | collective-permute-start | bytes 393224 | tf_op jit(solution)/shard_map/ppermute | solution.py:383
  26.7 3.5 %load.2.refs_4_.refs_0_.refs_1_ = bf16[1,2,512,4096]{3,2,1,0:T(8,128)(2,1)S(1)} custom-call(bf16[2,2,512,4096]{3,2,1,0:T(8,128)(2,1)} %reflection_ref.3, bf16[1,2,2,32,512]{4,3,2,1,0:T(8,128)(2,1)S(1)} %add.81.refs_0_), custom_call_target="tpu_custom_call" | custom-call | tf_op jit(solution)/shard_map/load/pallas_call | solution.py:140
  30.3 1.0 %collective-permute-done.9.refs_1_ = bf16[1,2,2,32,512]{4,3,2,1,0:T(8,128)(2,1)S(1)} collective-permute-done((bf16[1,2,2,32,512]{4,3,2,1,0:T(8,128)(2,1)S(1)}, bf16[1,2,2,32,512]{4,3,2,1,0:T(8,128)(2,1)S(1)}, u32[]{:S(2)}, u32[]{:S(2)}) %collective-permute-start.9) | collective-permute-done | bytes 131104 | tf_op jit(solution)/shard_map/ppermute | solution.py:383
  31.4 0.8 %collective-permute-start.10 = (bf16[2,2,2,32,512]{4,3,2,1,0:T(8,128)(2,1)S(1)}, bf16[2,2,2,32,512]{4,3,2,1,0:T(8,128)(2,1)S(1)}, u32[]{:S(2)}, u32[]{:S(2)}) collective-permute-start(bf16[2,2,2,32,512]{4,3,2,1,0:T(8,128)(2,1)S(1)} %stack.17.refs_2_), channel_id=1, source_target_pairs={{0,2},{1,3},{2,0},{3,1},{4,6},{5,7},{6,4},{7,5},{8,10},{9,11},{10,... | collective-permute-start | bytes 786440 | tf_op jit(solution)/shard_map/ppermute | solution.py:383
  32.2 3.4 %collective-permute-start.6 = (bf16[1,2,2,32,512]{4,3,2,1,0:T(8,128)(2,1)S(1)}, bf16[1,2,2,32,512]{4,3,2,1,0:T(8,128)(2,1)S(1)}, u32[]{:S(2)}, u32[]{:S(2)}) collective-permute-start(bf16[1,2,2,32,512]{4,3,2,1,0:T(8,128)(2,1)S(1)} %add.82.refs_0_.refs_2_), channel_id=1, source_target_pairs={{0,4},{1,5},{2,6},{3,7},{4,0},{5,1},{6,2},{7,3},{8,12},{9,13},{10,... | collective-permute-start | bytes 393224 | tf_op jit(solution)/shard_map/ppermute | solution.py:383
  35.6 0.8 %spread.1.refs_3_ = bf16[8192,256]{1,0:T(8,128)(2,1)S(1)} custom-call(bf16[2,16,512]{2,1,0:T(8,128)(2,1)S(1)} %constant_dynamic-update-slice_fusion.table_ref), custom_call_target="tpu_custom_call" | custom-call | bytes 4194304 | tf_op jit(solution)/shard_map/spread/pallas_call | solution.py:252
  36.3 3.5 %load.3.refs_2_.refs_1_ = bf16[1,2,512,4096]{3,2,1,0:T(8,128)(2,1)S(1)} custom-call(bf16[2,2,512,4096]{3,2,1,0:T(8,128)(2,1)} %reflection_ref.3, bf16[1,2,2,32,512]{4,3,2,1,0:T(8,128)(2,1)S(1)} %add.82.refs_0_.refs_2_), custom_call_target="tpu_custom_call" | custom-call | tf_op jit(solution)/shard_map/load/pallas_call | solution.py:140
  40.6 1.7 %collective-permute-start.7 = (bf16[2,2,2,32,512]{4,3,2,1,0:T(8,128)(2,1)S(1)}, bf16[2,2,2,32,512]{4,3,2,1,0:T(8,128)(2,1)S(1)}, u32[]{:S(2)}, u32[]{:S(2)}) collective-permute-start(bf16[2,2,2,32,512]{4,3,2,1,0:T(8,128)(2,1)S(1)} %stack.16.refs_6_.own_ref), channel_id=1, source_target_pairs={{0,2},{1,3},{2,0},{3,1},{4,6},{5,7},{6,4},{7,5},{8,10},{9,11},{10,... | collective-permute-start | bytes 786440 | tf_op jit(solution)/shard_map/ppermute | solution.py:383
  42.3 4.8 %respond.1.refs_2_.refs_0_ = bf16[2,2,32,512]{3,2,1,0:T(8,128)(2,1)S(1)} custom-call(bf16[1,2,512,4096]{3,2,1,0:T(8,128)(2,1)S(1)} %load.2.refs_4_.refs_0_.refs_1_, bf16[1,2,512,4096]{3,2,1,0:T(8,128)(2,1)S(1)} %load.3.refs_2_.refs_1_, bf16[2,2,2,32,512]{4,3,2,1,0:T(8,128)(2,1)S(1)} %stack.17.refs_2_, ...), custom_call_target="tpu_custom_call" | custom-call | bytes 1024 | tf_op jit(solution)/shard_map/respond/pallas_call | solution.py:176
  47.2 2.4 %respond_half.2.refs_1_.refs_0_ = f32[2,1024,64]{2,1,0:T(8,128)S(1)} custom-call(bf16[2,2,2,32,512]{4,3,2,1,0:T(8,128)(2,1)S(1)} %stack.16.refs_6_.own_ref, bf16[2,2,2,32,512]{4,3,2,1,0:T(8,128)(2,1)S(1)} %collective-permute-done.8.other_ref, bf16[1,2,512,4096]{3,2,1,0:T(8,128)(2,1)S(1)} %load.2.refs_4_.refs_0_.refs_1_, ...), custom_call_target="tpu_custom_call" | custom-call | bytes 1024 | tf_op jit(solution)/shard_map/respond_half/pallas_call | solution.py:226
  49.8 2.2 %collective-permute-start.19 = (bf16[2,2,32,512]{3,2,1,0:T(8,128)(2,1)S(1)}, bf16[2,2,32,512]{3,2,1,0:T(8,128)(2,1)S(1)}, u32[]{:S(2)}, u32[]{:S(2)}) collective-permute-start(bf16[2,2,32,512]{3,2,1,0:T(8,128)(2,1)S(1)} %respond.1.refs_2_.refs_0_), channel_id=1, source_target_pairs={{0,24},{8,16},{16,8},{24,0},{1,25},{9,17},{17,9},{25,1},{2,26},{10... | collective-permute-start | bytes 393224 | tf_op jit(solution)/shard_map/ppermute | solution.py:383
  52.0 0.8 %collective-permute-start.18 = (bf16[2,2,32,512]{3,2,1,0:T(8,128)(2,1)S(1)}, bf16[2,2,32,512]{3,2,1,0:T(8,128)(2,1)S(1)}, u32[]{:S(2)}, u32[]{:S(2)}) collective-permute-start(bf16[2,2,32,512]{3,2,1,0:T(8,128)(2,1)S(1)} %respond.1.refs_2_.refs_0_), channel_id=1, source_target_pairs={{0,16},{8,24},{16,0},{24,8},{1,17},{9,25},{17,1},{25,9},{2,18},{10... | collective-permute-start | bytes 393224 | tf_op jit(solution)/shard_map/ppermute | solution.py:383
  52.7 0.5 collective-permute-start.17
  53.3 2.4 %respond_half.3.refs_0_ = bf16[2,2,32,512]{3,2,1,0:T(8,128)(2,1)S(1)} custom-call(bf16[2,2,2,32,512]{4,3,2,1,0:T(8,128)(2,1)S(1)} %stack.18.own_ref, bf16[2,2,2,32,512]{4,3,2,1,0:T(8,128)(2,1)S(1)} %collective-permute-done.13.other_ref, f32[2,1024,64]{2,1,0:T(8,128)S(1)} %respond_half.2.refs_1_.refs_0_, ...), custom_call_target="tpu_custom_call" | custom-call | bytes 1024 | tf_op jit(solution)/shard_map/respond_half/pallas_call | solution.py:226
  55.7 2.2 %collective-permute-start.16 = (bf16[2,2,32,512]{3,2,1,0:T(8,128)(2,1)S(1)}, bf16[2,2,32,512]{3,2,1,0:T(8,128)(2,1)S(1)}, u32[]{:S(2)}, u32[]{:S(2)}) collective-permute-start(bf16[2,2,32,512]{3,2,1,0:T(8,128)(2,1)S(1)} %respond_half.3.refs_0_), channel_id=1, source_target_pairs={{0,24},{8,16},{16,8},{24,0},{1,25},{9,17},{17,9},{25,1},{2,26},{10... | collective-permute-start | bytes 393224 | tf_op jit(solution)/shard_map/ppermute | solution.py:383
  58.0 0.8 %collective-permute-start.15 = (bf16[2,2,32,512]{3,2,1,0:T(8,128)(2,1)S(1)}, bf16[2,2,32,512]{3,2,1,0:T(8,128)(2,1)S(1)}, u32[]{:S(2)}, u32[]{:S(2)}) collective-permute-start(bf16[2,2,32,512]{3,2,1,0:T(8,128)(2,1)S(1)} %respond_half.3.refs_0_), channel_id=1, source_target_pairs={{0,16},{8,24},{16,0},{24,8},{1,17},{9,25},{17,1},{25,9},{2,18},{10... | collective-permute-start | bytes 393224 | tf_op jit(solution)/shard_map/ppermute | solution.py:383
  59.7 6.3 %invert.2.refs_4_ = bf16[512,64,512]{2,1,0:T(8,128)(2,1)} custom-call(bf16[8192,256]{1,0:T(8,128)(2,1)S(1)} %spread.1.refs_3_, s32[64,512]{1,0:T(8,128)S(1)} %copy-done, bf16[2,2,32,512]{3,2,1,0:T(8,128)(2,1)S(1)} %respond.1.refs_2_.refs_0_, bf16[2,2,32,512]{3,2,1,0:T(8,128)(2,1)S(1)} %collective-permute-done.17.refs_1_, ...), custom_call_target="tpu_custom_call" | custom-call | flops 4294967296 | bytes 16777216 | tf_op jit(solution)/shard_map/invert/pallas_call | solution.py:321
  66.0 6.3 %invert.3 = bf16[512,64,512]{2,1,0:T(8,128)(2,1)} custom-call(bf16[8192,256]{1,0:T(8,128)(2,1)S(1)} %spread.1.refs_3_, s32[64,512]{1,0:T(8,128)S(1)} %copy-done, bf16[2,2,32,512]{3,2,1,0:T(8,128)(2,1)S(1)} %respond_half.3.refs_0_, bf16[2,2,32,512]{3,2,1,0:T(8,128)(2,1)S(1)} %collective-permute-done.14.refs_1_, ...), custom_call_target="tpu_custom_call", output_to_operand_aliasing={{}: (6, {})} | custom-call | flops 4294967296 | bytes 16777216 | tf_op jit(solution)/shard_map/invert/pallas_call | solution.py:321
  (45 shorter events, 2.5 us)
Async XLA Ops:
  8.1 15.5 %collective-permute-start.3 = (bf16[2,2,32,512]{3,2,1,0:T(8,128)(2,1)S(1)}, bf16[2,2,32,512]{3,2,1,0:T(8,128)(2,1)S(1)}, u32[]{:S(2)}, u32[]{:S(2)}) collective-permute-start(bf16[2,2,32,512]{3,2,1,0:T(8,128)(2,1)S(1)} %get-tuple-element.18), channel_id=1, source_target_pairs={{0,8},{8,0},{16,24},{24,16},{1,9},{9,1},{17,25},{25,17},{2,10},{10... | collective-permute-start | bytes 393224 | tf_op jit(solution)/shard_map/ppermute | solution.py:383
  11.1 12.5 %collective-permute-start.4 = (bf16[2,2,32,512]{3,2,1,0:T(8,128)(2,1)S(1)}, bf16[2,2,32,512]{3,2,1,0:T(8,128)(2,1)S(1)}, u32[]{:S(2)}, u32[]{:S(2)}) collective-permute-start(bf16[2,2,32,512]{3,2,1,0:T(8,128)(2,1)S(1)} %get-tuple-element.19), channel_id=1, source_target_pairs={{0,16},{8,24},{16,0},{24,8},{1,17},{9,25},{17,1},{25,9},{2,18},{10... | collective-permute-start | bytes 393224 | tf_op jit(solution)/shard_map/ppermute | solution.py:383
  12.6 11.0 %collective-permute-start.5 = (bf16[2,2,32,512]{3,2,1,0:T(8,128)(2,1)S(1)}, bf16[2,2,32,512]{3,2,1,0:T(8,128)(2,1)S(1)}, u32[]{:S(2)}, u32[]{:S(2)}) collective-permute-start(bf16[2,2,32,512]{3,2,1,0:T(8,128)(2,1)S(1)} %get-tuple-element.20), channel_id=1, source_target_pairs={{0,24},{8,16},{16,8},{24,0},{1,25},{9,17},{17,9},{25,1},{2,26},{10... | collective-permute-start | bytes 393224 | tf_op jit(solution)/shard_map/ppermute | solution.py:383
  20.0 10.2 %collective-permute-start = (bf16[2,2,32,512]{3,2,1,0:T(8,128)(2,1)S(1)}, bf16[2,2,32,512]{3,2,1,0:T(8,128)(2,1)S(1)}, u32[]{:S(2)}, u32[]{:S(2)}) collective-permute-start(bf16[2,2,32,512]{3,2,1,0:T(8,128)(2,1)S(1)} %get-tuple-element.14), channel_id=1, source_target_pairs={{0,8},{8,0},{16,24},{24,16},{1,9},{9,1},{17,25},{25,17},{2,10},{10... | collective-permute-start | bytes 393224 | tf_op jit(solution)/shard_map/ppermute | solution.py:383
  22.0 8.2 %collective-permute-start.1 = (bf16[2,2,32,512]{3,2,1,0:T(8,128)(2,1)S(1)}, bf16[2,2,32,512]{3,2,1,0:T(8,128)(2,1)S(1)}, u32[]{:S(2)}, u32[]{:S(2)}) collective-permute-start(bf16[2,2,32,512]{3,2,1,0:T(8,128)(2,1)S(1)} %get-tuple-element.15), channel_id=1, source_target_pairs={{0,16},{8,24},{16,0},{24,8},{1,17},{9,25},{17,1},{25,9},{2,18},{10... | collective-permute-start | bytes 393224 | tf_op jit(solution)/shard_map/ppermute | solution.py:383
  23.5 6.7 %collective-permute-start.2 = (bf16[2,2,32,512]{3,2,1,0:T(8,128)(2,1)S(1)}, bf16[2,2,32,512]{3,2,1,0:T(8,128)(2,1)S(1)}, u32[]{:S(2)}, u32[]{:S(2)}) collective-permute-start(bf16[2,2,32,512]{3,2,1,0:T(8,128)(2,1)S(1)} %get-tuple-element.16), channel_id=1, source_target_pairs={{0,24},{8,16},{16,8},{24,0},{1,25},{9,17},{17,9},{25,1},{2,26},{10... | collective-permute-start | bytes 393224 | tf_op jit(solution)/shard_map/ppermute | solution.py:383
  23.6 7.7 %collective-permute-start.9 = (bf16[1,2,2,32,512]{4,3,2,1,0:T(8,128)(2,1)S(1)}, bf16[1,2,2,32,512]{4,3,2,1,0:T(8,128)(2,1)S(1)}, u32[]{:S(2)}, u32[]{:S(2)}) collective-permute-start(bf16[1,2,2,32,512]{4,3,2,1,0:T(8,128)(2,1)S(1)} %add.81.refs_0_), channel_id=1, source_target_pairs={{0,4},{1,5},{2,6},{3,7},{4,0},{5,1},{6,2},{7,3},{8,12},{9,13},{10,... | collective-permute-start | bytes 393224 | tf_op jit(solution)/shard_map/ppermute | solution.py:383
  31.4 8.6 %collective-permute-start.10 = (bf16[2,2,2,32,512]{4,3,2,1,0:T(8,128)(2,1)S(1)}, bf16[2,2,2,32,512]{4,3,2,1,0:T(8,128)(2,1)S(1)}, u32[]{:S(2)}, u32[]{:S(2)}) collective-permute-start(bf16[2,2,2,32,512]{4,3,2,1,0:T(8,128)(2,1)S(1)} %stack.17.refs_2_), channel_id=1, source_target_pairs={{0,2},{1,3},{2,0},{3,1},{4,6},{5,7},{6,4},{7,5},{8,10},{9,11},{10,... | collective-permute-start | bytes 786440 | tf_op jit(solution)/shard_map/ppermute | solution.py:383
  32.2 8.2 %collective-permute-start.6 = (bf16[1,2,2,32,512]{4,3,2,1,0:T(8,128)(2,1)S(1)}, bf16[1,2,2,32,512]{4,3,2,1,0:T(8,128)(2,1)S(1)}, u32[]{:S(2)}, u32[]{:S(2)}) collective-permute-start(bf16[1,2,2,32,512]{4,3,2,1,0:T(8,128)(2,1)S(1)} %add.82.refs_0_.refs_2_), channel_id=1, source_target_pairs={{0,4},{1,5},{2,6},{3,7},{4,0},{5,1},{6,2},{7,3},{8,12},{9,13},{10,... | collective-permute-start | bytes 393224 | tf_op jit(solution)/shard_map/ppermute | solution.py:383
  39.8 2.5 %collective-permute-start.11 = (bf16[2,2,2,32,512]{4,3,2,1,0:T(8,128)(2,1)S(1)}, bf16[2,2,2,32,512]{4,3,2,1,0:T(8,128)(2,1)S(1)}, u32[]{:S(2)}, u32[]{:S(2)}) collective-permute-start(bf16[2,2,2,32,512]{4,3,2,1,0:T(8,128)(2,1)S(1)} %stack.17.refs_2_), channel_id=1, source_target_pairs={{0,1},{1,0},{2,3},{3,2},{4,5},{5,4},{6,7},{7,6},{8,9},{9,8},{10,11... | collective-permute-start | bytes 786440 | tf_op jit(solution)/shard_map/ppermute | solution.py:383
  40.0 2.4 %collective-permute-start.12 = (bf16[2,2,2,32,512]{4,3,2,1,0:T(8,128)(2,1)S(1)}, bf16[2,2,2,32,512]{4,3,2,1,0:T(8,128)(2,1)S(1)}, u32[]{:S(2)}, u32[]{:S(2)}) collective-permute-start(bf16[2,2,2,32,512]{4,3,2,1,0:T(8,128)(2,1)S(1)} %collective-permute-done.10.refs_3_), channel_id=1, source_target_pairs={{0,1},{1,0},{2,3},{3,2},{4,5},{5,4},{6,7},{7,6},{8,9},{9,8},{10,11... | collective-permute-start | bytes 786440 | tf_op jit(solution)/shard_map/ppermute | solution.py:383
  40.4 6.7 %collective-permute-start.8 = (bf16[2,2,2,32,512]{4,3,2,1,0:T(8,128)(2,1)S(1)}, bf16[2,2,2,32,512]{4,3,2,1,0:T(8,128)(2,1)S(1)}, u32[]{:S(2)}, u32[]{:S(2)}) collective-permute-start(bf16[2,2,2,32,512]{4,3,2,1,0:T(8,128)(2,1)S(1)} %stack.16.refs_6_.own_ref), channel_id=1, source_target_pairs={{0,1},{1,0},{2,3},{3,2},{4,5},{5,4},{6,7},{7,6},{8,9},{9,8},{10,11... | collective-permute-start | bytes 786440 | tf_op jit(solution)/shard_map/ppermute | solution.py:383
  40.6 8.9 %collective-permute-start.7 = (bf16[2,2,2,32,512]{4,3,2,1,0:T(8,128)(2,1)S(1)}, bf16[2,2,2,32,512]{4,3,2,1,0:T(8,128)(2,1)S(1)}, u32[]{:S(2)}, u32[]{:S(2)}) collective-permute-start(bf16[2,2,2,32,512]{4,3,2,1,0:T(8,128)(2,1)S(1)} %stack.16.refs_6_.own_ref), channel_id=1, source_target_pairs={{0,2},{1,3},{2,0},{3,1},{4,6},{5,7},{6,4},{7,5},{8,10},{9,11},{10,... | collective-permute-start | bytes 786440 | tf_op jit(solution)/shard_map/ppermute | solution.py:383
  47.1 12.5 %copy-start = (s32[64,512]{1,0:T(8,128)S(1)}, s32[64,512]{1,0:T(8,128)}, u32[]{:S(2)}) copy-start(s32[64,512]{1,0:T(8,128)} %onset_ref.3) | copy-start | bytes 393220
  49.6 3.7 %collective-permute-start.13 = (bf16[2,2,2,32,512]{4,3,2,1,0:T(8,128)(2,1)S(1)}, bf16[2,2,2,32,512]{4,3,2,1,0:T(8,128)(2,1)S(1)}, u32[]{:S(2)}, u32[]{:S(2)}) collective-permute-start(bf16[2,2,2,32,512]{4,3,2,1,0:T(8,128)(2,1)S(1)} %stack.18.own_ref), channel_id=1, source_target_pairs={{0,1},{1,0},{2,3},{3,2},{4,5},{5,4},{6,7},{7,6},{8,9},{9,8},{10,11... | collective-permute-start | bytes 786440 | tf_op jit(solution)/shard_map/ppermute | solution.py:383
  49.8 9.0 %collective-permute-start.19 = (bf16[2,2,32,512]{3,2,1,0:T(8,128)(2,1)S(1)}, bf16[2,2,32,512]{3,2,1,0:T(8,128)(2,1)S(1)}, u32[]{:S(2)}, u32[]{:S(2)}) collective-permute-start(bf16[2,2,32,512]{3,2,1,0:T(8,128)(2,1)S(1)} %respond.1.refs_2_.refs_0_), channel_id=1, source_target_pairs={{0,24},{8,16},{16,8},{24,0},{1,25},{9,17},{17,9},{25,1},{2,26},{10... | collective-permute-start | bytes 393224 | tf_op jit(solution)/shard_map/ppermute | solution.py:383
  52.0 7.7 %collective-permute-start.18 = (bf16[2,2,32,512]{3,2,1,0:T(8,128)(2,1)S(1)}, bf16[2,2,32,512]{3,2,1,0:T(8,128)(2,1)S(1)}, u32[]{:S(2)}, u32[]{:S(2)}) collective-permute-start(bf16[2,2,32,512]{3,2,1,0:T(8,128)(2,1)S(1)} %respond.1.refs_2_.refs_0_), channel_id=1, source_target_pairs={{0,16},{8,24},{16,0},{24,8},{1,17},{9,25},{17,1},{25,9},{2,18},{10... | collective-permute-start | bytes 393224 | tf_op jit(solution)/shard_map/ppermute | solution.py:383
  52.7 6.9 %collective-permute-start.17 = (bf16[2,2,32,512]{3,2,1,0:T(8,128)(2,1)S(1)}, bf16[2,2,32,512]{3,2,1,0:T(8,128)(2,1)S(1)}, u32[]{:S(2)}, u32[]{:S(2)}) collective-permute-start(bf16[2,2,32,512]{3,2,1,0:T(8,128)(2,1)S(1)} %respond.1.refs_2_.refs_0_), channel_id=1, source_target_pairs={{0,8},{8,0},{16,24},{24,16},{1,9},{9,1},{17,25},{25,17},{2,10},{10... | collective-permute-start | bytes 393224 | tf_op jit(solution)/shard_map/ppermute | solution.py:383
  55.7 10.2 %collective-permute-start.16 = (bf16[2,2,32,512]{3,2,1,0:T(8,128)(2,1)S(1)}, bf16[2,2,32,512]{3,2,1,0:T(8,128)(2,1)S(1)}, u32[]{:S(2)}, u32[]{:S(2)}) collective-permute-start(bf16[2,2,32,512]{3,2,1,0:T(8,128)(2,1)S(1)} %respond_half.3.refs_0_), channel_id=1, source_target_pairs={{0,24},{8,16},{16,8},{24,0},{1,25},{9,17},{17,9},{25,1},{2,26},{10... | collective-permute-start | bytes 393224 | tf_op jit(solution)/shard_map/ppermute | solution.py:383
  58.0 8.0 %collective-permute-start.15 = (bf16[2,2,32,512]{3,2,1,0:T(8,128)(2,1)S(1)}, bf16[2,2,32,512]{3,2,1,0:T(8,128)(2,1)S(1)}, u32[]{:S(2)}, u32[]{:S(2)}) collective-permute-start(bf16[2,2,32,512]{3,2,1,0:T(8,128)(2,1)S(1)} %respond_half.3.refs_0_), channel_id=1, source_target_pairs={{0,16},{8,24},{16,0},{24,8},{1,17},{9,25},{17,1},{25,9},{2,18},{10... | collective-permute-start | bytes 393224 | tf_op jit(solution)/shard_map/ppermute | solution.py:383
  58.8 7.2 %collective-permute-start.14 = (bf16[2,2,32,512]{3,2,1,0:T(8,128)(2,1)S(1)}, bf16[2,2,32,512]{3,2,1,0:T(8,128)(2,1)S(1)}, u32[]{:S(2)}, u32[]{:S(2)}) collective-permute-start(bf16[2,2,32,512]{3,2,1,0:T(8,128)(2,1)S(1)} %respond_half.3.refs_0_), channel_id=1, source_target_pairs={{0,8},{8,0},{16,24},{24,16},{1,9},{9,1},{17,25},{25,17},{2,10},{10... | collective-permute-start | bytes 393224 | tf_op jit(solution)/shard_map/ppermute | solution.py:383

commit v7 on v6

--- a/solution.py
+++ b/solution.py
@@ -10,8 +10,8 @@
 
 ROWS = 16
 CHUNKS = 2
-F_TIMES = 256
-F_SLOTS = 3
+F_TIMES = 128
+F_SLOTS = 4
 I_TIMES = 256
 I_SLOTS = 2
 I_CUTS = 8

time: 72.6 us -> 71.5 us (0.985)
  Pallas kernels: 45.1 us -> 44 us
    pallas_call x2, Pallas kernels: 15 us -> 13.9 us  [forward(): pl.pallas_call(functools.partial(forward_kernel, first, focal), in_specs=...]
where the time goes in v7:
time: 71.5 us; the launch traced here: 71.4 us
  Pallas kernels  44 us (62%)
  starting transfers between devices  25.1 us (35%)
  waiting for transfers between devices  1.51 us (2%)
    ppermute x20, starting transfers between devices, swap(): lax.ppermute(array, axis, [(i, i ^ mask) for i in range(lax.axis_size(axi...  25.1 us
    pallas_call x2, Pallas kernels, forward(): pl.pallas_call(functools.partial(forward_kernel, first, focal), in_specs=...  13.9 us
    pallas_call x2, Pallas kernels, invert(): pl.pallas_call(functools.partial(inverse_kernel, first, has_before), in_s...  12.5 us
    pallas_call x2, Pallas kernels, load(): pl.pallas_call(functools.partial(load_kernel, first), in_specs=[pl.BlockS...  6.97 us
    pallas_call x2, Pallas kernels, respond_half(): pl.pallas_call(functools.partial(half_kernel, masks, before is not None,...  4.97 us
    pallas_call x1, Pallas kernels, respond(): pl.pallas_call(functools.partial(response_kernel, masks, len(kept)), in_s...  4.63 us
    ppermute x20, waiting for transfers between devices, swap(): lax.ppermute(array, axis, [(i, i ^ mask) for i in range(lax.axis_size(axi...  1.51 us
  transfers between devices with their start and end apart: 20, of which 2 were waited for; matrix products, arithmetic and copies ran while one was open for 0% of the time, Pallas kernels for 43%

profile of v7, /device:TPU:0, one launch (start us, length us, event | category | flops | bytes accessed | tf_op | source)
XLA Modules:
  0.0 71.4 jit_solution(7790988364430708941)
XLA Ops:
  0.5 7.0 %forward.3 = (f32[2,2,32,512]{3,2,1,0:T(8,128)S(1)}, bf16[2,2,32,512]{3,2,1,0:T(8,128)(2,1)S(1)}, bf16[2,2,32,512]{3,2,1,0:T(8,128)(2,1)S(1)}, bf16[2,2,32,512]{3,2,1,0:T(8,128)(2,1)S(1)}) custom-call(bf16[2,16,512]{2,1,0:T(8,128)(2,1)S(1)} %constant_dynamic-update-slice_fusion.table_ref, bf16[512,64,512]{2,1,0:T(8,128)(2,1)} %traces_ref.3), custom_call_target="tpu_custom_call" | custom-call | flops 4294967296 | bytes 16777216 | tf_op jit(solution)/shard_map/forward/pallas_call | solution.py:103
  7.5 3.0 %collective-permute-start.3 = (bf16[2,2,32,512]{3,2,1,0:T(8,128)(2,1)S(1)}, bf16[2,2,32,512]{3,2,1,0:T(8,128)(2,1)S(1)}, u32[]{:S(2)}, u32[]{:S(2)}) collective-permute-start(bf16[2,2,32,512]{3,2,1,0:T(8,128)(2,1)S(1)} %get-tuple-element.18), channel_id=1, source_target_pairs={{0,8},{8,0},{16,24},{24,16},{1,9},{9,1},{17,25},{25,17},{2,10},{10... | collective-permute-start | bytes 393224 | tf_op jit(solution)/shard_map/ppermute | solution.py:383
  10.5 1.5 %collective-permute-start.4 = (bf16[2,2,32,512]{3,2,1,0:T(8,128)(2,1)S(1)}, bf16[2,2,32,512]{3,2,1,0:T(8,128)(2,1)S(1)}, u32[]{:S(2)}, u32[]{:S(2)}) collective-permute-start(bf16[2,2,32,512]{3,2,1,0:T(8,128)(2,1)S(1)} %get-tuple-element.19), channel_id=1, source_target_pairs={{0,16},{8,24},{16,0},{24,8},{1,17},{9,25},{17,1},{25,9},{2,18},{10... | collective-permute-start | bytes 393224 | tf_op jit(solution)/shard_map/ppermute | solution.py:383
  12.0 6.9 %forward.2 = (f32[2,2,32,512]{3,2,1,0:T(8,128)S(1)}, bf16[2,2,32,512]{3,2,1,0:T(8,128)(2,1)S(1)}, bf16[2,2,32,512]{3,2,1,0:T(8,128)(2,1)S(1)}, bf16[2,2,32,512]{3,2,1,0:T(8,128)(2,1)S(1)}) custom-call(bf16[2,16,512]{2,1,0:T(8,128)(2,1)S(1)} %constant_dynamic-update-slice_fusion.table_ref, bf16[512,64,512]{2,1,0:T(8,128)(2,1)} %traces_ref.3), custom_call_target="tpu_custom_call" | custom-call | flops 4294967296 | bytes 16777216 | tf_op jit(solution)/shard_map/forward/pallas_call | solution.py:103
  18.9 2.0 %collective-permute-start = (bf16[2,2,32,512]{3,2,1,0:T(8,128)(2,1)S(1)}, bf16[2,2,32,512]{3,2,1,0:T(8,128)(2,1)S(1)}, u32[]{:S(2)}, u32[]{:S(2)}) collective-permute-start(bf16[2,2,32,512]{3,2,1,0:T(8,128)(2,1)S(1)} %get-tuple-element.14), channel_id=1, source_target_pairs={{0,8},{8,0},{16,24},{24,16},{1,9},{9,1},{17,25},{25,17},{2,10},{10... | collective-permute-start | bytes 393224 | tf_op jit(solution)/shard_map/ppermute | solution.py:383
  21.0 1.5 %collective-permute-start.1 = (bf16[2,2,32,512]{3,2,1,0:T(8,128)(2,1)S(1)}, bf16[2,2,32,512]{3,2,1,0:T(8,128)(2,1)S(1)}, u32[]{:S(2)}, u32[]{:S(2)}) collective-permute-start(bf16[2,2,32,512]{3,2,1,0:T(8,128)(2,1)S(1)} %get-tuple-element.15), channel_id=1, source_target_pairs={{0,16},{8,24},{16,0},{24,8},{1,17},{9,25},{17,1},{25,9},{2,18},{10... | collective-permute-start | bytes 393224 | tf_op jit(solution)/shard_map/ppermute | solution.py:383
  22.6 3.1 %collective-permute-start.9 = (bf16[1,2,2,32,512]{4,3,2,1,0:T(8,128)(2,1)S(1)}, bf16[1,2,2,32,512]{4,3,2,1,0:T(8,128)(2,1)S(1)}, u32[]{:S(2)}, u32[]{:S(2)}) collective-permute-start(bf16[1,2,2,32,512]{4,3,2,1,0:T(8,128)(2,1)S(1)} %add.81.refs_0_), channel_id=1, source_target_pairs={{0,4},{1,5},{2,6},{3,7},{4,0},{5,1},{6,2},{7,3},{8,12},{9,13},{10,... | collective-permute-start | bytes 393224 | tf_op jit(solution)/shard_map/ppermute | solution.py:383
  25.7 3.5 %load.2.refs_4_.refs_0_.refs_1_ = bf16[1,2,512,4096]{3,2,1,0:T(8,128)(2,1)S(1)} custom-call(bf16[2,2,512,4096]{3,2,1,0:T(8,128)(2,1)} %reflection_ref.3, bf16[1,2,2,32,512]{4,3,2,1,0:T(8,128)(2,1)S(1)} %add.81.refs_0_), custom_call_target="tpu_custom_call" | custom-call | tf_op jit(solution)/shard_map/load/pallas_call | solution.py:140
  29.3 1.0 %collective-permute-done.9.refs_1_ = bf16[1,2,2,32,512]{4,3,2,1,0:T(8,128)(2,1)S(1)} collective-permute-done((bf16[1,2,2,32,512]{4,3,2,1,0:T(8,128)(2,1)S(1)}, bf16[1,2,2,32,512]{4,3,2,1,0:T(8,128)(2,1)S(1)}, u32[]{:S(2)}, u32[]{:S(2)}) %collective-permute-start.9) | collective-permute-done | bytes 131104 | tf_op jit(solution)/shard_map/ppermute | solution.py:383
  30.3 0.8 %collective-permute-start.10 = (bf16[2,2,2,32,512]{4,3,2,1,0:T(8,128)(2,1)S(1)}, bf16[2,2,2,32,512]{4,3,2,1,0:T(8,128)(2,1)S(1)}, u32[]{:S(2)}, u32[]{:S(2)}) collective-permute-start(bf16[2,2,2,32,512]{4,3,2,1,0:T(8,128)(2,1)S(1)} %stack.17.refs_2_), channel_id=1, source_target_pairs={{0,2},{1,3},{2,0},{3,1},{4,6},{5,7},{6,4},{7,5},{8,10},{9,11},{10,... | collective-permute-start | bytes 786440 | tf_op jit(solution)/shard_map/ppermute | solution.py:383
  31.1 3.4 %collective-permute-start.6 = (bf16[1,2,2,32,512]{4,3,2,1,0:T(8,128)(2,1)S(1)}, bf16[1,2,2,32,512]{4,3,2,1,0:T(8,128)(2,1)S(1)}, u32[]{:S(2)}, u32[]{:S(2)}) collective-permute-start(bf16[1,2,2,32,512]{4,3,2,1,0:T(8,128)(2,1)S(1)} %add.82.refs_0_.refs_2_), channel_id=1, source_target_pairs={{0,4},{1,5},{2,6},{3,7},{4,0},{5,1},{6,2},{7,3},{8,12},{9,13},{10,... | collective-permute-start | bytes 393224 | tf_op jit(solution)/shard_map/ppermute | solution.py:383
  34.5 0.8 %spread.1.refs_3_ = bf16[8192,256]{1,0:T(8,128)(2,1)S(1)} custom-call(bf16[2,16,512]{2,1,0:T(8,128)(2,1)S(1)} %constant_dynamic-update-slice_fusion.table_ref), custom_call_target="tpu_custom_call" | custom-call | bytes 4194304 | tf_op jit(solution)/shard_map/spread/pallas_call | solution.py:252
  35.3 3.5 %load.3.refs_2_.refs_1_ = bf16[1,2,512,4096]{3,2,1,0:T(8,128)(2,1)S(1)} custom-call(bf16[2,2,512,4096]{3,2,1,0:T(8,128)(2,1)} %reflection_ref.3, bf16[1,2,2,32,512]{4,3,2,1,0:T(8,128)(2,1)S(1)} %add.82.refs_0_.refs_2_), custom_call_target="tpu_custom_call" | custom-call | tf_op jit(solution)/shard_map/load/pallas_call | solution.py:140
  39.5 1.7 %collective-permute-start.7 = (bf16[2,2,2,32,512]{4,3,2,1,0:T(8,128)(2,1)S(1)}, bf16[2,2,2,32,512]{4,3,2,1,0:T(8,128)(2,1)S(1)}, u32[]{:S(2)}, u32[]{:S(2)}) collective-permute-start(bf16[2,2,2,32,512]{4,3,2,1,0:T(8,128)(2,1)S(1)} %stack.16.refs_6_.own_ref), channel_id=1, source_target_pairs={{0,2},{1,3},{2,0},{3,1},{4,6},{5,7},{6,4},{7,5},{8,10},{9,11},{10,... | collective-permute-start | bytes 786440 | tf_op jit(solution)/shard_map/ppermute | solution.py:383
  41.3 4.6 %respond.1.refs_2_.refs_0_ = bf16[2,2,32,512]{3,2,1,0:T(8,128)(2,1)S(1)} custom-call(bf16[1,2,512,4096]{3,2,1,0:T(8,128)(2,1)S(1)} %load.2.refs_4_.refs_0_.refs_1_, bf16[1,2,512,4096]{3,2,1,0:T(8,128)(2,1)S(1)} %load.3.refs_2_.refs_1_, bf16[2,2,2,32,512]{4,3,2,1,0:T(8,128)(2,1)S(1)} %stack.17.refs_2_, ...), custom_call_target="tpu_custom_call" | custom-call | bytes 1024 | tf_op jit(solution)/shard_map/respond/pallas_call | solution.py:176
  45.9 2.5 %respond_half.2.refs_1_.refs_0_ = f32[2,1024,64]{2,1,0:T(8,128)S(1)} custom-call(bf16[2,2,2,32,512]{4,3,2,1,0:T(8,128)(2,1)S(1)} %stack.16.refs_6_.own_ref, bf16[2,2,2,32,512]{4,3,2,1,0:T(8,128)(2,1)S(1)} %collective-permute-done.8.other_ref, bf16[1,2,512,4096]{3,2,1,0:T(8,128)(2,1)S(1)} %load.2.refs_4_.refs_0_.refs_1_, ...), custom_call_target="tpu_custom_call" | custom-call | bytes 1024 | tf_op jit(solution)/shard_map/respond_half/pallas_call | solution.py:226
  48.7 2.2 %collective-permute-start.19 = (bf16[2,2,32,512]{3,2,1,0:T(8,128)(2,1)S(1)}, bf16[2,2,32,512]{3,2,1,0:T(8,128)(2,1)S(1)}, u32[]{:S(2)}, u32[]{:S(2)}) collective-permute-start(bf16[2,2,32,512]{3,2,1,0:T(8,128)(2,1)S(1)} %respond.1.refs_2_.refs_0_), channel_id=1, source_target_pairs={{0,24},{8,16},{16,8},{24,0},{1,25},{9,17},{17,9},{25,1},{2,26},{10... | collective-permute-start | bytes 393224 | tf_op jit(solution)/shard_map/ppermute | solution.py:383
  50.9 0.8 %collective-permute-start.18 = (bf16[2,2,32,512]{3,2,1,0:T(8,128)(2,1)S(1)}, bf16[2,2,32,512]{3,2,1,0:T(8,128)(2,1)S(1)}, u32[]{:S(2)}, u32[]{:S(2)}) collective-permute-start(bf16[2,2,32,512]{3,2,1,0:T(8,128)(2,1)S(1)} %respond.1.refs_2_.refs_0_), channel_id=1, source_target_pairs={{0,16},{8,24},{16,0},{24,8},{1,17},{9,25},{17,1},{25,9},{2,18},{10... | collective-permute-start | bytes 393224 | tf_op jit(solution)/shard_map/ppermute | solution.py:383
  52.2 2.4 %respond_half.3.refs_0_ = bf16[2,2,32,512]{3,2,1,0:T(8,128)(2,1)S(1)} custom-call(bf16[2,2,2,32,512]{4,3,2,1,0:T(8,128)(2,1)S(1)} %stack.18.own_ref, bf16[2,2,2,32,512]{4,3,2,1,0:T(8,128)(2,1)S(1)} %collective-permute-done.13.other_ref, f32[2,1024,64]{2,1,0:T(8,128)S(1)} %respond_half.2.refs_1_.refs_0_, ...), custom_call_target="tpu_custom_call" | custom-call | bytes 1024 | tf_op jit(solution)/shard_map/respond_half/pallas_call | solution.py:226
  54.7 2.2 %collective-permute-start.16 = (bf16[2,2,32,512]{3,2,1,0:T(8,128)(2,1)S(1)}, bf16[2,2,32,512]{3,2,1,0:T(8,128)(2,1)S(1)}, u32[]{:S(2)}, u32[]{:S(2)}) collective-permute-start(bf16[2,2,32,512]{3,2,1,0:T(8,128)(2,1)S(1)} %respond_half.3.refs_0_), channel_id=1, source_target_pairs={{0,24},{8,16},{16,8},{24,0},{1,25},{9,17},{17,9},{25,1},{2,26},{10... | collective-permute-start | bytes 393224 | tf_op jit(solution)/shard_map/ppermute | solution.py:383
  56.9 0.8 %collective-permute-start.15 = (bf16[2,2,32,512]{3,2,1,0:T(8,128)(2,1)S(1)}, bf16[2,2,32,512]{3,2,1,0:T(8,128)(2,1)S(1)}, u32[]{:S(2)}, u32[]{:S(2)}) collective-permute-start(bf16[2,2,32,512]{3,2,1,0:T(8,128)(2,1)S(1)} %respond_half.3.refs_0_), channel_id=1, source_target_pairs={{0,16},{8,24},{16,0},{24,8},{1,17},{9,25},{17,1},{25,9},{2,18},{10... | collective-permute-start | bytes 393224 | tf_op jit(solution)/shard_map/ppermute | solution.py:383
  57.7 0.5 collective-permute-start.14
  58.6 6.3 %invert.2.refs_4_ = bf16[512,64,512]{2,1,0:T(8,128)(2,1)} custom-call(bf16[8192,256]{1,0:T(8,128)(2,1)S(1)} %spread.1.refs_3_, s32[64,512]{1,0:T(8,128)S(1)} %copy-done, bf16[2,2,32,512]{3,2,1,0:T(8,128)(2,1)S(1)} %respond.1.refs_2_.refs_0_, bf16[2,2,32,512]{3,2,1,0:T(8,128)(2,1)S(1)} %collective-permute-done.17.refs_1_, ...), custom_call_target="tpu_custom_call" | custom-call | flops 4294967296 | bytes 16777216 | tf_op jit(solution)/shard_map/invert/pallas_call | solution.py:321
  64.9 6.3 %invert.3 = bf16[512,64,512]{2,1,0:T(8,128)(2,1)} custom-call(bf16[8192,256]{1,0:T(8,128)(2,1)S(1)} %spread.1.refs_3_, s32[64,512]{1,0:T(8,128)S(1)} %copy-done, bf16[2,2,32,512]{3,2,1,0:T(8,128)(2,1)S(1)} %respond_half.3.refs_0_, bf16[2,2,32,512]{3,2,1,0:T(8,128)(2,1)S(1)} %collective-permute-done.14.refs_1_, ...), custom_call_target="tpu_custom_call", output_to_operand_aliasing={{}: (6, {})} | custom-call | flops 4294967296 | bytes 16777216 | tf_op jit(solution)/shard_map/invert/pallas_call | solution.py:321
  (45 shorter events, 2.5 us)
Async XLA Ops:
  7.5 15.0 %collective-permute-start.3 = (bf16[2,2,32,512]{3,2,1,0:T(8,128)(2,1)S(1)}, bf16[2,2,32,512]{3,2,1,0:T(8,128)(2,1)S(1)}, u32[]{:S(2)}, u32[]{:S(2)}) collective-permute-start(bf16[2,2,32,512]{3,2,1,0:T(8,128)(2,1)S(1)} %get-tuple-element.18), channel_id=1, source_target_pairs={{0,8},{8,0},{16,24},{24,16},{1,9},{9,1},{17,25},{25,17},{2,10},{10... | collective-permute-start | bytes 393224 | tf_op jit(solution)/shard_map/ppermute | solution.py:383
  10.5 12.0 %collective-permute-start.4 = (bf16[2,2,32,512]{3,2,1,0:T(8,128)(2,1)S(1)}, bf16[2,2,32,512]{3,2,1,0:T(8,128)(2,1)S(1)}, u32[]{:S(2)}, u32[]{:S(2)}) collective-permute-start(bf16[2,2,32,512]{3,2,1,0:T(8,128)(2,1)S(1)} %get-tuple-element.19), channel_id=1, source_target_pairs={{0,16},{8,24},{16,0},{24,8},{1,17},{9,25},{17,1},{25,9},{2,18},{10... | collective-permute-start | bytes 393224 | tf_op jit(solution)/shard_map/ppermute | solution.py:383
  12.0 10.5 %collective-permute-start.5 = (bf16[2,2,32,512]{3,2,1,0:T(8,128)(2,1)S(1)}, bf16[2,2,32,512]{3,2,1,0:T(8,128)(2,1)S(1)}, u32[]{:S(2)}, u32[]{:S(2)}) collective-permute-start(bf16[2,2,32,512]{3,2,1,0:T(8,128)(2,1)S(1)} %get-tuple-element.20), channel_id=1, source_target_pairs={{0,24},{8,16},{16,8},{24,0},{1,25},{9,17},{17,9},{25,1},{2,26},{10... | collective-permute-start | bytes 393224 | tf_op jit(solution)/shard_map/ppermute | solution.py:383
  18.9 10.2 %collective-permute-start = (bf16[2,2,32,512]{3,2,1,0:T(8,128)(2,1)S(1)}, bf16[2,2,32,512]{3,2,1,0:T(8,128)(2,1)S(1)}, u32[]{:S(2)}, u32[]{:S(2)}) collective-permute-start(bf16[2,2,32,512]{3,2,1,0:T(8,128)(2,1)S(1)} %get-tuple-element.14), channel_id=1, source_target_pairs={{0,8},{8,0},{16,24},{24,16},{1,9},{9,1},{17,25},{25,17},{2,10},{10... | collective-permute-start | bytes 393224 | tf_op jit(solution)/shard_map/ppermute | solution.py:383
  21.0 8.2 %collective-permute-start.1 = (bf16[2,2,32,512]{3,2,1,0:T(8,128)(2,1)S(1)}, bf16[2,2,32,512]{3,2,1,0:T(8,128)(2,1)S(1)}, u32[]{:S(2)}, u32[]{:S(2)}) collective-permute-start(bf16[2,2,32,512]{3,2,1,0:T(8,128)(2,1)S(1)} %get-tuple-element.15), channel_id=1, source_target_pairs={{0,16},{8,24},{16,0},{24,8},{1,17},{9,25},{17,1},{25,9},{2,18},{10... | collective-permute-start | bytes 393224 | tf_op jit(solution)/shard_map/ppermute | solution.py:383
  22.5 6.7 %collective-permute-start.2 = (bf16[2,2,32,512]{3,2,1,0:T(8,128)(2,1)S(1)}, bf16[2,2,32,512]{3,2,1,0:T(8,128)(2,1)S(1)}, u32[]{:S(2)}, u32[]{:S(2)}) collective-permute-start(bf16[2,2,32,512]{3,2,1,0:T(8,128)(2,1)S(1)} %get-tuple-element.16), channel_id=1, source_target_pairs={{0,24},{8,16},{16,8},{24,0},{1,25},{9,17},{17,9},{25,1},{2,26},{10... | collective-permute-start | bytes 393224 | tf_op jit(solution)/shard_map/ppermute | solution.py:383
  22.6 7.7 %collective-permute-start.9 = (bf16[1,2,2,32,512]{4,3,2,1,0:T(8,128)(2,1)S(1)}, bf16[1,2,2,32,512]{4,3,2,1,0:T(8,128)(2,1)S(1)}, u32[]{:S(2)}, u32[]{:S(2)}) collective-permute-start(bf16[1,2,2,32,512]{4,3,2,1,0:T(8,128)(2,1)S(1)} %add.81.refs_0_), channel_id=1, source_target_pairs={{0,4},{1,5},{2,6},{3,7},{4,0},{5,1},{6,2},{7,3},{8,12},{9,13},{10,... | collective-permute-start | bytes 393224 | tf_op jit(solution)/shard_map/ppermute | solution.py:383
  30.3 8.6 %collective-permute-start.10 = (bf16[2,2,2,32,512]{4,3,2,1,0:T(8,128)(2,1)S(1)}, bf16[2,2,2,32,512]{4,3,2,1,0:T(8,128)(2,1)S(1)}, u32[]{:S(2)}, u32[]{:S(2)}) collective-permute-start(bf16[2,2,2,32,512]{4,3,2,1,0:T(8,128)(2,1)S(1)} %stack.17.refs_2_), channel_id=1, source_target_pairs={{0,2},{1,3},{2,0},{3,1},{4,6},{5,7},{6,4},{7,5},{8,10},{9,11},{10,... | collective-permute-start | bytes 786440 | tf_op jit(solution)/shard_map/ppermute | solution.py:383
  31.1 8.2 %collective-permute-start.6 = (bf16[1,2,2,32,512]{4,3,2,1,0:T(8,128)(2,1)S(1)}, bf16[1,2,2,32,512]{4,3,2,1,0:T(8,128)(2,1)S(1)}, u32[]{:S(2)}, u32[]{:S(2)}) collective-permute-start(bf16[1,2,2,32,512]{4,3,2,1,0:T(8,128)(2,1)S(1)} %add.82.refs_0_.refs_2_), channel_id=1, source_target_pairs={{0,4},{1,5},{2,6},{3,7},{4,0},{5,1},{6,2},{7,3},{8,12},{9,13},{10,... | collective-permute-start | bytes 393224 | tf_op jit(solution)/shard_map/ppermute | solution.py:383
  38.8 2.5 %collective-permute-start.11 = (bf16[2,2,2,32,512]{4,3,2,1,0:T(8,128)(2,1)S(1)}, bf16[2,2,2,32,512]{4,3,2,1,0:T(8,128)(2,1)S(1)}, u32[]{:S(2)}, u32[]{:S(2)}) collective-permute-start(bf16[2,2,2,32,512]{4,3,2,1,0:T(8,128)(2,1)S(1)} %stack.17.refs_2_), channel_id=1, source_target_pairs={{0,1},{1,0},{2,3},{3,2},{4,5},{5,4},{6,7},{7,6},{8,9},{9,8},{10,11... | collective-permute-start | bytes 786440 | tf_op jit(solution)/shard_map/ppermute | solution.py:383
  38.9 2.4 %collective-permute-start.12 = (bf16[2,2,2,32,512]{4,3,2,1,0:T(8,128)(2,1)S(1)}, bf16[2,2,2,32,512]{4,3,2,1,0:T(8,128)(2,1)S(1)}, u32[]{:S(2)}, u32[]{:S(2)}) collective-permute-start(bf16[2,2,2,32,512]{4,3,2,1,0:T(8,128)(2,1)S(1)} %collective-permute-done.10.refs_3_), channel_id=1, source_target_pairs={{0,1},{1,0},{2,3},{3,2},{4,5},{5,4},{6,7},{7,6},{8,9},{9,8},{10,11... | collective-permute-start | bytes 786440 | tf_op jit(solution)/shard_map/ppermute | solution.py:383
  39.4 6.5 %collective-permute-start.8 = (bf16[2,2,2,32,512]{4,3,2,1,0:T(8,128)(2,1)S(1)}, bf16[2,2,2,32,512]{4,3,2,1,0:T(8,128)(2,1)S(1)}, u32[]{:S(2)}, u32[]{:S(2)}) collective-permute-start(bf16[2,2,2,32,512]{4,3,2,1,0:T(8,128)(2,1)S(1)} %stack.16.refs_6_.own_ref), channel_id=1, source_target_pairs={{0,1},{1,0},{2,3},{3,2},{4,5},{5,4},{6,7},{7,6},{8,9},{9,8},{10,11... | collective-permute-start | bytes 786440 | tf_op jit(solution)/shard_map/ppermute | solution.py:383
  39.5 8.9 %collective-permute-start.7 = (bf16[2,2,2,32,512]{4,3,2,1,0:T(8,128)(2,1)S(1)}, bf16[2,2,2,32,512]{4,3,2,1,0:T(8,128)(2,1)S(1)}, u32[]{:S(2)}, u32[]{:S(2)}) collective-permute-start(bf16[2,2,2,32,512]{4,3,2,1,0:T(8,128)(2,1)S(1)} %stack.16.refs_6_.own_ref), channel_id=1, source_target_pairs={{0,2},{1,3},{2,0},{3,1},{4,6},{5,7},{6,4},{7,5},{8,10},{9,11},{10,... | collective-permute-start | bytes 786440 | tf_op jit(solution)/shard_map/ppermute | solution.py:383
  45.9 12.7 %copy-start = (s32[64,512]{1,0:T(8,128)S(1)}, s32[64,512]{1,0:T(8,128)}, u32[]{:S(2)}) copy-start(s32[64,512]{1,0:T(8,128)} %onset_ref.3) | copy-start | bytes 393220
  48.5 3.7 %collective-permute-start.13 = (bf16[2,2,2,32,512]{4,3,2,1,0:T(8,128)(2,1)S(1)}, bf16[2,2,2,32,512]{4,3,2,1,0:T(8,128)(2,1)S(1)}, u32[]{:S(2)}, u32[]{:S(2)}) collective-permute-start(bf16[2,2,2,32,512]{4,3,2,1,0:T(8,128)(2,1)S(1)} %stack.18.own_ref), channel_id=1, source_target_pairs={{0,1},{1,0},{2,3},{3,2},{4,5},{5,4},{6,7},{7,6},{8,9},{9,8},{10,11... | collective-permute-start | bytes 786440 | tf_op jit(solution)/shard_map/ppermute | solution.py:383
  48.7 9.0 %collective-permute-start.19 = (bf16[2,2,32,512]{3,2,1,0:T(8,128)(2,1)S(1)}, bf16[2,2,32,512]{3,2,1,0:T(8,128)(2,1)S(1)}, u32[]{:S(2)}, u32[]{:S(2)}) collective-permute-start(bf16[2,2,32,512]{3,2,1,0:T(8,128)(2,1)S(1)} %respond.1.refs_2_.refs_0_), channel_id=1, source_target_pairs={{0,24},{8,16},{16,8},{24,0},{1,25},{9,17},{17,9},{25,1},{2,26},{10... | collective-permute-start | bytes 393224 | tf_op jit(solution)/shard_map/ppermute | solution.py:383
  50.9 7.7 %collective-permute-start.18 = (bf16[2,2,32,512]{3,2,1,0:T(8,128)(2,1)S(1)}, bf16[2,2,32,512]{3,2,1,0:T(8,128)(2,1)S(1)}, u32[]{:S(2)}, u32[]{:S(2)}) collective-permute-start(bf16[2,2,32,512]{3,2,1,0:T(8,128)(2,1)S(1)} %respond.1.refs_2_.refs_0_), channel_id=1, source_target_pairs={{0,16},{8,24},{16,0},{24,8},{1,17},{9,25},{17,1},{25,9},{2,18},{10... | collective-permute-start | bytes 393224 | tf_op jit(solution)/shard_map/ppermute | solution.py:383
  51.7 6.9 %collective-permute-start.17 = (bf16[2,2,32,512]{3,2,1,0:T(8,128)(2,1)S(1)}, bf16[2,2,32,512]{3,2,1,0:T(8,128)(2,1)S(1)}, u32[]{:S(2)}, u32[]{:S(2)}) collective-permute-start(bf16[2,2,32,512]{3,2,1,0:T(8,128)(2,1)S(1)} %respond.1.refs_2_.refs_0_), channel_id=1, source_target_pairs={{0,8},{8,0},{16,24},{24,16},{1,9},{9,1},{17,25},{25,17},{2,10},{10... | collective-permute-start | bytes 393224 | tf_op jit(solution)/shard_map/ppermute | solution.py:383
  54.7 10.2 %collective-permute-start.16 = (bf16[2,2,32,512]{3,2,1,0:T(8,128)(2,1)S(1)}, bf16[2,2,32,512]{3,2,1,0:T(8,128)(2,1)S(1)}, u32[]{:S(2)}, u32[]{:S(2)}) collective-permute-start(bf16[2,2,32,512]{3,2,1,0:T(8,128)(2,1)S(1)} %respond_half.3.refs_0_), channel_id=1, source_target_pairs={{0,24},{8,16},{16,8},{24,0},{1,25},{9,17},{17,9},{25,1},{2,26},{10... | collective-permute-start | bytes 393224 | tf_op jit(solution)/shard_map/ppermute | solution.py:383
  56.9 8.0 %collective-permute-start.15 = (bf16[2,2,32,512]{3,2,1,0:T(8,128)(2,1)S(1)}, bf16[2,2,32,512]{3,2,1,0:T(8,128)(2,1)S(1)}, u32[]{:S(2)}, u32[]{:S(2)}) collective-permute-start(bf16[2,2,32,512]{3,2,1,0:T(8,128)(2,1)S(1)} %respond_half.3.refs_0_), channel_id=1, source_target_pairs={{0,16},{8,24},{16,0},{24,8},{1,17},{9,25},{17,1},{25,9},{2,18},{10... | collective-permute-start | bytes 393224 | tf_op jit(solution)/shard_map/ppermute | solution.py:383
  57.7 7.2 %collective-permute-start.14 = (bf16[2,2,32,512]{3,2,1,0:T(8,128)(2,1)S(1)}, bf16[2,2,32,512]{3,2,1,0:T(8,128)(2,1)S(1)}, u32[]{:S(2)}, u32[]{:S(2)}) collective-permute-start(bf16[2,2,32,512]{3,2,1,0:T(8,128)(2,1)S(1)} %respond_half.3.refs_0_), channel_id=1, source_target_pairs={{0,8},{8,0},{16,24},{24,16},{1,9},{9,1},{17,25},{25,17},{2,10},{10... | collective-permute-start | bytes 393224 | tf_op jit(solution)/shard_map/ppermute | solution.py:383

commit v8 on v7

--- a/solution.py
+++ b/solution.py
@@ -10,8 +10,8 @@
 
 ROWS = 16
 CHUNKS = 2
-F_TIMES = 128
-F_SLOTS = 4
+F_TIMES = 64
+F_SLOTS = 8
 I_TIMES = 256
 I_SLOTS = 2
 I_CUTS = 8

time: 71.5 us -> 71 us (level)
  no operation moved by 1% of the time
where the time goes in v8:
time: 71 us; the launch traced here: 70.9 us
  Pallas kernels  43.5 us (61%)
  starting transfers between devices  25.1 us (35%)
  waiting for transfers between devices  1.48 us (2%)
    ppermute x20, starting transfers between devices, swap(): lax.ppermute(array, axis, [(i, i ^ mask) for i in range(lax.axis_size(axi...  25.1 us
    pallas_call x2, Pallas kernels, forward(): pl.pallas_call(functools.partial(forward_kernel, first, focal), in_specs=...  13.5 us
    pallas_call x2, Pallas kernels, invert(): pl.pallas_call(functools.partial(inverse_kernel, first, has_before), in_s...  12.5 us
    pallas_call x2, Pallas kernels, load(): pl.pallas_call(functools.partial(load_kernel, first), in_specs=[pl.BlockS...  6.97 us
    pallas_call x2, Pallas kernels, respond_half(): pl.pallas_call(functools.partial(half_kernel, masks, before is not None,...  4.97 us
    pallas_call x1, Pallas kernels, respond(): pl.pallas_call(functools.partial(response_kernel, masks, len(kept)), in_s...  4.63 us
    ppermute x20, waiting for transfers between devices, swap(): lax.ppermute(array, axis, [(i, i ^ mask) for i in range(lax.axis_size(axi...  1.48 us
  transfers between devices with their start and end apart: 20, of which 2 were waited for; matrix products, arithmetic and copies ran while one was open for 0% of the time, Pallas kernels for 43%

profile of v8, /device:TPU:0, one launch (start us, length us, event | category | flops | bytes accessed | tf_op | source)
XLA Modules:
  0.0 70.9 jit_solution(4547022898950389686)
XLA Ops:
  0.5 6.7 %forward.3 = (f32[2,2,32,512]{3,2,1,0:T(8,128)S(1)}, bf16[2,2,32,512]{3,2,1,0:T(8,128)(2,1)S(1)}, bf16[2,2,32,512]{3,2,1,0:T(8,128)(2,1)S(1)}, bf16[2,2,32,512]{3,2,1,0:T(8,128)(2,1)S(1)}) custom-call(bf16[2,16,512]{2,1,0:T(8,128)(2,1)S(1)} %constant_dynamic-update-slice_fusion.table_ref, bf16[512,64,512]{2,1,0:T(8,128)(2,1)} %traces_ref.3), custom_call_target="tpu_custom_call" | custom-call | flops 4294967296 | bytes 16777216 | tf_op jit(solution)/shard_map/forward/pallas_call | solution.py:103
  7.2 3.0 %collective-permute-start.3 = (bf16[2,2,32,512]{3,2,1,0:T(8,128)(2,1)S(1)}, bf16[2,2,32,512]{3,2,1,0:T(8,128)(2,1)S(1)}, u32[]{:S(2)}, u32[]{:S(2)}) collective-permute-start(bf16[2,2,32,512]{3,2,1,0:T(8,128)(2,1)S(1)} %get-tuple-element.18), channel_id=1, source_target_pairs={{0,8},{8,0},{16,24},{24,16},{1,9},{9,1},{17,25},{25,17},{2,10},{10... | collective-permute-start | bytes 393224 | tf_op jit(solution)/shard_map/ppermute | solution.py:383
  10.2 1.5 %collective-permute-start.4 = (bf16[2,2,32,512]{3,2,1,0:T(8,128)(2,1)S(1)}, bf16[2,2,32,512]{3,2,1,0:T(8,128)(2,1)S(1)}, u32[]{:S(2)}, u32[]{:S(2)}) collective-permute-start(bf16[2,2,32,512]{3,2,1,0:T(8,128)(2,1)S(1)} %get-tuple-element.19), channel_id=1, source_target_pairs={{0,16},{8,24},{16,0},{24,8},{1,17},{9,25},{17,1},{25,9},{2,18},{10... | collective-permute-start | bytes 393224 | tf_op jit(solution)/shard_map/ppermute | solution.py:383
  11.7 6.7 %forward.2 = (f32[2,2,32,512]{3,2,1,0:T(8,128)S(1)}, bf16[2,2,32,512]{3,2,1,0:T(8,128)(2,1)S(1)}, bf16[2,2,32,512]{3,2,1,0:T(8,128)(2,1)S(1)}, bf16[2,2,32,512]{3,2,1,0:T(8,128)(2,1)S(1)}) custom-call(bf16[2,16,512]{2,1,0:T(8,128)(2,1)S(1)} %constant_dynamic-update-slice_fusion.table_ref, bf16[512,64,512]{2,1,0:T(8,128)(2,1)} %traces_ref.3), custom_call_target="tpu_custom_call" | custom-call | flops 4294967296 | bytes 16777216 | tf_op jit(solution)/shard_map/forward/pallas_call | solution.py:103
  18.5 2.0 %collective-permute-start = (bf16[2,2,32,512]{3,2,1,0:T(8,128)(2,1)S(1)}, bf16[2,2,32,512]{3,2,1,0:T(8,128)(2,1)S(1)}, u32[]{:S(2)}, u32[]{:S(2)}) collective-permute-start(bf16[2,2,32,512]{3,2,1,0:T(8,128)(2,1)S(1)} %get-tuple-element.14), channel_id=1, source_target_pairs={{0,8},{8,0},{16,24},{24,16},{1,9},{9,1},{17,25},{25,17},{2,10},{10... | collective-permute-start | bytes 393224 | tf_op jit(solution)/shard_map/ppermute | solution.py:383
  20.5 1.5 %collective-permute-start.1 = (bf16[2,2,32,512]{3,2,1,0:T(8,128)(2,1)S(1)}, bf16[2,2,32,512]{3,2,1,0:T(8,128)(2,1)S(1)}, u32[]{:S(2)}, u32[]{:S(2)}) collective-permute-start(bf16[2,2,32,512]{3,2,1,0:T(8,128)(2,1)S(1)} %get-tuple-element.15), channel_id=1, source_target_pairs={{0,16},{8,24},{16,0},{24,8},{1,17},{9,25},{17,1},{25,9},{2,18},{10... | collective-permute-start | bytes 393224 | tf_op jit(solution)/shard_map/ppermute | solution.py:383
  22.1 3.1 %collective-permute-start.9 = (bf16[1,2,2,32,512]{4,3,2,1,0:T(8,128)(2,1)S(1)}, bf16[1,2,2,32,512]{4,3,2,1,0:T(8,128)(2,1)S(1)}, u32[]{:S(2)}, u32[]{:S(2)}) collective-permute-start(bf16[1,2,2,32,512]{4,3,2,1,0:T(8,128)(2,1)S(1)} %add.81.refs_0_), channel_id=1, source_target_pairs={{0,4},{1,5},{2,6},{3,7},{4,0},{5,1},{6,2},{7,3},{8,12},{9,13},{10,... | collective-permute-start | bytes 393224 | tf_op jit(solution)/shard_map/ppermute | solution.py:383
  25.2 3.5 %load.2.refs_4_.refs_0_.refs_1_ = bf16[1,2,512,4096]{3,2,1,0:T(8,128)(2,1)S(1)} custom-call(bf16[2,2,512,4096]{3,2,1,0:T(8,128)(2,1)} %reflection_ref.3, bf16[1,2,2,32,512]{4,3,2,1,0:T(8,128)(2,1)S(1)} %add.81.refs_0_), custom_call_target="tpu_custom_call" | custom-call | tf_op jit(solution)/shard_map/load/pallas_call | solution.py:140
  28.8 1.0 %collective-permute-done.9.refs_1_ = bf16[1,2,2,32,512]{4,3,2,1,0:T(8,128)(2,1)S(1)} collective-permute-done((bf16[1,2,2,32,512]{4,3,2,1,0:T(8,128)(2,1)S(1)}, bf16[1,2,2,32,512]{4,3,2,1,0:T(8,128)(2,1)S(1)}, u32[]{:S(2)}, u32[]{:S(2)}) %collective-permute-start.9) | collective-permute-done | bytes 131104 | tf_op jit(solution)/shard_map/ppermute | solution.py:383
  29.9 0.8 %collective-permute-start.10 = (bf16[2,2,2,32,512]{4,3,2,1,0:T(8,128)(2,1)S(1)}, bf16[2,2,2,32,512]{4,3,2,1,0:T(8,128)(2,1)S(1)}, u32[]{:S(2)}, u32[]{:S(2)}) collective-permute-start(bf16[2,2,2,32,512]{4,3,2,1,0:T(8,128)(2,1)S(1)} %stack.17.refs_2_), channel_id=1, source_target_pairs={{0,2},{1,3},{2,0},{3,1},{4,6},{5,7},{6,4},{7,5},{8,10},{9,11},{10,... | collective-permute-start | bytes 786440 | tf_op jit(solution)/shard_map/ppermute | solution.py:383
  30.7 3.4 %collective-permute-start.6 = (bf16[1,2,2,32,512]{4,3,2,1,0:T(8,128)(2,1)S(1)}, bf16[1,2,2,32,512]{4,3,2,1,0:T(8,128)(2,1)S(1)}, u32[]{:S(2)}, u32[]{:S(2)}) collective-permute-start(bf16[1,2,2,32,512]{4,3,2,1,0:T(8,128)(2,1)S(1)} %add.82.refs_0_.refs_2_), channel_id=1, source_target_pairs={{0,4},{1,5},{2,6},{3,7},{4,0},{5,1},{6,2},{7,3},{8,12},{9,13},{10,... | collective-permute-start | bytes 393224 | tf_op jit(solution)/shard_map/ppermute | solution.py:383
  34.0 0.8 %spread.1.refs_3_ = bf16[8192,256]{1,0:T(8,128)(2,1)S(1)} custom-call(bf16[2,16,512]{2,1,0:T(8,128)(2,1)S(1)} %constant_dynamic-update-slice_fusion.table_ref), custom_call_target="tpu_custom_call" | custom-call | bytes 4194304 | tf_op jit(solution)/shard_map/spread/pallas_call | solution.py:252
  34.8 3.5 %load.3.refs_2_.refs_1_ = bf16[1,2,512,4096]{3,2,1,0:T(8,128)(2,1)S(1)} custom-call(bf16[2,2,512,4096]{3,2,1,0:T(8,128)(2,1)} %reflection_ref.3, bf16[1,2,2,32,512]{4,3,2,1,0:T(8,128)(2,1)S(1)} %add.82.refs_0_.refs_2_), custom_call_target="tpu_custom_call" | custom-call | tf_op jit(solution)/shard_map/load/pallas_call | solution.py:140
  39.1 1.7 %collective-permute-start.7 = (bf16[2,2,2,32,512]{4,3,2,1,0:T(8,128)(2,1)S(1)}, bf16[2,2,2,32,512]{4,3,2,1,0:T(8,128)(2,1)S(1)}, u32[]{:S(2)}, u32[]{:S(2)}) collective-permute-start(bf16[2,2,2,32,512]{4,3,2,1,0:T(8,128)(2,1)S(1)} %stack.16.refs_6_.own_ref), channel_id=1, source_target_pairs={{0,2},{1,3},{2,0},{3,1},{4,6},{5,7},{6,4},{7,5},{8,10},{9,11},{10,... | collective-permute-start | bytes 786440 | tf_op jit(solution)/shard_map/ppermute | solution.py:383
  40.8 4.6 %respond.1.refs_2_.refs_0_ = bf16[2,2,32,512]{3,2,1,0:T(8,128)(2,1)S(1)} custom-call(bf16[1,2,512,4096]{3,2,1,0:T(8,128)(2,1)S(1)} %load.2.refs_4_.refs_0_.refs_1_, bf16[1,2,512,4096]{3,2,1,0:T(8,128)(2,1)S(1)} %load.3.refs_2_.refs_1_, bf16[2,2,2,32,512]{4,3,2,1,0:T(8,128)(2,1)S(1)} %stack.17.refs_2_, ...), custom_call_target="tpu_custom_call" | custom-call | bytes 1024 | tf_op jit(solution)/shard_map/respond/pallas_call | solution.py:176
  45.5 2.5 %respond_half.2.refs_1_.refs_0_ = f32[2,1024,64]{2,1,0:T(8,128)S(1)} custom-call(bf16[2,2,2,32,512]{4,3,2,1,0:T(8,128)(2,1)S(1)} %stack.16.refs_6_.own_ref, bf16[2,2,2,32,512]{4,3,2,1,0:T(8,128)(2,1)S(1)} %collective-permute-done.8.other_ref, bf16[1,2,512,4096]{3,2,1,0:T(8,128)(2,1)S(1)} %load.2.refs_4_.refs_0_.refs_1_, ...), custom_call_target="tpu_custom_call" | custom-call | bytes 1024 | tf_op jit(solution)/shard_map/respond_half/pallas_call | solution.py:226
  48.3 2.2 %collective-permute-start.19 = (bf16[2,2,32,512]{3,2,1,0:T(8,128)(2,1)S(1)}, bf16[2,2,32,512]{3,2,1,0:T(8,128)(2,1)S(1)}, u32[]{:S(2)}, u32[]{:S(2)}) collective-permute-start(bf16[2,2,32,512]{3,2,1,0:T(8,128)(2,1)S(1)} %respond.1.refs_2_.refs_0_), channel_id=1, source_target_pairs={{0,24},{8,16},{16,8},{24,0},{1,25},{9,17},{17,9},{25,1},{2,26},{10... | collective-permute-start | bytes 393224 | tf_op jit(solution)/shard_map/ppermute | solution.py:383
  50.4 0.8 %collective-permute-start.18 = (bf16[2,2,32,512]{3,2,1,0:T(8,128)(2,1)S(1)}, bf16[2,2,32,512]{3,2,1,0:T(8,128)(2,1)S(1)}, u32[]{:S(2)}, u32[]{:S(2)}) collective-permute-start(bf16[2,2,32,512]{3,2,1,0:T(8,128)(2,1)S(1)} %respond.1.refs_2_.refs_0_), channel_id=1, source_target_pairs={{0,16},{8,24},{16,0},{24,8},{1,17},{9,25},{17,1},{25,9},{2,18},{10... | collective-permute-start | bytes 393224 | tf_op jit(solution)/shard_map/ppermute | solution.py:383
  51.8 2.4 %respond_half.3.refs_0_ = bf16[2,2,32,512]{3,2,1,0:T(8,128)(2,1)S(1)} custom-call(bf16[2,2,2,32,512]{4,3,2,1,0:T(8,128)(2,1)S(1)} %stack.18.own_ref, bf16[2,2,2,32,512]{4,3,2,1,0:T(8,128)(2,1)S(1)} %collective-permute-done.13.other_ref, f32[2,1024,64]{2,1,0:T(8,128)S(1)} %respond_half.2.refs_1_.refs_0_, ...), custom_call_target="tpu_custom_call" | custom-call | bytes 1024 | tf_op jit(solution)/shard_map/respond_half/pallas_call | solution.py:226
  54.2 2.2 %collective-permute-start.16 = (bf16[2,2,32,512]{3,2,1,0:T(8,128)(2,1)S(1)}, bf16[2,2,32,512]{3,2,1,0:T(8,128)(2,1)S(1)}, u32[]{:S(2)}, u32[]{:S(2)}) collective-permute-start(bf16[2,2,32,512]{3,2,1,0:T(8,128)(2,1)S(1)} %respond_half.3.refs_0_), channel_id=1, source_target_pairs={{0,24},{8,16},{16,8},{24,0},{1,25},{9,17},{17,9},{25,1},{2,26},{10... | collective-permute-start | bytes 393224 | tf_op jit(solution)/shard_map/ppermute | solution.py:383
  56.4 0.8 %collective-permute-start.15 = (bf16[2,2,32,512]{3,2,1,0:T(8,128)(2,1)S(1)}, bf16[2,2,32,512]{3,2,1,0:T(8,128)(2,1)S(1)}, u32[]{:S(2)}, u32[]{:S(2)}) collective-permute-start(bf16[2,2,32,512]{3,2,1,0:T(8,128)(2,1)S(1)} %respond_half.3.refs_0_), channel_id=1, source_target_pairs={{0,16},{8,24},{16,0},{24,8},{1,17},{9,25},{17,1},{25,9},{2,18},{10... | collective-permute-start | bytes 393224 | tf_op jit(solution)/shard_map/ppermute | solution.py:383
  57.2 0.5 collective-permute-start.14
  58.1 6.3 %invert.2.refs_4_ = bf16[512,64,512]{2,1,0:T(8,128)(2,1)} custom-call(bf16[8192,256]{1,0:T(8,128)(2,1)S(1)} %spread.1.refs_3_, s32[64,512]{1,0:T(8,128)S(1)} %copy-done, bf16[2,2,32,512]{3,2,1,0:T(8,128)(2,1)S(1)} %respond.1.refs_2_.refs_0_, bf16[2,2,32,512]{3,2,1,0:T(8,128)(2,1)S(1)} %collective-permute-done.17.refs_1_, ...), custom_call_target="tpu_custom_call" | custom-call | flops 4294967296 | bytes 16777216 | tf_op jit(solution)/shard_map/invert/pallas_call | solution.py:321
  64.4 6.3 %invert.3 = bf16[512,64,512]{2,1,0:T(8,128)(2,1)} custom-call(bf16[8192,256]{1,0:T(8,128)(2,1)S(1)} %spread.1.refs_3_, s32[64,512]{1,0:T(8,128)S(1)} %copy-done, bf16[2,2,32,512]{3,2,1,0:T(8,128)(2,1)S(1)} %respond_half.3.refs_0_, bf16[2,2,32,512]{3,2,1,0:T(8,128)(2,1)S(1)} %collective-permute-done.14.refs_1_, ...), custom_call_target="tpu_custom_call", output_to_operand_aliasing={{}: (6, {})} | custom-call | flops 4294967296 | bytes 16777216 | tf_op jit(solution)/shard_map/invert/pallas_call | solution.py:321
  (45 shorter events, 2.5 us)
Async XLA Ops:
  7.2 14.8 %collective-permute-start.3 = (bf16[2,2,32,512]{3,2,1,0:T(8,128)(2,1)S(1)}, bf16[2,2,32,512]{3,2,1,0:T(8,128)(2,1)S(1)}, u32[]{:S(2)}, u32[]{:S(2)}) collective-permute-start(bf16[2,2,32,512]{3,2,1,0:T(8,128)(2,1)S(1)} %get-tuple-element.18), channel_id=1, source_target_pairs={{0,8},{8,0},{16,24},{24,16},{1,9},{9,1},{17,25},{25,17},{2,10},{10... | collective-permute-start | bytes 393224 | tf_op jit(solution)/shard_map/ppermute | solution.py:383
  10.2 11.8 %collective-permute-start.4 = (bf16[2,2,32,512]{3,2,1,0:T(8,128)(2,1)S(1)}, bf16[2,2,32,512]{3,2,1,0:T(8,128)(2,1)S(1)}, u32[]{:S(2)}, u32[]{:S(2)}) collective-permute-start(bf16[2,2,32,512]{3,2,1,0:T(8,128)(2,1)S(1)} %get-tuple-element.19), channel_id=1, source_target_pairs={{0,16},{8,24},{16,0},{24,8},{1,17},{9,25},{17,1},{25,9},{2,18},{10... | collective-permute-start | bytes 393224 | tf_op jit(solution)/shard_map/ppermute | solution.py:383
  11.7 10.3 %collective-permute-start.5 = (bf16[2,2,32,512]{3,2,1,0:T(8,128)(2,1)S(1)}, bf16[2,2,32,512]{3,2,1,0:T(8,128)(2,1)S(1)}, u32[]{:S(2)}, u32[]{:S(2)}) collective-permute-start(bf16[2,2,32,512]{3,2,1,0:T(8,128)(2,1)S(1)} %get-tuple-element.20), channel_id=1, source_target_pairs={{0,24},{8,16},{16,8},{24,0},{1,25},{9,17},{17,9},{25,1},{2,26},{10... | collective-permute-start | bytes 393224 | tf_op jit(solution)/shard_map/ppermute | solution.py:383
  18.5 10.2 %collective-permute-start = (bf16[2,2,32,512]{3,2,1,0:T(8,128)(2,1)S(1)}, bf16[2,2,32,512]{3,2,1,0:T(8,128)(2,1)S(1)}, u32[]{:S(2)}, u32[]{:S(2)}) collective-permute-start(bf16[2,2,32,512]{3,2,1,0:T(8,128)(2,1)S(1)} %get-tuple-element.14), channel_id=1, source_target_pairs={{0,8},{8,0},{16,24},{24,16},{1,9},{9,1},{17,25},{25,17},{2,10},{10... | collective-permute-start | bytes 393224 | tf_op jit(solution)/shard_map/ppermute | solution.py:383
  20.5 8.2 %collective-permute-start.1 = (bf16[2,2,32,512]{3,2,1,0:T(8,128)(2,1)S(1)}, bf16[2,2,32,512]{3,2,1,0:T(8,128)(2,1)S(1)}, u32[]{:S(2)}, u32[]{:S(2)}) collective-permute-start(bf16[2,2,32,512]{3,2,1,0:T(8,128)(2,1)S(1)} %get-tuple-element.15), channel_id=1, source_target_pairs={{0,16},{8,24},{16,0},{24,8},{1,17},{9,25},{17,1},{25,9},{2,18},{10... | collective-permute-start | bytes 393224 | tf_op jit(solution)/shard_map/ppermute | solution.py:383
  22.0 6.7 %collective-permute-start.2 = (bf16[2,2,32,512]{3,2,1,0:T(8,128)(2,1)S(1)}, bf16[2,2,32,512]{3,2,1,0:T(8,128)(2,1)S(1)}, u32[]{:S(2)}, u32[]{:S(2)}) collective-permute-start(bf16[2,2,32,512]{3,2,1,0:T(8,128)(2,1)S(1)} %get-tuple-element.16), channel_id=1, source_target_pairs={{0,24},{8,16},{16,8},{24,0},{1,25},{9,17},{17,9},{25,1},{2,26},{10... | collective-permute-start | bytes 393224 | tf_op jit(solution)/shard_map/ppermute | solution.py:383
  22.1 7.7 %collective-permute-start.9 = (bf16[1,2,2,32,512]{4,3,2,1,0:T(8,128)(2,1)S(1)}, bf16[1,2,2,32,512]{4,3,2,1,0:T(8,128)(2,1)S(1)}, u32[]{:S(2)}, u32[]{:S(2)}) collective-permute-start(bf16[1,2,2,32,512]{4,3,2,1,0:T(8,128)(2,1)S(1)} %add.81.refs_0_), channel_id=1, source_target_pairs={{0,4},{1,5},{2,6},{3,7},{4,0},{5,1},{6,2},{7,3},{8,12},{9,13},{10,... | collective-permute-start | bytes 393224 | tf_op jit(solution)/shard_map/ppermute | solution.py:383
  29.9 8.6 %collective-permute-start.10 = (bf16[2,2,2,32,512]{4,3,2,1,0:T(8,128)(2,1)S(1)}, bf16[2,2,2,32,512]{4,3,2,1,0:T(8,128)(2,1)S(1)}, u32[]{:S(2)}, u32[]{:S(2)}) collective-permute-start(bf16[2,2,2,32,512]{4,3,2,1,0:T(8,128)(2,1)S(1)} %stack.17.refs_2_), channel_id=1, source_target_pairs={{0,2},{1,3},{2,0},{3,1},{4,6},{5,7},{6,4},{7,5},{8,10},{9,11},{10,... | collective-permute-start | bytes 786440 | tf_op jit(solution)/shard_map/ppermute | solution.py:383
  30.7 8.2 %collective-permute-start.6 = (bf16[1,2,2,32,512]{4,3,2,1,0:T(8,128)(2,1)S(1)}, bf16[1,2,2,32,512]{4,3,2,1,0:T(8,128)(2,1)S(1)}, u32[]{:S(2)}, u32[]{:S(2)}) collective-permute-start(bf16[1,2,2,32,512]{4,3,2,1,0:T(8,128)(2,1)S(1)} %add.82.refs_0_.refs_2_), channel_id=1, source_target_pairs={{0,4},{1,5},{2,6},{3,7},{4,0},{5,1},{6,2},{7,3},{8,12},{9,13},{10,... | collective-permute-start | bytes 393224 | tf_op jit(solution)/shard_map/ppermute | solution.py:383
  38.3 2.5 %collective-permute-start.11 = (bf16[2,2,2,32,512]{4,3,2,1,0:T(8,128)(2,1)S(1)}, bf16[2,2,2,32,512]{4,3,2,1,0:T(8,128)(2,1)S(1)}, u32[]{:S(2)}, u32[]{:S(2)}) collective-permute-start(bf16[2,2,2,32,512]{4,3,2,1,0:T(8,128)(2,1)S(1)} %stack.17.refs_2_), channel_id=1, source_target_pairs={{0,1},{1,0},{2,3},{3,2},{4,5},{5,4},{6,7},{7,6},{8,9},{9,8},{10,11... | collective-permute-start | bytes 786440 | tf_op jit(solution)/shard_map/ppermute | solution.py:383
  38.4 2.4 %collective-permute-start.12 = (bf16[2,2,2,32,512]{4,3,2,1,0:T(8,128)(2,1)S(1)}, bf16[2,2,2,32,512]{4,3,2,1,0:T(8,128)(2,1)S(1)}, u32[]{:S(2)}, u32[]{:S(2)}) collective-permute-start(bf16[2,2,2,32,512]{4,3,2,1,0:T(8,128)(2,1)S(1)} %collective-permute-done.10.refs_3_), channel_id=1, source_target_pairs={{0,1},{1,0},{2,3},{3,2},{4,5},{5,4},{6,7},{7,6},{8,9},{9,8},{10,11... | collective-permute-start | bytes 786440 | tf_op jit(solution)/shard_map/ppermute | solution.py:383
  38.9 6.5 %collective-permute-start.8 = (bf16[2,2,2,32,512]{4,3,2,1,0:T(8,128)(2,1)S(1)}, bf16[2,2,2,32,512]{4,3,2,1,0:T(8,128)(2,1)S(1)}, u32[]{:S(2)}, u32[]{:S(2)}) collective-permute-start(bf16[2,2,2,32,512]{4,3,2,1,0:T(8,128)(2,1)S(1)} %stack.16.refs_6_.own_ref), channel_id=1, source_target_pairs={{0,1},{1,0},{2,3},{3,2},{4,5},{5,4},{6,7},{7,6},{8,9},{9,8},{10,11... | collective-permute-start | bytes 786440 | tf_op jit(solution)/shard_map/ppermute | solution.py:383
  39.1 8.9 %collective-permute-start.7 = (bf16[2,2,2,32,512]{4,3,2,1,0:T(8,128)(2,1)S(1)}, bf16[2,2,2,32,512]{4,3,2,1,0:T(8,128)(2,1)S(1)}, u32[]{:S(2)}, u32[]{:S(2)}) collective-permute-start(bf16[2,2,2,32,512]{4,3,2,1,0:T(8,128)(2,1)S(1)} %stack.16.refs_6_.own_ref), channel_id=1, source_target_pairs={{0,2},{1,3},{2,0},{3,1},{4,6},{5,7},{6,4},{7,5},{8,10},{9,11},{10,... | collective-permute-start | bytes 786440 | tf_op jit(solution)/shard_map/ppermute | solution.py:383
  45.4 12.7 %copy-start = (s32[64,512]{1,0:T(8,128)S(1)}, s32[64,512]{1,0:T(8,128)}, u32[]{:S(2)}) copy-start(s32[64,512]{1,0:T(8,128)} %onset_ref.3) | copy-start | bytes 393220
  48.0 3.7 %collective-permute-start.13 = (bf16[2,2,2,32,512]{4,3,2,1,0:T(8,128)(2,1)S(1)}, bf16[2,2,2,32,512]{4,3,2,1,0:T(8,128)(2,1)S(1)}, u32[]{:S(2)}, u32[]{:S(2)}) collective-permute-start(bf16[2,2,2,32,512]{4,3,2,1,0:T(8,128)(2,1)S(1)} %stack.18.own_ref), channel_id=1, source_target_pairs={{0,1},{1,0},{2,3},{3,2},{4,5},{5,4},{6,7},{7,6},{8,9},{9,8},{10,11... | collective-permute-start | bytes 786440 | tf_op jit(solution)/shard_map/ppermute | solution.py:383
  48.3 9.0 %collective-permute-start.19 = (bf16[2,2,32,512]{3,2,1,0:T(8,128)(2,1)S(1)}, bf16[2,2,32,512]{3,2,1,0:T(8,128)(2,1)S(1)}, u32[]{:S(2)}, u32[]{:S(2)}) collective-permute-start(bf16[2,2,32,512]{3,2,1,0:T(8,128)(2,1)S(1)} %respond.1.refs_2_.refs_0_), channel_id=1, source_target_pairs={{0,24},{8,16},{16,8},{24,0},{1,25},{9,17},{17,9},{25,1},{2,26},{10... | collective-permute-start | bytes 393224 | tf_op jit(solution)/shard_map/ppermute | solution.py:383
  50.4 7.7 %collective-permute-start.18 = (bf16[2,2,32,512]{3,2,1,0:T(8,128)(2,1)S(1)}, bf16[2,2,32,512]{3,2,1,0:T(8,128)(2,1)S(1)}, u32[]{:S(2)}, u32[]{:S(2)}) collective-permute-start(bf16[2,2,32,512]{3,2,1,0:T(8,128)(2,1)S(1)} %respond.1.refs_2_.refs_0_), channel_id=1, source_target_pairs={{0,16},{8,24},{16,0},{24,8},{1,17},{9,25},{17,1},{25,9},{2,18},{10... | collective-permute-start | bytes 393224 | tf_op jit(solution)/shard_map/ppermute | solution.py:383
  51.2 6.9 %collective-permute-start.17 = (bf16[2,2,32,512]{3,2,1,0:T(8,128)(2,1)S(1)}, bf16[2,2,32,512]{3,2,1,0:T(8,128)(2,1)S(1)}, u32[]{:S(2)}, u32[]{:S(2)}) collective-permute-start(bf16[2,2,32,512]{3,2,1,0:T(8,128)(2,1)S(1)} %respond.1.refs_2_.refs_0_), channel_id=1, source_target_pairs={{0,8},{8,0},{16,24},{24,16},{1,9},{9,1},{17,25},{25,17},{2,10},{10... | collective-permute-start | bytes 393224 | tf_op jit(solution)/shard_map/ppermute | solution.py:383
  54.2 10.2 %collective-permute-start.16 = (bf16[2,2,32,512]{3,2,1,0:T(8,128)(2,1)S(1)}, bf16[2,2,32,512]{3,2,1,0:T(8,128)(2,1)S(1)}, u32[]{:S(2)}, u32[]{:S(2)}) collective-permute-start(bf16[2,2,32,512]{3,2,1,0:T(8,128)(2,1)S(1)} %respond_half.3.refs_0_), channel_id=1, source_target_pairs={{0,24},{8,16},{16,8},{24,0},{1,25},{9,17},{17,9},{25,1},{2,26},{10... | collective-permute-start | bytes 393224 | tf_op jit(solution)/shard_map/ppermute | solution.py:383
  56.4 8.0 %collective-permute-start.15 = (bf16[2,2,32,512]{3,2,1,0:T(8,128)(2,1)S(1)}, bf16[2,2,32,512]{3,2,1,0:T(8,128)(2,1)S(1)}, u32[]{:S(2)}, u32[]{:S(2)}) collective-permute-start(bf16[2,2,32,512]{3,2,1,0:T(8,128)(2,1)S(1)} %respond_half.3.refs_0_), channel_id=1, source_target_pairs={{0,16},{8,24},{16,0},{24,8},{1,17},{9,25},{17,1},{25,9},{2,18},{10... | collective-permute-start | bytes 393224 | tf_op jit(solution)/shard_map/ppermute | solution.py:383
  57.2 7.2 %collective-permute-start.14 = (bf16[2,2,32,512]{3,2,1,0:T(8,128)(2,1)S(1)}, bf16[2,2,32,512]{3,2,1,0:T(8,128)(2,1)S(1)}, u32[]{:S(2)}, u32[]{:S(2)}) collective-permute-start(bf16[2,2,32,512]{3,2,1,0:T(8,128)(2,1)S(1)} %respond_half.3.refs_0_), channel_id=1, source_target_pairs={{0,8},{8,0},{16,24},{24,16},{1,9},{9,1},{17,25},{25,17},{2,10},{10... | collective-permute-start | bytes 393224 | tf_op jit(solution)/shard_map/ppermute | solution.py:383
